TPU v7x, 32 devices: a whole 2x2x4 slice. The times are simulated.
32 devices in a mesh: dp: 32 (over z, y, x, core).
Axes of the slice: x: 2, y: 2, z: 4, core: 2. Of those that a mesh axis runs over, the one named last changes fastest.
Arguments:
- attention_in: float32 [768, 1152], P('dp'), may hold values from -0.3125 to 0.3125
- attention_out: float32 [768, 384], P('dp'), may hold values from -1.25 to 1.25
- hidden_in: float32 [768, 1536], P('dp'), may hold values from -0.3125 to 0.3125
- hidden_out: float32 [3072, 384], P('dp'), may hold values from -0.15625 to 0.15625
- patch_weight: float32 [768, 384], P('dp'), may hold values from -0.21875 to 0.21875
- vector_rows: float32 [202, 384], replicated
- prototypes: float32 [1024, 384], P('dp'), may hold values from -6 to 6
- first_attention_in: float32 [768, 1152], P('dp'), may hold values from -7.6293945e-06 to 7.6293945e-06
- first_attention_out: float32 [768, 384], P('dp'), may hold values from -7.6293945e-06 to 7.6293945e-06
- first_hidden_in: float32 [768, 1536], P('dp'), may hold values from -7.6293945e-06 to 7.6293945e-06
- first_hidden_out: float32 [3072, 384], P('dp'), may hold values from -7.6293945e-06 to 7.6293945e-06
- first_patch_weight: float32 [768, 384], P('dp'), may hold values from -7.6293945e-06 to 7.6293945e-06
- first_vector_rows: float32 [202, 384], replicated, may hold values from -7.6293945e-06 to 7.6293945e-06
- first_prototypes: float32 [1024, 384], P('dp'), may hold values from -7.6293945e-06 to 7.6293945e-06
- second_attention_in: float32 [768, 1152], P('dp'), may hold values from 2.3230746e-14 to 9.2922984e-14
- second_attention_out: float32 [768, 384], P('dp'), may hold values from 2.3230746e-14 to 9.2922984e-14
- second_hidden_in: float32 [768, 1536], P('dp'), may hold values from 2.3230746e-14 to 9.2922984e-14
- second_hidden_out: float32 [3072, 384], P('dp'), may hold values from 2.3230746e-14 to 9.2922984e-14
- second_patch_weight: float32 [768, 384], P('dp'), may hold values from 2.3230746e-14 to 9.2922984e-14
- second_vector_rows: float32 [202, 384], replicated, may hold values from 2.3230746e-14 to 9.2922984e-14
- second_prototypes: float32 [1024, 384], P('dp'), may hold values from 2.3230746e-14 to 9.2922984e-14
- teacher_attention_in: bfloat16 [768, 1152], P('dp'), may hold values from -0.3125 to 0.3125
- teacher_attention_out: bfloat16 [768, 384], P('dp'), may hold values from -1.25 to 1.25
- teacher_hidden_in: bfloat16 [768, 1536], P('dp'), may hold values from -0.3125 to 0.3125
- teacher_hidden_out: bfloat16 [3072, 384], P('dp'), may hold values from -0.15625 to 0.15625
- teacher_patch_weight: bfloat16 [768, 384], P('dp'), may hold values from -0.21875 to 0.21875
- teacher_vector_rows: bfloat16 [202, 384], replicated
- teacher_prototypes: bfloat16 [1024, 384], P('dp'), may hold values from -6 to 6
- anchor_patches: bfloat16 [2, 96, 196, 768], P(None, 'dp'), may hold values from -6 to 6
- target_patches: bfloat16 [2, 96, 196, 768], P(None, 'dp'), may hold values from -6 to 6
- patch_keep: int32 [2, 96, 196], P(None, 'dp'), may hold values 0 or 1
- step_count: int32 [], replicated, may hold values from 2 to 20
Outputs:
- loss: float32 [], replicated
- grad_norm: float32 [], replicated
- new_attention_in: float32 [768, 1152], P('dp')
- new_attention_out: float32 [768, 384], P('dp')
- new_hidden_in: float32 [768, 1536], P('dp')
- new_hidden_out: float32 [3072, 384], P('dp')
- new_patch_weight: float32 [768, 384], P('dp')
- new_vector_rows: float32 [202, 384], replicated
- new_prototypes: float32 [1024, 384], P('dp')
- moment_attention_in: float32 [768, 1152], P('dp')
- moment_attention_out: float32 [768, 384], P('dp')
- moment_hidden_in: float32 [768, 1536], P('dp')
- moment_hidden_out: float32 [3072, 384], P('dp')
- moment_patch_weight: float32 [768, 384], P('dp')
- moment_vector_rows: float32 [202, 384], replicated
- moment_prototypes: float32 [1024, 384], P('dp')
- square_attention_in: float32 [768, 1152], P('dp')
- square_attention_out: float32 [768, 384], P('dp')
- square_hidden_in: float32 [768, 1536], P('dp')
- square_hidden_out: float32 [3072, 384], P('dp')
- square_patch_weight: float32 [768, 384], P('dp')
- square_vector_rows: float32 [202, 384], replicated
- square_prototypes: float32 [1024, 384], P('dp')
Inputs may be any that keep to these rules, and one draw needn't show every extreme that they name: `patch_keep`: 1 keeps a patch in the student's view, 0 drops it.
All inputs are finite; a program needn't handle non-finite values. No bound on the sum of `patch_keep` on one device may be relied on, other than what follows from the above.
Results may differ from a plain program's by a relative error of at most 0.014.
Values may be sent and summed in bfloat16 or wider, within the bound.
No kernel may reach another device: no remote copies, remote signals or barrier semaphores. Data moves between devices by JAX's collectives and lax.ppermute only.
A program may use at most 256 MiB of HBM per device.

v0:
```python
import jax
import jax.numpy as jnp
from jax import lax
from jax.experimental import pallas as pl
from jax.experimental.pallas import tpu as pltpu
from jax.sharding import PartitionSpec as P

D = 384
HEADS = 6
HEAD_DIM = 64
FF = 1536
PATCHES = 196
PATCH_DIM = 768
PROTOS = 1024
SEQ = 197
VROWS = 202
ROWS = 208
CLS = 196
CR = 16
SCALE = HEAD_DIM ** (-0.5)

student_softness = 0.04
teacher_sharpness = 0.02
clip_limit = 0.01
matrix_rate = 0.05
table_rate = 0.4
decay_rate = 0.05
beta_one = 0.9
beta_two = 0.999
adam_floor = 1e-08

f32 = jnp.float32
bf16 = jnp.bfloat16
GELU_C = 0.7978845608028654
GELU_A = 0.044715


def dot(a, b):
    return lax.dot_general(a, b, (((1,), (0,)), ((), ())), preferred_element_type=f32)


def dot_bt(a, b):
    return lax.dot_general(a, b, (((1,), (1,)), ((), ())), preferred_element_type=f32)


def dot_at(a, b):
    return lax.dot_general(a, b, (((0,), (0,)), ((), ())), preferred_element_type=f32)


def normalize(x):
    centre = x - jnp.sum(x, -1, keepdims=True) * (1.0 / D)
    spread = jnp.sum(centre * centre, -1, keepdims=True) * (1.0 / D)
    inverse = lax.rsqrt(spread + 1e-06)
    return centre * inverse, inverse


def norm_back(hat, inverse, gain, upstream):
    gain_slope = jnp.sum(upstream * hat, 0, keepdims=True)
    scaled = upstream * gain
    mean_one = jnp.sum(scaled, -1, keepdims=True) * (1.0 / D)
    mean_two = jnp.sum(scaled * hat, -1, keepdims=True) * (1.0 / D)
    return inverse * (scaled - mean_one - hat * mean_two), gain_slope


def gelu_parts(x, slope):
    square = x * x
    t = jnp.tanh(x * (GELU_C + (GELU_C * GELU_A) * square))
    half = 0.5 + 0.5 * t
    act = x * half
    if not slope:
        return act, None
    inner = GELU_C + (3.0 * GELU_C * GELU_A) * square
    return act, half + act * (1.0 - t) * inner


def half_masks():
    lane = lax.broadcasted_iota(jnp.int32, (1, 128), 1)
    first = jnp.where(lane < HEAD_DIM, 1.0, 0.0)
    return first.astype(bf16), (1.0 - first).astype(bf16)


def spot_masks():
    lane = lax.broadcasted_iota(jnp.int32, (1, 128), 1)
    return jnp.where(lane == HEAD_DIM, 1.0, 0.0).astype(bf16), jnp.where(lane == 0, 1.0, 0.0).astype(bf16)


def head_mask():
    row = lax.broadcasted_iota(jnp.int32, (CR, D), 0)
    lane = lax.broadcasted_iota(jnp.int32, (CR, D), 1)
    low = row * HEAD_DIM
    return jnp.where(jnp.logical_and(lane >= low, lane < low + HEAD_DIM), 1.0, 0.0)


def natural_down(ref, natural):
    for pair in range(8):
        rows = ref[pl.ds(48 * pair, 48), :].astype(f32)
        pieces = [rows[24 * b : 24 * (b + 1), D * j : D * (j + 1)] for b in range(2) for j in range(4)]
        natural[pl.ds(192 * pair, 192), :] = jnp.concatenate(pieces, 0).astype(bf16)


def natural_protos(ref, rest, natural):
    for pair in range(16):
        rows = ref[pl.ds(48 * pair, 48), :].astype(f32)
        tail = rest[pl.ds(48 * pair, 48), :].astype(f32)
        pieces = []
        for b in range(2):
            pieces.append(rows[24 * b : 24 * (b + 1)])
            pieces.append(jnp.concatenate([tail[24 * b + 8 * j : 24 * b + 8 * (j + 1)] for j in range(3)], 1))
        natural[pl.ds(64 * pair, 64), :] = jnp.concatenate(pieces, 0).astype(bf16)


def step_rows(ref, height):
    return ref.at[pl.ds(pl.multiple_of(pl.program_id(0) * height, 16), height)]


def layer_views(weights, packed, layer):
    if packed:
        (full,) = weights
        at = lambda name: full.at[pl.ds(D * layer, D), pl.ds(PLACE[name], WIDTHS[name])]
        return tuple(at(name) for name in ("mix", "out", "up", "down"))
    mix, out, up, down = weights[:4]
    rows = pl.ds(D * layer, D)
    return mix.at[rows], out.at[rows], up.at[rows], down.at[pl.ds(FF * layer, FF)]


def forward_kernel(save, packed, count, *refs):
    (pats, tab, bias_all, key_bias_all, gains, gains_one), refs = refs[:6], refs[6:]
    weights, refs = refs[: 1 if packed else 6], refs[1 if packed else 6 :]
    step = pl.program_id(0)
    group = pats.shape[1]
    height = group * ROWS
    pat = pats.at[pl.ds(step, 1)]
    if save:
        states, class_refs, naturals = refs[0], refs[8:18], refs[18:]
        out, first, mix, share, att, mid, act, dgelu = (step_rows(ref, height) if i != 3 else ref.at[pl.ds(step * group, group)] for i, ref in enumerate(refs[:8]))
    else:
        share = mid = act = dgelu = None
        (target, first, mix, att, kv, att_c, cls, states) = refs[:8]
        class_refs = (target, kv, att_c, cls)
        out = step_rows(states, height)
    win, wo, w1, w2 = layer_views(weights, packed, 0)
    if packed:
        down, down_one, protos = naturals
        wp = weights[0].at[:, pl.ds(PLACE["patch"], D)]

        @pl.when(step == 0)
        def _():
            natural_down(w2, down)

    else:
        wp, down = weights[4], w2
    group = pat.shape[1]
    table = tab[...]
    for g in range(group):
        embedded = dot(pat[0, g], wp[...])
        first[pl.ds(g * ROWS, PATCHES), :] = embedded + table[:PATCHES]
        first[pl.ds(g * ROWS + PATCHES, ROWS - PATCHES), :] = table[PATCHES:]
    state = first[...]
    hat, _ = normalize(state)
    normed = (hat * gains[0:1, :]).astype(bf16)
    mix[...] = dot(normed, win[...]).astype(bf16)
    masks, spots = half_masks(), spot_masks()

    for g in range(group):
        rows = pl.ds(g * ROWS, ROWS)
        key_bias = key_bias_all[step * group + g]
        for pair in range(HEADS // 2):
            query = mix[rows, pl.ds(128 * pair, 128)] * jnp.asarray(SCALE, bf16)
            keys = mix[rows, pl.ds(D + 128 * pair, 128)]
            values = mix[rows, pl.ds(2 * D + 128 * pair, 128)]
            total = None
            for half in range(2):
                scores = dot_bt(keys * masks[half] + key_bias * spots[half], query * masks[half] + spots[half])
                e = jnp.exp(scores - jnp.max(scores, 0, keepdims=True))
                p = (e * (1.0 / jnp.sum(e, 0, keepdims=True))).astype(bf16)
                if save:
                    share[g, 2 * pair + half] = p
                o = dot_at(p, values * masks[half])
                total = o if total is None else total + o
            att[rows, pl.ds(128 * pair, 128)] = total.astype(bf16)
    middle = first[...] + dot(att[...], wo[...])
    if save:
        mid[...] = middle
    hat, _ = normalize(middle)
    normed = (hat * gains[1:2, :]).astype(bf16)
    result = middle
    for j in range(FF // D):
        cols = pl.ds(D * j, D)
        a, slope = gelu_parts(dot(normed, w1[:, cols]), save)
        a = a.astype(bf16)
        if save:
            act[:, cols] = a
            dgelu[:, cols] = slope.astype(bf16)
        result = result + dot(a, down[cols, :])
    out[...] = result

    @pl.when(step == pl.num_programs(0) - 1)
    def _():
        win, wo, w1, w2 = layer_views(weights, packed, 1)
        if packed:
            natural_down(w2, down_one)
            natural_protos(weights[0].at[:, pl.ds(PLACE["protos"], D)], weights[0].at[:, pl.ds(PLACE["rest"], 128)], protos)
            late = (win, wo, w1, down_one, protos)
        else:
            late = (win, wo, w1, w2, weights[5])
        class_forward(save, count, states, bias_all, late, gains_one, class_refs)


def class_forward(student, count, state, bias, weights, gains, refs):
    win, wo, w1, w2, protos = weights
    if student:
        (logs, sums, kv, queries, shares, att, mid_c, expanded_out, last, cls) = refs
    else:
        (target, kv, att, cls) = refs
    hat, _ = normalize(state[...])
    normed = (hat * gains[0:1, :]).astype(bf16)
    kv[...] = dot(normed, win[:, D:]).astype(bf16)
    cls[...] = jnp.zeros((CR, D), f32)
    for g in range(count):
        cls[g : g + 1, :] = state[pl.ds(g * ROWS + CLS, 1), :]
    class_state = cls[...]
    hat, _ = normalize(class_state)
    query = dot((hat * gains[0:1, :]).astype(bf16), win[:, :D]).astype(bf16)
    if student:
        queries[...] = query
    mask = head_mask()
    for g in range(count):
        rows = pl.ds(g * ROWS, ROWS)
        spread = (jnp.broadcast_to(query[g : g + 1, :].astype(f32) * SCALE, (CR, D)) * mask).astype(bf16)
        scores = dot_bt(spread, kv[rows, pl.ds(0, D)]) + bias[g]
        e = jnp.exp(scores - jnp.max(scores, -1, keepdims=True))
        p = e * (1.0 / jnp.sum(e, -1, keepdims=True))
        if student:
            shares[g] = p
        o = dot(p.astype(bf16), kv[rows, pl.ds(D, D)])
        att[g : g + 1, :] = jnp.sum(o * mask, 0, keepdims=True)
    att[count:, :] = jnp.zeros((CR - count, D), f32)
    middle = class_state + dot(att[...].astype(bf16), wo[...])
    hat, _ = normalize(middle)
    expanded = dot((hat * gains[1:2, :]).astype(bf16), w1[...])
    act, _ = gelu_parts(expanded, False)
    result = middle + dot(act.astype(bf16), w2[...])
    if student:
        mid_c[...] = middle
        expanded_out[...] = expanded
        last[...] = result
    hat, _ = normalize(result)
    unit, _ = unit_parts(hat * gains[2:3, :])
    proto_unit, _ = unit_parts(protos[...].astype(f32))
    raw = dot_bt(unit.astype(bf16), proto_unit.astype(bf16))
    logits = raw * (1.0 / (student_softness if student else teacher_sharpness))
    logits = logits - jnp.max(logits, -1, keepdims=True)
    e = jnp.exp(logits)
    total = jnp.sum(e, -1, keepdims=True)
    if student:
        log_share = logits - jnp.log(total)
        logs[...] = log_share
        share = jnp.exp(log_share)
        row = lax.broadcasted_iota(jnp.int32, (CR, PROTOS), 0)
        per = count // 2
        lines = []
        for m in range(2):
            inside = jnp.logical_and(row >= m * per, row < (m + 1) * per)
            line = jnp.sum(jnp.where(inside, share, 0.0), 0, keepdims=True)
            lines += [line[:, 128 * k : 128 * (k + 1)] for k in range(PROTOS // 128)]
        lines = jnp.concatenate(lines, 0)
        for d in range(sums.shape[0]):
            sums[d] = lines.astype(bf16)
    else:
        target[...] = e / total


def forward(patches, table, bias, net, gains, gains_one, save, n):
    groups, group = patches.shape[:2]
    count = groups * group
    rows = count * ROWS
    step = group * ROWS
    packed = net["packed"]
    if save:
        out_shape = [
            jax.ShapeDtypeStruct((rows, D), f32),
            jax.ShapeDtypeStruct((rows, D), f32),
            jax.ShapeDtypeStruct((rows, 3 * D), bf16),
            jax.ShapeDtypeStruct((count, HEADS, ROWS, ROWS), bf16),
            jax.ShapeDtypeStruct((rows, D), bf16),
            jax.ShapeDtypeStruct((rows, D), f32),
            jax.ShapeDtypeStruct((rows, FF), bf16),
            jax.ShapeDtypeStruct((rows, FF), bf16),
            jax.ShapeDtypeStruct((CR, PROTOS), f32),
            jax.ShapeDtypeStruct((n, 16, 128), bf16),
            jax.ShapeDtypeStruct((rows, 2 * D), bf16),
            jax.ShapeDtypeStruct((CR, D), bf16),
            jax.ShapeDtypeStruct((count, CR, ROWS), f32),
            jax.ShapeDtypeStruct((CR, D), f32),
            jax.ShapeDtypeStruct((CR, D), f32),
            jax.ShapeDtypeStruct((CR, FF), f32),
            jax.ShapeDtypeStruct((CR, D), f32),
            jax.ShapeDtypeStruct((CR, D), f32),
        ]
        scratch = []
    else:
        out_shape = [jax.ShapeDtypeStruct((CR, PROTOS), f32)]
        scratch = [
            pltpu.VMEM((step, D), f32),
            pltpu.VMEM((step, 3 * D), bf16),
            pltpu.VMEM((step, D), bf16),
            pltpu.VMEM((rows, 2 * D), bf16),
            pltpu.VMEM((CR, D), f32),
            pltpu.VMEM((CR, D), f32),
            pltpu.VMEM((rows, D), f32),
        ]
    if packed:
        out_shape += [jax.ShapeDtypeStruct(shape, bf16) for shape in ((FF, D), (FF, D), (PROTOS, D))]
    key_bias = jnp.broadcast_to(bias.reshape(count, ROWS, 1).astype(bf16), (count, ROWS, 128))
    operands = (patches, table, bias, key_bias, gains, gains_one, *net["arrays"])
    return pl.pallas_call(
        lambda *refs: forward_kernel(save, packed, count, *refs),
        grid=(groups,),
        in_specs=[whole()] * len(operands),
        out_specs=[whole()] * len(out_shape),
        out_shape=out_shape,
        scratch_shapes=scratch,
        compiler_params=pltpu.CompilerParams(dimension_semantics=("arbitrary",), vmem_limit_bytes=megabytes(LIMITS[0 if save else 1])),
        cost_estimate=cost(30),
        name="student_forward" if save else "teacher_forward",
    )(*operands)


LIMITS = [12, 18, 20, 14, 14, 10]


def megabytes(count):
    return count * 1024 * 1024


def cost(micros):
    return pl.CostEstimate(flops=int(micros * 1e9), transcendentals=0, bytes_accessed=int(micros * 3e6))


def unit_parts(v):
    inverse = lax.rsqrt(jnp.sum(v * v, -1, keepdims=True) + 1e-06)
    return v * inverse, inverse


def whole():
    return pl.BlockSpec(memory_space=pltpu.VMEM)


def class_back_kernel(packed, count, inverse_count, *refs):
    (logs, target, mean_sum, state, kv, queries, shares, att, mid_c, expanded, last, cls) = refs[:12]
    if packed:
        (me, gains, full, w2, protos), refs = refs[12:17], refs[17:]
        (delta, s_gain, report, keep, send, dkv, dq_all, s_up, s_down) = refs
        s_proto, s_in, s_out = s_down.at[pl.ds(0, PROTOS)], s_up.at[:, pl.ds(0, 3 * D)], s_up.at[:, pl.ds(3 * D, D)]
        win, wo, w1, _ = layer_views((full,), True, 1)
    else:
        gains, weights = refs[12], refs[13:19]
        (delta, s_gain, report, s_in, s_out, s_up, s_down, s_proto, dkv, dq_all) = refs[19:]
        (win, wo, w1, w2), protos = layer_views(weights, False, 1), weights[5]
    mask = head_mask()
    row = lax.broadcasted_iota(jnp.int32, (CR, 1), 0)
    live = row < count
    log_share = logs[...]
    share = jnp.exp(log_share)
    targets = target[...]
    total = mean_sum[0].astype(f32)
    for device in range(1, mean_sum.shape[0]):
        total = total + mean_sum[device].astype(f32)
    lines = [jnp.concatenate([total[8 * m + k : 8 * m + k + 1] for k in range(PROTOS // 128)], 1) for m in range(2)]
    mean_share = jnp.concatenate(lines, 0) * (2.0 * inverse_count)
    log_mean = jnp.log(mean_share)
    cross = -jnp.sum(jnp.where(live, targets * log_share, 0.0), -1, keepdims=True)
    cross = jnp.sum(cross, 0, keepdims=True) * inverse_count
    entropy = jnp.sum(jnp.sum(mean_share * log_mean, -1, keepdims=True), 0, keepdims=True) * 0.5
    lane = lax.broadcasted_iota(jnp.int32, (8, 128), 1)
    report[...] = jnp.where(lane == 0, cross, jnp.where(lane == 1, entropy, 0.0))
    log_row = jnp.where(row < count // 2, log_mean[0:1, :], log_mean[1:2, :])
    slope = share - targets + share * (log_row - jnp.sum(share * log_row, -1, keepdims=True))
    slope = jnp.where(live, slope * (inverse_count / student_softness), 0.0).astype(bf16)
    hat_f, inv_f = normalize(last[...])
    summary = hat_f * gains[2:3, :]
    unit, inv_u = unit_parts(summary)
    proto = protos[...].astype(f32)
    proto_unit, inv_p = unit_parts(proto)
    d_unit = dot(slope, proto_unit.astype(bf16))
    d_proto = dot_at(slope, unit.astype(bf16))
    s_proto[...] = inv_p * (d_proto - proto_unit * jnp.sum(proto_unit * d_proto, -1, keepdims=True))
    if packed:
        pack_blocks(me[0], keep, send, [], [(s_proto, 32)], 288)
    d_summary = inv_u * (d_unit - unit * jnp.sum(unit * d_unit, -1, keepdims=True))
    d, gain_f = norm_back(hat_f, inv_f, gains[2:3, :], d_summary)
    s_gain[...] = jnp.zeros((8, D), f32)
    s_gain[2:3, :] = gain_f
    d_low = d.astype(bf16)
    act, gslope = gelu_parts(expanded[...], True)
    s_down[...] = dot_at(act.astype(bf16), d_low)
    d_exp = (dot_bt(d_low, w2[...]) * gslope).astype(bf16)
    if packed:
        pack_blocks(me[0], keep, send, [(s_down, 96)], [], 192)
    hat_m, inv_m = normalize(mid_c[...])
    s_up[...] = dot_at((hat_m * gains[1:2, :]).astype(bf16), d_exp)
    d_mid, gain_two = norm_back(hat_m, inv_m, gains[1:2, :], dot_bt(d_exp, w1[...]))
    s_gain[1:2, :] = gain_two
    if packed:
        pack_blocks(me[0], keep, send, [(s_up, 24)], [], 96)
    d_mid = d + d_mid
    d_mid_low = d_mid.astype(bf16)
    s_out[...] = dot_at(att[...].astype(bf16), d_mid_low)
    d_att = dot_bt(d_mid_low, wo[...]).astype(bf16)
    dq_all[...] = jnp.zeros((CR, D), f32)
    for g in range(count):
        rows = pl.ds(g * ROWS, ROWS)
        d_spread = (jnp.broadcast_to(d_att[g : g + 1, :].astype(f32), (CR, D)) * mask).astype(bf16)
        q_spread = (jnp.broadcast_to(queries[g : g + 1, :].astype(f32) * SCALE, (CR, D)) * mask).astype(bf16)
        p = shares[g]
        d_p = dot_bt(d_spread, kv[rows, pl.ds(D, D)])
        d_s = (p * (d_p - jnp.sum(p * d_p, -1, keepdims=True))).astype(bf16)
        dkv[rows, pl.ds(D, D)] = dot_at(p.astype(bf16), d_spread).astype(bf16)
        dkv[rows, pl.ds(0, D)] = dot_at(d_s, q_spread).astype(bf16)
        dq = dot(d_s, kv[rows, pl.ds(0, D)]) * mask
        dq_all[g : g + 1, :] = jnp.sum(dq, 0, keepdims=True) * SCALE
    dq_low = dq_all[...].astype(bf16)
    hat_c, _ = normalize(cls[...])
    s_in[:, :D] = dot_at((hat_c * gains[0:1, :]).astype(bf16), dq_low)
    hat, inv = normalize(state[...])
    s_in[:, D:] = dot_at((hat * gains[0:1, :]).astype(bf16), dkv[...])
    d_class = dot_bt(dq_low, win[:, :D])
    delta[...] = dot_bt(dkv[...], win[:, D:])
    for g in range(count):
        one = pl.ds(g * ROWS + CLS, 1)
        delta[one, :] = delta[one, :] + d_class[g : g + 1, :]
    d_state, gain_one = norm_back(hat, inv, gains[0:1, :], delta[...])
    s_gain[0:1, :] = gain_one
    delta[...] = d_state
    for g in range(count):
        one = pl.ds(g * ROWS + CLS, 1)
        delta[one, :] = delta[one, :] + d_mid[g : g + 1, :]
    if packed:
        pack_blocks(me[0], keep, send, [(s_up, 24)], [], 0)


BITS = {"c": 0, "x": 1, "y": 2, "z": 3}
PATHS = (("c", "x", "y", "z"), ("c", "y", "z", "x"), ("c", "z", "x", "y"))
LAYER_ROWS = 288
CHUNK_ROWS = (352, 192, 160)


def pack_blocks(me, keep, send, layered, wide, start=0):
    for path in range(3):
        for place in range(16):
            mask = 0
            for k in range(4):
                mask |= ((place >> (3 - k)) & 1) << BITS[PATHS[path][k]]
            owner = (me & 15) ^ mask
            pieces = []
            for ref, rows in layered:
                at = pl.ds(pl.multiple_of(owner * rows, 8), rows)
                for j in range(ref.shape[1] // D):
                    pieces.append(ref[at, pl.ds(D * j + 128 * path, 128)])
            for other in range(2):
                half = (me >> 4) ^ other
                for ref, rows in wide:
                    at = pl.ds(pl.multiple_of((half * 16 + owner) * rows, 8), rows)
                    pieces.append(ref[at, pl.ds(128 * path, 128)])
            value = jnp.concatenate(pieces, 0).astype(bf16)
            target, at = (keep, place) if place < 8 else (send, place - 8)
            target[path, at, pl.ds(start, value.shape[0]), :] = value


def chunk_shapes(chunk):
    return [jax.ShapeDtypeStruct((3, 8, CHUNK_ROWS[chunk], 128), bf16)] * 2


def layer_one_back(args, net, gains, inverse_count, me):
    count = args[6].shape[0]
    packed = net["fast"]
    weights = (net["arrays"][0], *net["natural"][1:]) if packed else net["arrays"]
    rows = count * ROWS
    slopes = [(D, 3 * D), (D, D), (D, FF), (FF, D), (PROTOS, D)]
    out_shape = [
        jax.ShapeDtypeStruct((rows, D), f32),
        jax.ShapeDtypeStruct((8, D), f32),
        jax.ShapeDtypeStruct((8, 128), f32),
    ]
    scratch = [pltpu.VMEM((rows, 2 * D), bf16), pltpu.VMEM((CR, D), f32)]
    if packed:
        out_shape += chunk_shapes(0)
        scratch += [pltpu.VMEM(shape, f32) for shape in ((D, FF), (FF, D))]
    else:
        out_shape += [jax.ShapeDtypeStruct(shape, f32) for shape in slopes]
    scalar = [pl.BlockSpec(memory_space=pltpu.SMEM)] if packed else []
    return pl.pallas_call(
        lambda *refs: class_back_kernel(packed, count, inverse_count, *refs),
        in_specs=[whole()] * 12 + scalar + [whole()] * (1 + len(weights)),
        out_specs=[whole()] * len(out_shape),
        out_shape=out_shape,
        scratch_shapes=scratch,
        compiler_params=pltpu.CompilerParams(vmem_limit_bytes=megabytes(LIMITS[2])),
        cost_estimate=cost(13),
        name="layer_one_back",
    )(*args, *([me] if packed else []), gains, *weights)


def mlp_back_kernel(packed, group, *refs):
    (delta, act, dgelu, mid), (gains, ups, downs), refs = (step_rows(ref, group * ROWS) for ref in refs[:4]), refs[4:7], refs[7:]
    w1 = layer_views((ups,), True, 0)[2] if packed else ups.at[pl.ds(0, D)]
    w2 = downs.at[pl.ds(0, FF)]
    first = pl.program_id(0) == 0
    if packed:
        me, d_mid, s_gain, keep, send, s_up, s_down = refs
    else:
        d_mid, s_gain, s_up, s_down = refs
    d_mid = step_rows(d_mid, group * ROWS)

    @pl.when(first)
    def _():
        s_up[...] = jnp.zeros(s_up.shape, f32)
        s_down[...] = jnp.zeros(s_down.shape, f32)
        s_gain[...] = jnp.zeros(s_gain.shape, f32)

    d = delta[...]
    d_low = d.astype(bf16)
    hat, inv = normalize(mid[...])
    normed = (hat * gains[1:2, :]).astype(bf16)
    d_normed = None
    for j in range(FF // D):
        cols = pl.ds(D * j, D)
        s_down[cols, :] += dot_at(act[:, cols], d_low)
        d_exp = (dot_bt(d_low, w2[cols, :]) * dgelu[:, cols].astype(f32)).astype(bf16)
        s_up[:, cols] += dot_at(normed, d_exp)
        part = dot_bt(d_exp, w1[:, cols])
        d_normed = part if d_normed is None else d_normed + part
    back, gain = norm_back(hat, inv, gains[1:2, :], d_normed)
    s_gain[0:1, :] += gain
    d_mid[...] = d + back
    if packed:

        @pl.when(pl.program_id(0) == pl.num_programs(0) - 1)
        def _():
            pack_blocks(me[0], keep, send, [(s_up, 24), (s_down, 96)], [])


def backward_shapes(packed, slopes, chunk):
    if packed:
        return chunk_shapes(chunk), [pltpu.VMEM(shape, f32) for shape in slopes]
    return [jax.ShapeDtypeStruct(shape, f32) for shape in slopes], []


def layer_zero_mlp_back(delta, act, dgelu, mid, net, gains, group, me):
    packed = net["fast"]
    weights = (net["arrays"][0], net["natural"][0]) if packed else net["arrays"][2:4]
    slopes, scratch = backward_shapes(packed, [(D, FF), (FF, D)], 1)
    scalar = [pl.BlockSpec(memory_space=pltpu.SMEM)] if packed else []
    rows = delta.shape[0]
    step = group * ROWS
    return pl.pallas_call(
        lambda *refs: mlp_back_kernel(packed, group, *refs),
        grid=(rows // step,),
        in_specs=[whole()] * 7 + scalar,
        out_specs=[whole()] * (2 + len(slopes)),
        out_shape=[jax.ShapeDtypeStruct((rows, D), f32), jax.ShapeDtypeStruct((8, D), f32)] + slopes,
        scratch_shapes=scratch,
        compiler_params=pltpu.CompilerParams(dimension_semantics=("arbitrary",), vmem_limit_bytes=megabytes(LIMITS[3])),
        cost_estimate=cost(17),
        name="layer_zero_mlp_back",
    )(delta, act, dgelu, mid, gains, *weights, *([me] if packed else []))


def attention_back_kernel(packed, group, *refs):
    (d_mid, state, mix, att) = (step_rows(ref, group * ROWS) for ref in refs[:4])
    if packed:
        (shares, pats, mixes, gains, gain_two, gain_one), refs = refs[4:10], refs[10:]
    else:
        (shares, pats, mixes, outs, gains, gain_two, gain_one), refs = refs[4:11], refs[11:]
    base = pl.program_id(0) * group
    share = shares.at[pl.ds(base, group)]
    win, wo = layer_views((mixes,), True, 0)[:2] if packed else (mixes.at[pl.ds(0, D)], outs.at[pl.ds(0, D)])
    if packed:
        me, keep, send, s_in, s_out, s_patch, s_vector, d_att, dmix = refs
    else:
        s_in, s_out, s_patch, s_vector, d_att, dmix = refs

    @pl.when(pl.program_id(0) == 0)
    def _():
        s_in[...] = jnp.zeros(s_in.shape, f32)
        s_out[...] = jnp.zeros(s_out.shape, f32)
        s_patch[...] = jnp.zeros(s_patch.shape, f32)
        s_vector[...] = jnp.zeros(s_vector.shape, f32)
        s_vector[ROWS + 1 : ROWS + 2, :] = gain_two[0:1, :]
        s_vector[ROWS + 2 : ROWS + 5, :] = gain_one[0:3, :]

    d_low = d_mid[...].astype(bf16)
    s_out[...] += dot_at(att[...], d_low)
    d_att[...] = dot_bt(d_low, wo[...]).astype(bf16)
    masks = half_masks()
    for g in range(group):
        rows = pl.ds(g * ROWS, ROWS)
        for pair in range(HEADS // 2):
            lanes = [pl.ds(D * part + 128 * pair, 128) for part in range(3)]
            query = mix[rows, lanes[0]] * jnp.asarray(SCALE, bf16)
            keys = mix[rows, lanes[1]] * jnp.asarray(SCALE, bf16)
            values = mix[rows, lanes[2]]
            upstream = d_att[rows, lanes[0]]
            dq = dk = dv = None
            for half in range(2):
                p = share[g, 2 * pair + half]
                up = upstream * masks[half]
                d_p = dot_bt(values, up)
                p_wide = p.astype(f32)
                weighted = p_wide * d_p
                d_s = (weighted - p_wide * jnp.sum(weighted, 0, keepdims=True)).astype(bf16)
                parts = (
                    dot_at(d_s, keys * masks[half]),
                    dot(d_s, query * masks[half]),
                    dot(p, up),
                )
                dq, dk, dv = parts if dq is None else (dq + parts[0], dk + parts[1], dv + parts[2])
            dmix[rows, lanes[0]] = dq.astype(bf16)
            dmix[rows, lanes[1]] = dk.astype(bf16)
            dmix[rows, lanes[2]] = dv.astype(bf16)
    hat, inv = normalize(state[...])
    normed = (hat * gains[0:1, :]).astype(bf16)
    s_in[...] += dot_at(normed, dmix[...])
    back, gain = norm_back(hat, inv, gains[0:1, :], dot_bt(dmix[...], win[...]))
    s_vector[ROWS : ROWS + 1, :] += gain
    d_state = d_mid[...] + back
    for g in range(group):
        one = d_state[g * ROWS : (g + 1) * ROWS]
        s_vector[0:ROWS, :] += one
        image = base + g
        s_patch[...] += dot_at(pats[image // pats.shape[1], image % pats.shape[1]], one[:PATCHES].astype(bf16))
    if packed:

        @pl.when(pl.program_id(0) == pl.num_programs(0) - 1)
        def _():
            pack_blocks(me[0], keep, send, [(s_in, 24), (s_out, 24)], [(s_patch, 24), (s_vector, 8)])


VECTORS = 256


def layer_zero_attention_back(d_mid, state, mix, share, att, patches, net, gains, gain_two, gain_one, group, me):
    packed = net["fast"]
    weights = net["arrays"][:1] if packed else net["arrays"][:2]
    slopes, scratch = backward_shapes(packed, [(D, 3 * D), (D, D), (PATCH_DIM, D), (VECTORS, D)], 2)
    scalar = [pl.BlockSpec(memory_space=pltpu.SMEM)] if packed else []
    rows = d_mid.shape[0]
    step = group * ROWS
    return pl.pallas_call(
        lambda *refs: attention_back_kernel(packed, group, *refs),
        grid=(rows // step,),
        in_specs=[whole()] * (9 + len(weights)) + scalar,
        out_specs=[whole()] * len(slopes),
        out_shape=slopes,
        scratch_shapes=scratch + [pltpu.VMEM((step, D), bf16), pltpu.VMEM((step, 3 * D), bf16)],
        compiler_params=pltpu.CompilerParams(dimension_semantics=("arbitrary",), vmem_limit_bytes=megabytes(LIMITS[4])),
        cost_estimate=cost(21),
        name="layer_zero_attention_back",
    )(d_mid, state, mix, att, share, patches, *weights, gains, gain_two, gain_one, *([me] if packed else []))


NAMES = ("mix", "out", "up", "down", "patch", "protos")
WIDTHS = {"up": FF, "down": FF, "patch": D, "mix": 3 * D, "out": D, "protos": D, "rest": 128}
PLACE = {}
COLUMNS = 0
for _key in WIDTHS:
    PLACE[_key] = COLUMNS
    COLUMNS += WIDTHS[_key]


def pack_pieces(values):
    pieces = {name: values[name] for name in ("mix", "out", "up", "patch")}
    r = values["patch"].shape[0]
    down, protos = values["down"], values["protos"]
    pieces["down"] = jnp.concatenate([down[r * j : r * (j + 1)] for j in range(4)], 1)
    pieces["protos"] = protos[:r]
    pieces["rest"] = jnp.concatenate([protos[r:, 128 * j : 128 * (j + 1)] for j in range(3)], 0)
    return pieces


def pack_kernel(*refs):
    for net in range(2):
        out = refs[12 + net]
        values = {name: ref[...].astype(f32) for name, ref in zip(NAMES, refs[6 * net : 6 * net + 6])}
        for name, piece in pack_pieces(values).items():
            out[:, pl.ds(PLACE[name], WIDTHS[name])] = piece.astype(bf16)


THIRDS = ((0, 1792), (1792, 3584), (3584, 5504))


def chain_gather(mine):
    got = swap(mine, 4)
    arrays = [jnp.stack([mine[:, a:b], got[:, a:b]]) for a, b in THIRDS]
    for stage in (1, 2, 3):
        got = [swap(arrays[path], BITS[PATHS[path][stage]]) for path in range(3)]
        arrays = [jnp.concatenate([a, g], 0) for a, g in zip(arrays, got)]
    return arrays, [swap(a, 0) for a in arrays]


CHIPS_A_STEP = 4


def unpack_kernel(me, *refs):
    ins, outs = refs[: 6 * CHIPS_A_STEP], dict(zip(NAMES, refs[6 * CHIPS_A_STEP :]))
    first_core = (me[0] & 1) == 0
    pieces = {name: [] for name in NAMES}
    for chip in range(CHIPS_A_STEP):
        mine, got = ins[6 * chip : 6 * chip + 3], ins[6 * chip + 3 : 6 * chip + 6]
        own = jnp.concatenate([ref[0].astype(f32) for ref in mine], 1)
        other = jnp.concatenate([ref[0].astype(f32) for ref in got], 1)
        for rows in (jnp.where(first_core, own, other), jnp.where(first_core, other, own)):
            for name in ("mix", "out", "up", "patch"):
                pieces[name].append(rows[:, PLACE[name] : PLACE[name] + WIDTHS[name]])
            for j in range(4):
                pieces["down"].append(rows[:, PLACE["down"] + D * j : PLACE["down"] + D * (j + 1)])
            rest = rows[:, PLACE["rest"] :]
            pieces["protos"].append(rows[:, PLACE["protos"] : PLACE["protos"] + D])
            pieces["protos"].append(jnp.concatenate([rest[8 * j : 8 * (j + 1)] for j in range(3)], 1))
    for name in NAMES:
        outs[name][...] = jnp.concatenate(pieces[name], 0).astype(bf16)


def unpack_weights(arrays, got, me):
    def index(chip, path):
        def at(i, me_ref):
            other = (CHIPS_A_STEP * i + chip) ^ (me_ref[0] >> 1)
            place = (other >> 3) & 1
            for k in range(3):
                place = place + (((other >> (BITS[PATHS[path][k + 1]] - 1)) & 1) << (k + 1))
            return place, 0, 0

        return at

    in_specs, operands = [], []
    for chip in range(CHIPS_A_STEP):
        for source in (arrays, got):
            for path in range(3):
                in_specs.append(pl.BlockSpec((1,) + source[path].shape[1:], index(chip, path)))
                operands.append(source[path])
    shapes = ((2 * D, 3 * D), (2 * D, D), (2 * D, FF), (2 * FF, D), (PATCH_DIM, D), (PROTOS, D))
    steps = 16 // CHIPS_A_STEP
    return pl.pallas_call(
        unpack_kernel,
        grid_spec=pltpu.PrefetchScalarGridSpec(
            num_scalar_prefetch=1,
            grid=(steps,),
            in_specs=in_specs,
            out_specs=[pl.BlockSpec((a // steps, b), lambda i, me_ref: (i, 0)) for a, b in shapes],
        ),
        out_shape=[jax.ShapeDtypeStruct(shape, bf16) for shape in shapes],
        compiler_params=pltpu.CompilerParams(dimension_semantics=("arbitrary",), vmem_limit_bytes=megabytes(LIMITS[5])),
        cost_estimate=cost(9),
        name="unpack_weights",
    )(me, *operands)


def natural_net(mix, out, up, down, patch, protos, fast):
    return {"packed": False, "fast": fast, "arrays": (mix, out, up, down, patch, protos)}


def gathered_net(full):
    return {"packed": True, "fast": True, "arrays": (full,)}


def plain_net(full, n):
    r = full.shape[0] // n
    part = lambda name: full[:, PLACE[name] : PLACE[name] + WIDTHS[name]]
    down = part("down").reshape(n, r, 4, D).transpose(0, 2, 1, 3).reshape(2 * FF, D)
    rest = part("rest").reshape(n, 3, r // 3, 128).transpose(0, 2, 1, 3).reshape(n, r // 3, D)
    protos = jnp.concatenate([part("protos").reshape(n, r, D), rest], 1).reshape(PROTOS, D)
    return natural_net(part("mix"), part("out"), part("up"), down, part("patch"), protos, False)


def gather_networks(student, teacher, me, n):
    gather = lambda rows: lax.all_gather(rows, "dp", axis=0, tiled=True)
    r = student[0].shape[0]
    if n != 32:
        nets = []
        for shards in (student, teacher):
            pieces = pack_pieces(dict(zip(NAMES, shards)))
            nets.append(plain_net(gather(jnp.concatenate([pieces[name].astype(bf16) for name in WIDTHS], 1)), n))
        return nets
    student_rows, teacher_rows = pl.pallas_call(
        pack_kernel,
        in_specs=[whole()] * 12,
        out_specs=[whole()] * 2,
        out_shape=[jax.ShapeDtypeStruct((r, COLUMNS), bf16)] * 2,
        cost_estimate=cost(2),
        name="pack_weights",
    )(*student, *teacher)
    full = gather(student_rows)
    arrays, got = chain_gather(teacher_rows)
    return gathered_net(full), natural_net(*unpack_weights(arrays, got, me), True)


def swap(value, bit):
    size = lax.axis_size("dp")
    return lax.ppermute(value, "dp", [(i, i ^ (1 << bit)) for i in range(size)])


def core_stage(parts):
    got = [swap(send, 0) for _, send in parts]
    one, mlp, rest = [(keep.astype(f32) + g.astype(f32)).astype(bf16) for (keep, _), g in zip(parts, got)]

    def join(path, places):
        a, b, c = one[path, places], mlp[path, places], rest[path, places]
        return jnp.concatenate([a[:, :288], c[:, :96], b, a[:, 288:320], c[:, 96:128], a[:, 320:], c[:, 128:]], 1)

    return [(join(path, slice(0, 4)), join(path, slice(4, 8))) for path in range(3)]


def axis_stage(stage, arrays):
    got = [swap(arrays[path][1], BITS[PATHS[path][stage]]) for path in range(3)]
    total = [arrays[path][0].astype(f32) + got[path].astype(f32) for path in range(3)]
    if stage == 3:
        return jnp.concatenate(total, 0)
    half = total[0].shape[0] // 2
    total = [t.astype(bf16) for t in total]
    return [(t[:half], t[half:]) for t in total]


def scatter_gradients(parts, me):
    arrays = core_stage(parts)
    for stage in (1, 2, 3):
        arrays = axis_stage(stage, arrays)
    upper = (me[0] >> 4) == 1
    one, zero = arrays[:, :288], arrays[:, 288:576]
    keep = jnp.concatenate([jnp.where(upper, one, zero), arrays[:, 576:640]], 1)
    send = jnp.concatenate([jnp.where(upper, zero, one), arrays[:, 640:]], 1)
    return keep, swap(send.astype(bf16), 4)


def square_sum(value):
    return jnp.sum(jnp.sum(value * value, -1, keepdims=True), 0, keepdims=True)


def three_parts(value):
    high = value.astype(bf16).astype(f32)
    middle = (value - high).astype(bf16).astype(f32)
    return high, middle, value - high - middle


def collect_kernel(*refs):
    (keep, got, report) = refs[:3]
    (mix, out, up, down, patch, protos, line) = refs[3:]
    vectors = []
    for path in range(3):
        a = keep[path] + got[path].astype(f32)
        lanes = pl.ds(128 * path, 128)
        for j in range(3):
            mix[:, pl.ds(D * j + 128 * path, 128)] = a[24 * j : 24 * (j + 1)]
        out[:, lanes] = a[72:96]
        for j in range(4):
            up[:, pl.ds(D * j + 128 * path, 128)] = a[96 + 24 * j : 120 + 24 * j]
        down[:, lanes] = a[192:288]
        protos[:, lanes] = a[288:320]
        patch[:, lanes] = a[320:344]
        vectors.append(a[344:352])
    write_line(line, (mix, out, up, down, patch, protos), jnp.concatenate(vectors, 1), report)


def write_line(line, slopes, vectors, report):
    squares = square_sum(vectors)
    for ref in slopes:
        squares = squares + square_sum(ref[...])
    cross = report[0:1, 0:1]
    rows = vectors.shape[0]
    lane = lax.broadcasted_iota(jnp.int32, (rows, 128), 1)
    row = lax.broadcasted_iota(jnp.int32, (rows, 128), 0)
    tail = jnp.zeros((rows, 128), f32)
    for i, part in enumerate(three_parts(squares) + three_parts(cross)):
        tail = jnp.where(jnp.logical_and(lane == i, row == 0), part, tail)
    full = jnp.concatenate([vectors, tail], 1).astype(bf16)
    for d in range(line.shape[0]):
        line[d] = full


RATES = (matrix_rate,) * 5 + (table_rate,) * 2


def update_kernel(rows, *refs):
    (fixes, report, arrived), refs = refs[:3], refs[3:]
    slopes, masters, firsts, seconds = refs[:6], refs[6:13], refs[13:20], refs[20:27]
    news, moments, squares, scalars, vector = refs[27:34], refs[34:41], refs[41:48], refs[48:50], refs[50]
    tail = jnp.zeros((1, 128), f32)
    for d in range(arrived.shape[0]):
        tail = tail + arrived[d, 0:1, pl.ds(D, 128)].astype(f32)
    lane = lax.broadcasted_iota(jnp.int32, (1, 128), 1)
    norm = jnp.sqrt(jnp.sum(jnp.where(lane < 3, tail, 0.0), -1, keepdims=True))
    cross = jnp.sum(jnp.where(jnp.logical_and(lane >= 3, lane < 6), tail, 0.0), -1, keepdims=True)
    loss = cross + report[0:1, 1:2]
    scalars[0][...] = loss
    scalars[1][...] = norm
    factor = jnp.minimum(1.0, clip_limit / (norm + 1e-06))
    per_device = arrived.shape[1]
    table = jnp.concatenate([arrived[d, :, pl.ds(0, D)].astype(f32) for d in range(arrived.shape[0])], 0)
    vector[0:1, :] = table[CLS : CLS + 1]
    vector[1:SEQ, :] = table[:PATCHES]
    vector[SEQ:VROWS, :] = table[ROWS : ROWS + 5]
    scale_one, scale_two = 1.0 / fixes[0], 1.0 / fixes[1]
    order = (0, 1, 2, 3, 4, None, 5)
    for i in range(7):
        slope = vector if order[i] is None else slopes[order[i]]
        clipped = slope[...] * factor
        moment = beta_one * firsts[i][...] + (1.0 - beta_one) * clipped
        square = beta_two * seconds[i][...] + (1.0 - beta_two) * clipped * clipped
        stepped = (moment * scale_one) / (jnp.sqrt(square * scale_two) + adam_floor)
        weight = masters[i][...]
        news[i][...] = weight - RATES[i] * (stepped + decay_rate * weight)
        moments[i][...] = moment
        squares[i][...] = square


def update_rows(slopes, arrived, report, masters, firsts, seconds, fixes):
    shapes = [jax.ShapeDtypeStruct(w.shape, f32) for w in masters]
    out_shape = shapes * 3 + [jax.ShapeDtypeStruct((1, 1), f32)] * 2
    return pl.pallas_call(
        lambda *refs: update_kernel(None, *refs),
        in_specs=[pl.BlockSpec(memory_space=pltpu.SMEM)] + [whole()] * 29,
        out_specs=[whole()] * len(out_shape),
        out_shape=out_shape,
        scratch_shapes=[pltpu.VMEM((VROWS, D), f32)],
        compiler_params=pltpu.CompilerParams(vmem_limit_bytes=megabytes(LIMITS[5])),
        cost_estimate=cost(4),
        name="update_rows",
    )(fixes, report, arrived, *slopes, *masters, *firsts, *seconds)


def update_plain(slopes, arrived, report, masters, firsts, seconds, fixes):
    tail = jnp.sum(arrived[:, 0, D:].astype(f32), 0)
    table = arrived[:, :, :D].astype(f32).reshape(-1, D)
    vector = jnp.concatenate([table[CLS : CLS + 1], table[:PATCHES], table[ROWS : ROWS + 5]], 0)
    norm = jnp.sqrt(tail[0] + tail[1] + tail[2])
    loss = tail[3] + tail[4] + tail[5] + report[0, 1]
    factor = jnp.minimum(1.0, clip_limit / (norm + 1e-06))
    slopes = list(slopes[:5]) + [vector, slopes[5]]
    news, moments, squares = ([], [], [])
    for weight, first, second, slope, rate in zip(masters, firsts, seconds, slopes, RATES):
        clipped = slope * factor
        moment = beta_one * first + (1.0 - beta_one) * clipped
        square = beta_two * second + (1.0 - beta_two) * clipped * clipped
        stepped = moment / fixes[0] / (jnp.sqrt(square / fixes[1]) + adam_floor)
        news.append(weight - rate * (stepped + decay_rate * weight))
        moments.append(moment)
        squares.append(square)
    return (*news, *moments, *squares, loss[None, None], norm[None, None])


def collect(keep, got, report, n, r):
    shapes = [(r, 3 * D), (r, D), (r, FF), (4 * r, D), (r, D), (4 * r // 3, D)]
    out_shape = [jax.ShapeDtypeStruct(shape, f32) for shape in shapes] + [jax.ShapeDtypeStruct((n, VECTORS // n, 512), bf16)]
    *slopes, line = pl.pallas_call(
        collect_kernel,
        in_specs=[whole()] * 3,
        out_specs=[whole()] * len(out_shape),
        out_shape=out_shape,
        compiler_params=pltpu.CompilerParams(vmem_limit_bytes=megabytes(LIMITS[5])),
        cost_estimate=cost(3),
        name="collect_gradients",
    )(keep, got, report)
    return slopes, line


def collect_plain(one, mlp, rest, report, n):
    mix1, out1, up1, down1, protos = one
    up0, down0 = mlp
    mix0, out0, patch, vectors = rest
    scatter = lambda *v: lax.psum_scatter(jnp.concatenate(v, 0), "dp", scatter_dimension=0, tiled=True)
    slopes = [scatter(mix0, mix1), scatter(out0, out1), scatter(up0, up1), scatter(down0, down1), scatter(patch), scatter(protos)]
    vectors = scatter(vectors)
    squares = sum(jnp.sum(s * s) for s in slopes) + jnp.sum(vectors * vectors)
    tail = jnp.stack(three_parts(squares) + three_parts(report[0, 0]))
    tail = jnp.zeros((vectors.shape[0], 128), f32).at[0, :6].set(tail)
    line = jnp.concatenate([vectors, tail], 1).astype(bf16)
    return slopes, jnp.broadcast_to(line[None], (n,) + line.shape)


def local(
    attention_in, attention_out, hidden_in, hidden_out, patch_weight, vector_rows, prototypes,
    first_attention_in, first_attention_out, first_hidden_in, first_hidden_out, first_patch_weight, first_vector_rows, first_prototypes,
    second_attention_in, second_attention_out, second_hidden_in, second_hidden_out, second_patch_weight, second_vector_rows, second_prototypes,
    teacher_attention_in, teacher_attention_out, teacher_hidden_in, teacher_hidden_out, teacher_patch_weight, teacher_vector_rows, teacher_prototypes,
    anchor_patches, target_patches, patch_keep, step_count,
):
    n = lax.axis_size("dp")
    me = lax.axis_index("dp").astype(jnp.int32)[None]
    groups, per = anchor_patches.shape[:2]
    count = groups * per
    inverse_count = 1.0 / (count * n)
    masters = (attention_in, attention_out, hidden_in, hidden_out, patch_weight, vector_rows, prototypes)
    firsts = (first_attention_in, first_attention_out, first_hidden_in, first_hidden_out, first_patch_weight, first_vector_rows, first_prototypes)
    seconds = (second_attention_in, second_attention_out, second_hidden_in, second_hidden_out, second_patch_weight, second_vector_rows, second_prototypes)
    student, teacher = gather_networks(
        (attention_in, attention_out, hidden_in, hidden_out, patch_weight, prototypes),
        (teacher_attention_in, teacher_attention_out, teacher_hidden_in, teacher_hidden_out, teacher_patch_weight, teacher_prototypes),
        me,
        n,
    )

    def table_of(rows):
        return jnp.concatenate([rows[1:SEQ], rows[0:1], jnp.zeros((ROWS - SEQ, D), f32)], 0)

    def gains_of(rows):
        zeros = jnp.zeros((5, D), f32)
        first = jnp.concatenate([rows[SEQ : SEQ + 2], jnp.zeros((6, D), f32)], 0)
        second = jnp.concatenate([rows[SEQ + 2 : SEQ + 5], zeros], 0)
        return first, second

    keep = patch_keep.reshape(count, PATCHES)
    bias = jnp.where(keep == 1, 0.0, -1000000000.0).astype(f32)
    ends = jnp.where(jnp.arange(ROWS - PATCHES) == 0, 0.0, -1000000000.0).astype(f32)
    ends = jnp.broadcast_to(ends, (count, ROWS - PATCHES))
    bias = jnp.concatenate([bias, ends], 1)[:, None]
    plain = jnp.concatenate([jnp.zeros((count, PATCHES), f32), ends], 1)[:, None]
    gains0, gains1 = gains_of(vector_rows)
    teacher_rows = teacher_vector_rows.astype(f32)
    teacher_gains0, teacher_gains1 = gains_of(teacher_rows)
    counter = step_count.astype(f32)
    fixes = jnp.stack([1.0 - beta_one**counter, 1.0 - beta_two**counter])

    (targets,) = forward(target_patches, table_of(teacher_rows), plain, teacher, teacher_gains0, teacher_gains1, False, n)
    if student["fast"]:
        targets, bias = lax.optimization_barrier((targets, bias))
    state1, state0, mix, share, att, mid, act, dgelu, logs, sums, kv, queries, shares, att_c, mid_c, expanded, last, cls, *natural = forward(
        anchor_patches, table_of(vector_rows), bias, student, gains0, gains1, True, n)
    student["natural"] = natural
    mean_sum = lax.all_to_all(sums, "dp", 0, 0, tiled=True)
    delta, gain_one, report, *one = layer_one_back(
        (logs, targets, mean_sum, state1, kv, queries, shares, att_c, mid_c, expanded, last, cls), student, gains1, inverse_count, me)
    d_mid, gain_two, *mlp = layer_zero_mlp_back(delta, act, dgelu, mid, student, gains0, GROUP, me)
    rest = layer_zero_attention_back(d_mid, state0, mix, share, att, anchor_patches, student, gains0, gain_two, gain_one, GROUP, me)
    if student["fast"]:
        slopes, line = collect(*scatter_gradients([one, mlp, rest], me), report, n, attention_in.shape[0])
        update = update_rows
    else:
        slopes, line = collect_plain(one, mlp, rest, report, n)
        update = update_plain
    arrived = lax.all_to_all(line, "dp", 0, 0, tiled=True)
    *states, loss, norm = update(slopes, arrived, report, masters, firsts, seconds, fixes)
    return (loss[0, 0], norm[0, 0], *states)


GROUP = 3


def solution(mesh):
    rows, same, images = P("dp", None), P(), P(None, "dp", None, None)
    weights = (rows,) * 5 + (same, rows)
    return jax.shard_map(
        local,
        mesh=mesh,
        in_specs=weights * 4 + (images, images, P(None, "dp", None), same),
        out_specs=(same, same) + weights * 3,
        check_vma=False,
    )
```

profile of v0, /device:TPU:0, one launch (start us, length us, event | category | flops | bytes accessed | tf_op | source)
XLA Modules:
  0.0 270.2 jit_solution(1205518432157913591)
XLA Ops:
  7.2 2.0 pack_weights.1
  9.3 4.1 %collective-permute-start = (bf16[24,5504]{1,0:T(8,128)(2,1)}, bf16[24,5504]{1,0:T(8,128)(2,1)S(1)}, u32[]{:S(2)}, u32[]{:S(2)}) collective-permute-start(bf16[24,5504]{1,0:T(8,128)(2,1)} %get-tuple-element.95), channel_id=1, source_target_pairs={{0,16},{1,17},{2,18},{3,19},{4,20},{5,21},{6,22},{7,23},{8,24},{9,... | collective-permute-start | bytes 792584 | tf_op jit(solution)/shard_map/ppermute | solution.py:799
  14.3 1.6 constant_dynamic-update-slice_fusion.9
  17.8 7.8 %collective-permute-done = bf16[24,5504]{1,0:T(8,128)(2,1)S(1)} collective-permute-done((bf16[24,5504]{1,0:T(8,128)(2,1)}, bf16[24,5504]{1,0:T(8,128)(2,1)S(1)}, u32[]{:S(2)}, u32[]{:S(2)}) %collective-permute-start) | collective-permute-done | bytes 264224 | tf_op jit(solution)/shard_map/ppermute | solution.py:799
  25.7 1.6 collective-permute-start.4
  28.9 2.8 %collective-permute-start.7 = (bf16[2,24,1920]{2,1,0:T(8,128)(2,1)S(1)}, bf16[2,24,1920]{2,1,0:T(8,128)(2,1)S(1)}, u32[]{:S(2)}, u32[]{:S(2)}) collective-permute-start(bf16[2,24,1920]{2,1,0:T(8,128)(2,1)S(1)} %pad_maximum_fusion.9), channel_id=1, source_target_pairs={{0,8},{1,9},{2,10},{3,11},{4,12},{5,13},{6,14},{7,15},{8,0},{9,1},... | collective-permute-start | bytes 552968 | tf_op jit(solution)/shard_map/ppermute | solution.py:799
  32.5 2.4 collective-permute-start.5
  39.9 9.9 %collective-permute-done.5 = bf16[4,24,1792]{2,1,0:T(8,128)(2,1)S(1)} collective-permute-done((bf16[4,24,1792]{2,1,0:T(8,128)(2,1)S(1)}, bf16[4,24,1792]{2,1,0:T(8,128)(2,1)S(1)}, u32[]{:S(2)}, u32[]{:S(2)}) %collective-permute-start.5) | collective-permute-done | bytes 344096 | tf_op jit(solution)/shard_map/ppermute | solution.py:799
  50.8 5.6 %collective-permute-done.8 = bf16[4,24,1920]{2,1,0:T(8,128)(2,1)S(1)} collective-permute-done((bf16[4,24,1920]{2,1,0:T(8,128)(2,1)S(1)}, bf16[4,24,1920]{2,1,0:T(8,128)(2,1)S(1)}, u32[]{:S(2)}, u32[]{:S(2)}) %collective-permute-start.8) | collective-permute-done | bytes 368672 | tf_op jit(solution)/shard_map/ppermute | solution.py:799
  58.8 12.0 %collective-permute-done.6 = bf16[8,24,1792]{2,1,0:T(8,128)(2,1)S(1)} collective-permute-done((bf16[8,24,1792]{2,1,0:T(8,128)(2,1)S(1)}, bf16[8,24,1792]{2,1,0:T(8,128)(2,1)S(1)}, u32[]{:S(2)}, u32[]{:S(2)}) %collective-permute-start.6) | collective-permute-done | bytes 688160 | tf_op jit(solution)/shard_map/ppermute | solution.py:799
  75.1 1.9 copy.60.refs_0_
  78.9 2.2 collective-permute-done.10.refs_3_.refs_9_.refs_15_.refs_21_
  81.2 5.3 %unpack_weights.1 = (bf16[768,1152]{1,0:T(8,128)(2,1)S(1)}, bf16[768,384]{1,0:T(8,128)(2,1)S(1)}, bf16[768,1536]{1,0:T(8,128)(2,1)S(1)}, bf16[3072,384]{1,0:T(8,...) custom-call(s32[1]{0:T(128)} %bitcast.3.me.refs_12_.refs_7_.refs_10_, ...), custom_call_target="tpu_custom_call" | custom-call | flops 8999999488 | bytes 27000000 | tf_op jit(solution)/shard_map/unpack_weights/pallas_call | solution.py:743
  86.7 19.6 %teacher_forward.1.refs_1_ = f32[16,1024]{1,0:T(8,128)S(1)} custom-call(bf16[2,3,196,768]{3,2,1,0:T(8,128)(2,1)S(1)} %copy.60.refs_0_, f32[208,384]{1,0:T(8,128)S(1)} %get-tuple-element.195.refs_1_, f32[6,1,208]{2,1,0:T(1,128)S(1)} %copy.61.refs_2_, bf16[6,208,128]{2,1,0:T(8,128)(2,1)S(1)} %broadcast_in_dim.45.refs_3_, f32[8,384]{1,0:T(8,128)S(1)} %concatenate.91.refs_4_, ...), custom_call_target="tpu_custom_call" | custom-call | flops 30000001024 | bytes 90000000 | tf_op jit(solution)/shard_map/teacher_forward/pallas_call | solution.py:316
  106.6 3.4 %copy-done.5 = bf16[768,5504]{1,0:T(8,128)(2,1)S(1)} copy-done((bf16[768,5504]{1,0:T(8,128)(2,1)S(1)}, bf16[768,5504]{1,0:T(8,128)(2,1)}, u32[]{:S(2)}) %copy-start.5) | copy-done | bytes 8454168
  110.0 22.2 %student_forward.1 = (f32[1248,384]{1,0:T(8,128)S(1)}, f32[1248,384]{1,0:T(8,128)S(1)}, bf16[1248,1152]{1,0:T(8,128)(2,1)S(1)}, bf16[6,6,208,208]{3,2,1,0:T(8,12...) custom-call(bf16[2,3,196,768]{3,2,1,0:T(8,128)(2,1)S(1)} %copy-done,, ...), custom_call_target="tpu_custom_call" | custom-call | flops 30000001024 | bytes 90000000 | tf_op jit(solution)/shard_map/student_forward/pallas_call | solution.py:316
  133.4 1.6 copy-done.29
  136.3 12.1 %all_to_all.10.refs_2_ = bf16[32,16,128]{2,1,0:T(8,128)(2,1)S(1)} all-to-all(bf16[32,16,128]{2,1,0:T(8,128)(2,1)S(1)} %get-tuple-element.106), channel_id=1, replica_groups=mesh['dp'=32] {'dp'}, dimensions={0} | all-to-all | bytes 262144 | tf_op jit(solution)/shard_map/all_to_all | solution.py:1028
  148.4 9.7 %layer_one_back.1 = (f32[1248,384]{1,0:T(8,128)S(1)}, f32[8,384]{1,0:T(8,128)S(1)}, f32[8,128]{1,0:T(8,128)S(1)}, bf16[3,8,352,128]{3,2,1,0:T(8,128)(2,1)S(1)}, bf16[3,8,352,128]{3,2,1,0:T(8,128)(2,1)}) custom-call(f32[16,1024]{1,0:T(8,128)S(1)} %get-tuple-element.104.refs_0_, f32[16,1024]{1,0:T(8,128)S(1)} %teacher_forward.1.refs_1_, ...), custom_call_target="tpu_custom_call" | custom-call | flops 12999999488 | bytes 39000000 | tf_op jit(solution)/shard_map/layer_one_back/pallas_call | solution.py:492
  158.4 12.9 %layer_zero_mlp_back.1 = (f32[1248,384]{1,0:T(8,128)S(1)}, f32[8,384]{1,0:T(8,128)S(1)}, bf16[3,8,192,128]{3,2,1,0:T(8,128)(2,1)S(1)}, bf16[3,8,192,128]{3,2,1,0:T(8,128)(2,1)}) custom-call(f32[1248,384]{1,0:T(8,128)S(1)} %get-tuple-element.121.refs_0_, bf16[1248,1536]{1,0:T(8,128)(2,1)S(1)} %get-tuple-element.122.refs_1_, ...), custom_call_target="tpu_custom_call" | custom-call | flops 16999999488 | bytes 51000000 | tf_op jit(solution)/shard_map/layer_zero_mlp_back/pallas_call | solution.py:556
  171.2 15.5 %layer_zero_attention_back.1 = (bf16[3,8,160,128]{3,2,1,0:T(8,128)(2,1)S(1)}, bf16[3,8,160,128]{3,2,1,0:T(8,128)(2,1)}) custom-call(f32[1248,384]{1,0:T(8,128)S(1)} %get-tuple-element.126.refs_0_, f32[1248,384]{1,0:T(8,128)S(1)} %copy-done.32, bf16[1248,1152]{1,0:T(8,128)(2,1)S(1)} %copy-done.30, bf16[1248,384]{1,0:T(8,128)(2,1)S(1)} %get-tuple-element.129.refs_3_, ...), custom_call_target="tpu_custom_call" | custom-call | flops 20999999488 | bytes 63000000 | tf_op jit(solution)/shard_map/layer_zero_attention_back/pallas_call | solution.py:649
  188.2 2.4 collective-permute-done.14
  190.6 1.8 add_convert_fusion.2
  192.5 1.6 add_convert_fusion.1
  194.1 2.2 add_convert_fusion
  199.5 15.9 %collective-permute-done.16 = bf16[4,704,128]{2,1,0:T(8,128)(2,1)S(1)} collective-permute-done((bf16[4,704,128]{2,1,0:T(8,128)(2,1)S(1)}, bf16[4,704,128]{2,1,0:T(8,128)(2,1)S(1)}, u32[]{:S(2)}, u32[]{:S(2)}) %collective-permute-start.16) | collective-permute-done | bytes 720928 | tf_op jit(solution)/shard_map/ppermute | solution.py:799
  218.6 6.9 %collective-permute-done.17 = bf16[2,704,128]{2,1,0:T(8,128)(2,1)S(1)} collective-permute-done((bf16[2,704,128]{2,1,0:T(8,128)(2,1)S(1)}, bf16[2,704,128]{2,1,0:T(8,128)(2,1)S(1)}, u32[]{:S(2)}, u32[]{:S(2)}) %collective-permute-start.17) | collective-permute-done | bytes 360480 | tf_op jit(solution)/shard_map/ppermute | solution.py:799
  228.5 2.7 %collective-permute-done.18 = bf16[1,704,128]{2,1,0:T(8,128)(2,1)S(1)} collective-permute-done((bf16[1,704,128]{2,1,0:T(8,128)(2,1)S(1)}, bf16[1,704,128]{2,1,0:T(8,128)(2,1)S(1)}, u32[]{:S(2)}, u32[]{:S(2)}) %collective-permute-start.18) | collective-permute-done | bytes 180256 | tf_op jit(solution)/shard_map/ppermute | solution.py:799
  234.3 11.1 %collective-permute-done.25.refs_1_ = bf16[3,352,128]{2,1,0:T(8,128)(2,1)S(1)} collective-permute-done((bf16[3,352,128]{2,1,0:T(8,128)(2,1)S(1)}, bf16[3,352,128]{2,1,0:T(8,128)(2,1)S(1)}, u32[]{:S(2)}, u32[]{:S(2)}) %collective-permute-start.25) | collective-permute-done | bytes 270368 | tf_op jit(solution)/shard_map/ppermute | solution.py:799
  246.6 3.2 %all-to-all-start.1 = ((bf16[32,8,512]{2,1,0:T(8,128)(2,1)}), bf16[32,8,512]{2,1,0:T(8,128)(2,1)S(1)}, u32[]{:S(2)}, u32[]{:S(2)}) async-start(bf16[32,8,512]{2,1,0:T(8,128)(2,1)} %get-tuple-element.137), calls=%async_computation.1 | async-start | bytes 524288 | tf_op jit(solution)/shard_map/all_to_all | solution.py:1039
  250.6 9.8 %all-to-all-done.1.refs_2_ = bf16[32,8,512]{2,1,0:T(8,128)(2,1)S(1)} async-done(((bf16[32,8,512]{2,1,0:T(8,128)(2,1)}), bf16[32,8,512]{2,1,0:T(8,128)(2,1)S(1)}, u32[]{:S(2)}, u32[]{:S(2)}) %all-to-all-start.1) | async-done | bytes 262176 | tf_op jit(solution)/shard_map/all_to_all | solution.py:1039
  260.6 2.6 update_rows.1
  (230 shorter events, 37.7 us)
Async XLA Ops:
  7.2 99.1 %all-gather.2.cloned.1.call-start = ((), (), s32[]{:S(2)}) async-start(), calls=%async_computation.2 | async-start | bytes 8718336 | tf_op jit(solution)/shard_map/all_gather | solution.py:776
  9.3 16.3 %collective-permute-start = (bf16[24,5504]{1,0:T(8,128)(2,1)}, bf16[24,5504]{1,0:T(8,128)(2,1)S(1)}, u32[]{:S(2)}, u32[]{:S(2)}) collective-permute-start(bf16[24,5504]{1,0:T(8,128)(2,1)} %get-tuple-element.95), channel_id=1, source_target_pairs={{0,16},{1,17},{2,18},{3,19},{4,20},{5,21},{6,22},{7,23},{8,24},{9,... | collective-permute-start | bytes 792584 | tf_op jit(solution)/shard_map/ppermute | solution.py:799
  25.7 6.8 %collective-permute-start.4 = (bf16[2,24,1792]{2,1,0:T(8,128)(2,1)S(1)}, bf16[2,24,1792]{2,1,0:T(8,128)(2,1)S(1)}, u32[]{:S(2)}, u32[]{:S(2)}) collective-permute-start(bf16[2,24,1792]{2,1,0:T(8,128)(2,1)S(1)} %pad_maximum_fusion.11), channel_id=1, source_target_pairs={{0,4},{1,5},{2,6},{3,7},{4,0},{5,1},{6,2},{7,3},{8,12},{9,13},{10,... | collective-permute-start | bytes 516104 | tf_op jit(solution)/shard_map/ppermute | solution.py:799
  27.3 7.5 %collective-permute-start.1 = (bf16[2,24,1792]{2,1,0:T(8,128)(2,1)S(1)}, bf16[2,24,1792]{2,1,0:T(8,128)(2,1)S(1)}, u32[]{:S(2)}, u32[]{:S(2)}) collective-permute-start(bf16[2,24,1792]{2,1,0:T(8,128)(2,1)S(1)} %pad_maximum_fusion.10), channel_id=1, source_target_pairs={{0,2},{1,3},{2,0},{3,1},{4,6},{5,7},{6,4},{7,5},{8,10},{9,11},{10,... | collective-permute-start | bytes 516104 | tf_op jit(solution)/shard_map/ppermute | solution.py:799
  28.9 9.8 %collective-permute-start.7 = (bf16[2,24,1920]{2,1,0:T(8,128)(2,1)S(1)}, bf16[2,24,1920]{2,1,0:T(8,128)(2,1)S(1)}, u32[]{:S(2)}, u32[]{:S(2)}) collective-permute-start(bf16[2,24,1920]{2,1,0:T(8,128)(2,1)S(1)} %pad_maximum_fusion.9), channel_id=1, source_target_pairs={{0,8},{1,9},{2,10},{3,11},{4,12},{5,13},{6,14},{7,15},{8,0},{9,1},... | collective-permute-start | bytes 552968 | tf_op jit(solution)/shard_map/ppermute | solution.py:799
  32.5 17.3 %collective-permute-start.5 = (bf16[4,24,1792]{2,1,0:T(8,128)(2,1)S(1)}, bf16[4,24,1792]{2,1,0:T(8,128)(2,1)S(1)}, u32[]{:S(2)}, u32[]{:S(2)}) collective-permute-start(bf16[4,24,1792]{2,1,0:T(8,128)(2,1)S(1)} %pad_maximum_fusion.7), channel_id=1, source_target_pairs={{0,8},{1,9},{2,10},{3,11},{4,12},{5,13},{6,14},{7,15},{8,0},{9,1},... | collective-permute-start | bytes 1032200 | tf_op jit(solution)/shard_map/ppermute | solution.py:799
  34.9 15.7 %collective-permute-start.2 = (bf16[4,24,1792]{2,1,0:T(8,128)(2,1)S(1)}, bf16[4,24,1792]{2,1,0:T(8,128)(2,1)S(1)}, u32[]{:S(2)}, u32[]{:S(2)}) collective-permute-start(bf16[4,24,1792]{2,1,0:T(8,128)(2,1)S(1)} %pad_maximum_fusion.6), channel_id=1, source_target_pairs={{0,4},{1,5},{2,6},{3,7},{4,0},{5,1},{6,2},{7,3},{8,12},{9,13},{10,... | collective-permute-start | bytes 1032200 | tf_op jit(solution)/shard_map/ppermute | solution.py:799
  38.8 17.6 %collective-permute-start.8 = (bf16[4,24,1920]{2,1,0:T(8,128)(2,1)S(1)}, bf16[4,24,1920]{2,1,0:T(8,128)(2,1)S(1)}, u32[]{:S(2)}, u32[]{:S(2)}) collective-permute-start(bf16[4,24,1920]{2,1,0:T(8,128)(2,1)S(1)} %pad_maximum_fusion.5), channel_id=1, source_target_pairs={{0,2},{1,3},{2,0},{3,1},{4,6},{5,7},{6,4},{7,5},{8,10},{9,11},{10,... | collective-permute-start | bytes 1105928 | tf_op jit(solution)/shard_map/ppermute | solution.py:799
  49.9 20.8 %collective-permute-start.6 = (bf16[8,24,1792]{2,1,0:T(8,128)(2,1)S(1)}, bf16[8,24,1792]{2,1,0:T(8,128)(2,1)S(1)}, u32[]{:S(2)}, u32[]{:S(2)}) collective-permute-start(bf16[8,24,1792]{2,1,0:T(8,128)(2,1)S(1)} %pad_maximum_fusion.3), channel_id=1, source_target_pairs={{0,2},{1,3},{2,0},{3,1},{4,6},{5,7},{6,4},{7,5},{8,10},{9,11},{10,... | collective-permute-start | bytes 2064392 | tf_op jit(solution)/shard_map/ppermute | solution.py:799
  50.7 21.8 %collective-permute-start.3 = (bf16[8,24,1792]{2,1,0:T(8,128)(2,1)S(1)}, bf16[8,24,1792]{2,1,0:T(8,128)(2,1)S(1)}, u32[]{:S(2)}, u32[]{:S(2)}) collective-permute-start(bf16[8,24,1792]{2,1,0:T(8,128)(2,1)S(1)} %pad_maximum_fusion.2), channel_id=1, source_target_pairs={{0,8},{1,9},{2,10},{3,11},{4,12},{5,13},{6,14},{7,15},{8,0},{9,1},... | collective-permute-start | bytes 2064392 | tf_op jit(solution)/shard_map/ppermute | solution.py:799
  56.5 15.2 %collective-permute-start.9 = (bf16[8,24,1920]{2,1,0:T(8,128)(2,1)S(1)}, bf16[8,24,1920]{2,1,0:T(8,128)(2,1)S(1)}, u32[]{:S(2)}, u32[]{:S(2)}) collective-permute-start(bf16[8,24,1920]{2,1,0:T(8,128)(2,1)S(1)} %pad_maximum_fusion.1), channel_id=1, source_target_pairs={{0,4},{1,5},{2,6},{3,7},{4,0},{5,1},{6,2},{7,3},{8,12},{9,13},{10,... | collective-permute-start | bytes 2211848 | tf_op jit(solution)/shard_map/ppermute | solution.py:799
  71.6 7.3 %collective-permute-start.11 = (bf16[16,24,1792]{2,1,0:T(8,128)(2,1)}, bf16[16,24,1792]{2,1,0:T(8,128)(2,1)}, u32[]{:S(2)}, u32[]{:S(2)}) collective-permute-start(bf16[16,24,1792]{2,1,0:T(8,128)(2,1)} %constant_dynamic-update-slice_fusion.5.refs_1_.refs_7_.refs_13_.refs_19_), channel_id=1, source_target_pairs={{0,1},{1,0},{2,3},{3,2},{4,5},{5,4},{6,7},{7,6},{8,9},{9,8},{10,11... | collective-permute-start | bytes 4128776 | tf_op jit(solution)/shard_map/ppermute | solution.py:799
  71.8 9.4 %collective-permute-start.12 = (bf16[16,24,1920]{2,1,0:T(8,128)(2,1)S(1)}, bf16[16,24,1920]{2,1,0:T(8,128)(2,1)S(1)}, u32[]{:S(2)}, u32[]{:S(2)}) collective-permute-start(bf16[16,24,1920]{2,1,0:T(8,128)(2,1)S(1)} %constant_dynamic-update-slice_fusion.10.refs_2_.refs_8_.refs_14_.refs_20_), channel_id=1, source_target_pairs={{0,1},{1,0},{2,3},{3,2},{4,5},{5,4},{6,7},{7,6},{8,9},{9,8},{10,11... | collective-permute-start | bytes 4423688 | tf_op jit(solution)/shard_map/ppermute | solution.py:799
  73.4 7.8 %collective-permute-start.10 = (bf16[16,24,1792]{2,1,0:T(8,128)(2,1)}, bf16[16,24,1792]{2,1,0:T(8,128)(2,1)}, u32[]{:S(2)}, u32[]{:S(2)}) collective-permute-start(bf16[16,24,1792]{2,1,0:T(8,128)(2,1)} %constant_dynamic-update-slice_fusion.refs_0_.refs_6_.refs_12_.refs_18_), channel_id=1, source_target_pairs={{0,1},{1,0},{2,3},{3,2},{4,5},{5,4},{6,7},{7,6},{8,9},{9,8},{10,11... | collective-permute-start | bytes 4128776 | tf_op jit(solution)/shard_map/ppermute | solution.py:799
  86.7 19.9 %copy-start = (bf16[2,3,196,768]{3,2,1,0:T(8,128)(2,1)S(1)}, bf16[2,3,196,768]{3,2,1,0:T(8,128)(2,1)}, u32[]{:S(2)}) copy-start(bf16[2,3,196,768]{3,2,1,0:T(8,128)(2,1)} %copy.63.refs_0_.refs_5_) | copy-start | bytes 5419012
  110.0 38.4 %copy-start.6 = (bf16[768,5504]{1,0:T(8,128)(2,1)S(1)}, bf16[768,5504]{1,0:T(8,128)(2,1)}, u32[]{:S(2)}) copy-start(bf16[768,5504]{1,0:T(8,128)(2,1)} %all-gather.2.cloned.1.call-done.refs_6_.refs_14_.refs_5_) | copy-start | bytes 25362436
  158.1 36.0 %collective-permute-start.13 = (bf16[3,8,352,128]{3,2,1,0:T(8,128)(2,1)}, bf16[3,8,352,128]{3,2,1,0:T(8,128)(2,1)}, u32[]{:S(2)}, u32[]{:S(2)}) collective-permute-start(bf16[3,8,352,128]{3,2,1,0:T(8,128)(2,1)} %get-tuple-element.120), channel_id=1, source_target_pairs={{0,1},{1,0},{2,3},{3,2},{4,5},{5,4},{6,7},{7,6},{8,9},{9,8},{10,11... | collective-permute-start | bytes 6488072 | tf_op jit(solution)/shard_map/ppermute | solution.py:799
  187.7 2.9 %collective-permute-start.14 = (bf16[3,8,160,128]{3,2,1,0:T(8,128)(2,1)}, bf16[3,8,160,128]{3,2,1,0:T(8,128)(2,1)}, u32[]{:S(2)}, u32[]{:S(2)}) collective-permute-start(bf16[3,8,160,128]{3,2,1,0:T(8,128)(2,1)} %get-tuple-element.134), channel_id=1, source_target_pairs={{0,1},{1,0},{2,3},{3,2},{4,5},{5,4},{6,7},{7,6},{8,9},{9,8},{10,11... | collective-permute-start | bytes 2949128 | tf_op jit(solution)/shard_map/ppermute | solution.py:799
  188.0 4.5 %collective-permute-start.15 = (bf16[3,8,192,128]{3,2,1,0:T(8,128)(2,1)}, bf16[3,8,192,128]{3,2,1,0:T(8,128)(2,1)}, u32[]{:S(2)}, u32[]{:S(2)}) collective-permute-start(bf16[3,8,192,128]{3,2,1,0:T(8,128)(2,1)} %get-tuple-element.136), channel_id=1, source_target_pairs={{0,1},{1,0},{2,3},{3,2},{4,5},{5,4},{6,7},{7,6},{8,9},{9,8},{10,11... | collective-permute-start | bytes 3538952 | tf_op jit(solution)/shard_map/ppermute | solution.py:799
  197.0 18.4 %collective-permute-start.16 = (bf16[4,704,128]{2,1,0:T(8,128)(2,1)S(1)}, bf16[4,704,128]{2,1,0:T(8,128)(2,1)S(1)}, u32[]{:S(2)}, u32[]{:S(2)}) collective-permute-start(bf16[4,704,128]{2,1,0:T(8,128)(2,1)S(1)} %constant_dynamic-update-slice_fusion.20), channel_id=1, source_target_pairs={{0,2},{1,3},{2,0},{3,1},{4,6},{5,7},{6,4},{7,5},{8,10},{9,11},{10,... | collective-permute-start | bytes 2162696 | tf_op jit(solution)/shard_map/ppermute | solution.py:799
  197.6 18.8 %collective-permute-start.19 = (bf16[4,704,128]{2,1,0:T(8,128)(2,1)S(1)}, bf16[4,704,128]{2,1,0:T(8,128)(2,1)S(1)}, u32[]{:S(2)}, u32[]{:S(2)}) collective-permute-start(bf16[4,704,128]{2,1,0:T(8,128)(2,1)S(1)} %constant_dynamic-update-slice_fusion.30), channel_id=1, source_target_pairs={{0,4},{1,5},{2,6},{3,7},{4,0},{5,1},{6,2},{7,3},{8,12},{9,13},{10,... | collective-permute-start | bytes 2162696 | tf_op jit(solution)/shard_map/ppermute | solution.py:799
  198.7 18.6 %collective-permute-start.22 = (bf16[4,704,128]{2,1,0:T(8,128)(2,1)S(1)}, bf16[4,704,128]{2,1,0:T(8,128)(2,1)S(1)}, u32[]{:S(2)}, u32[]{:S(2)}) collective-permute-start(bf16[4,704,128]{2,1,0:T(8,128)(2,1)S(1)} %constant_dynamic-update-slice_fusion.40), channel_id=1, source_target_pairs={{0,8},{1,9},{2,10},{3,11},{4,12},{5,13},{6,14},{7,15},{8,0},{9,1},... | collective-permute-start | bytes 2162696 | tf_op jit(solution)/shard_map/ppermute | solution.py:799
  215.7 9.9 %collective-permute-start.17 = (bf16[2,704,128]{2,1,0:T(8,128)(2,1)S(1)}, bf16[2,704,128]{2,1,0:T(8,128)(2,1)S(1)}, u32[]{:S(2)}, u32[]{:S(2)}) collective-permute-start(bf16[2,704,128]{2,1,0:T(8,128)(2,1)S(1)} %slice.363), channel_id=1, source_target_pairs={{0,4},{1,5},{2,6},{3,7},{4,0},{5,1},{6,2},{7,3},{8,12},{9,13},{10,... | collective-permute-start | bytes 1081352 | tf_op jit(solution)/shard_map/ppermute | solution.py:799
  216.6 9.8 %collective-permute-start.20 = (bf16[2,704,128]{2,1,0:T(8,128)(2,1)S(1)}, bf16[2,704,128]{2,1,0:T(8,128)(2,1)S(1)}, u32[]{:S(2)}, u32[]{:S(2)}) collective-permute-start(bf16[2,704,128]{2,1,0:T(8,128)(2,1)S(1)} %slice.385), channel_id=1, source_target_pairs={{0,8},{1,9},{2,10},{3,11},{4,12},{5,13},{6,14},{7,15},{8,0},{9,1},... | collective-permute-start | bytes 1081352 | tf_op jit(solution)/shard_map/ppermute | solution.py:799
  217.6 9.7 %collective-permute-start.23 = (bf16[2,704,128]{2,1,0:T(8,128)(2,1)S(1)}, bf16[2,704,128]{2,1,0:T(8,128)(2,1)S(1)}, u32[]{:S(2)}, u32[]{:S(2)}) collective-permute-start(bf16[2,704,128]{2,1,0:T(8,128)(2,1)S(1)} %slice.407), channel_id=1, source_target_pairs={{0,2},{1,3},{2,0},{3,1},{4,6},{5,7},{6,4},{7,5},{8,10},{9,11},{10,... | collective-permute-start | bytes 1081352 | tf_op jit(solution)/shard_map/ppermute | solution.py:799
  225.6 5.6 %collective-permute-start.18 = (bf16[1,704,128]{2,1,0:T(8,128)(2,1)S(1)}, bf16[1,704,128]{2,1,0:T(8,128)(2,1)S(1)}, u32[]{:S(2)}, u32[]{:S(2)}) collective-permute-start(bf16[1,704,128]{2,1,0:T(8,128)(2,1)S(1)} %slice.365), channel_id=1, source_target_pairs={{0,8},{1,9},{2,10},{3,11},{4,12},{5,13},{6,14},{7,15},{8,0},{9,1},... | collective-permute-start | bytes 540680 | tf_op jit(solution)/shard_map/ppermute | solution.py:799
  226.6 5.6 %collective-permute-start.21 = (bf16[1,704,128]{2,1,0:T(8,128)(2,1)S(1)}, bf16[1,704,128]{2,1,0:T(8,128)(2,1)S(1)}, u32[]{:S(2)}, u32[]{:S(2)}) collective-permute-start(bf16[1,704,128]{2,1,0:T(8,128)(2,1)S(1)} %slice.387), channel_id=1, source_target_pairs={{0,2},{1,3},{2,0},{3,1},{4,6},{5,7},{6,4},{7,5},{8,10},{9,11},{10,... | collective-permute-start | bytes 540680 | tf_op jit(solution)/shard_map/ppermute | solution.py:799
  227.4 5.6 %collective-permute-start.24 = (bf16[1,704,128]{2,1,0:T(8,128)(2,1)S(1)}, bf16[1,704,128]{2,1,0:T(8,128)(2,1)S(1)}, u32[]{:S(2)}, u32[]{:S(2)}) collective-permute-start(bf16[1,704,128]{2,1,0:T(8,128)(2,1)S(1)} %slice.409), channel_id=1, source_target_pairs={{0,4},{1,5},{2,6},{3,7},{4,0},{5,1},{6,2},{7,3},{8,12},{9,13},{10,... | collective-permute-start | bytes 540680 | tf_op jit(solution)/shard_map/ppermute | solution.py:799
  233.2 12.2 %collective-permute-start.25 = (bf16[3,352,128]{2,1,0:T(8,128)(2,1)S(1)}, bf16[3,352,128]{2,1,0:T(8,128)(2,1)S(1)}, u32[]{:S(2)}, u32[]{:S(2)}) collective-permute-start(bf16[3,352,128]{2,1,0:T(8,128)(2,1)S(1)} %pad_maximum_fusion.8), channel_id=1, source_target_pairs={{0,16},{1,17},{2,18},{3,19},{4,20},{5,21},{6,22},{7,23},{8,24},{9,... | collective-permute-start | bytes 811016 | tf_op jit(solution)/shard_map/ppermute | solution.py:799
  245.5 15.0 %copy-start.10 = (f32[96,384]{1,0:T(8,128)S(1)}, f32[96,384]{1,0:T(8,128)}, u32[]{:S(2)}) copy-start(f32[96,384]{1,0:T(8,128)} %refs_12_.1) | copy-start | bytes 442372
  245.5 15.0 %copy-start.11 = (f32[24,1536]{1,0:T(8,128)S(1)}, f32[24,1536]{1,0:T(8,128)}, u32[]{:S(2)}) copy-start(f32[24,1536]{1,0:T(8,128)} %refs_18_.1) | copy-start | bytes 442372
  246.6 13.8 %all-to-all-start.1 = ((bf16[32,8,512]{2,1,0:T(8,128)(2,1)}), bf16[32,8,512]{2,1,0:T(8,128)(2,1)S(1)}, u32[]{:S(2)}, u32[]{:S(2)}) async-start(bf16[32,8,512]{2,1,0:T(8,128)(2,1)} %get-tuple-element.137), calls=%async_computation.1 | async-start | bytes 524288 | tf_op jit(solution)/shard_map/all_to_all | solution.py:1039
  (35 other events, 355.4 us)
Sparse Core Ops, SparseCore 0:
  11.5 92.0 all-gather.1
where the time goes:
time: 274 us; the launch traced here: 270 us
  Pallas kernels  90.6 us (33%)
  waiting for transfers between devices  89.4 us (33%)
  starting transfers between devices  29.5 us (11%)
  local copies, waits for them, and re-layouts  25.2 us (9%)
  between operations  16 us (6%)
  blocking collectives  12.1 us (4%)
  other arithmetic  7.46 us (3%)
    ppermute x26, waiting for transfers between devices, swap(): return lax.ppermute(value, 'dp', [(i, i ^ 1 << bit) for i in range(size)])  79.5 us
    pallas_call x2, Pallas kernels, forward(): pl.pallas_call(lambda *refs: forward_kernel(save, packed, count, *refs),...  41.8 us
    ppermute x26, starting transfers between devices, swap(): return lax.ppermute(value, 'dp', [(i, i ^ 1 << bit) for i in range(size)])  26.2 us
    unnamed x117, local copies, waits for them, and re-layouts  18.8 us
    pallas_call x1, Pallas kernels, layer_zero_attention_back(): pl.pallas_call(lambda *refs: attention_back_kernel(packed, group, *refs),...  15.5 us
    pallas_call x1, Pallas kernels, layer_zero_mlp_back(): pl.pallas_call(lambda *refs: mlp_back_kernel(packed, group, *refs), grid=...  12.9 us
    all_to_all x1, blocking collectives, local(): mean_sum = lax.all_to_all(sums, 'dp', 0, 0, tiled=True)  12.1 us
    all_to_all x1, waiting for transfers between devices, local(): arrived = lax.all_to_all(line, 'dp', 0, 0, tiled=True)  9.79 us
  transfers between devices with their start and end apart: 28, of which 15 were waited for; matrix products, arithmetic and copies ran while one was open for 8% of the time, Pallas kernels for 20%

commit v1 on v0

--- a/solution.py
+++ b/solution.py
@@ -16,6 +16,7 @@
 VROWS = 202
 ROWS = 208
 CLS = 196
+WIDE = 512
 CR = 16
 SCALE = HEAD_DIM ** (-0.5)
 
@@ -109,10 +110,6 @@
         natural[pl.ds(64 * pair, 64), :] = jnp.concatenate(pieces, 0).astype(bf16)
 
 
-def step_rows(ref, height):
-    return ref.at[pl.ds(pl.multiple_of(pl.program_id(0) * height, 16), height)]
-
-
 def layer_views(weights, packed, layer):
     if packed:
         (full,) = weights
@@ -126,33 +123,25 @@
 def forward_kernel(save, packed, count, *refs):
     (pats, tab, bias_all, key_bias_all, gains, gains_one), refs = refs[:6], refs[6:]
     weights, refs = refs[: 1 if packed else 6], refs[1 if packed else 6 :]
-    step = pl.program_id(0)
-    group = pats.shape[1]
-    height = group * ROWS
-    pat = pats.at[pl.ds(step, 1)]
+    group = count
+    per = pats.shape[1]
     if save:
-        states, class_refs, naturals = refs[0], refs[8:18], refs[18:]
-        out, first, mix, share, att, mid, act, dgelu = (step_rows(ref, height) if i != 3 else ref.at[pl.ds(step * group, group)] for i, ref in enumerate(refs[:8]))
+        out, first, mix, share, att, mid = refs[:6]
+        class_refs, naturals = refs[6:16], refs[16:]
     else:
-        share = mid = act = dgelu = None
-        (target, first, mix, att, kv, att_c, cls, states) = refs[:8]
+        share = mid = None
+        (target, first, mix, att, kv, att_c, cls, out) = refs[:8]
         class_refs = (target, kv, att_c, cls)
-        out = step_rows(states, height)
     win, wo, w1, w2 = layer_views(weights, packed, 0)
     if packed:
         down, down_one, protos = naturals
         wp = weights[0].at[:, pl.ds(PLACE["patch"], D)]
-
-        @pl.when(step == 0)
-        def _():
-            natural_down(w2, down)
-
+        natural_down(w2, down)
     else:
         wp, down = weights[4], w2
-    group = pat.shape[1]
     table = tab[...]
     for g in range(group):
-        embedded = dot(pat[0, g], wp[...])
+        embedded = dot(pats[g // per, g % per], wp[...])
         first[pl.ds(g * ROWS, PATCHES), :] = embedded + table[:PATCHES]
         first[pl.ds(g * ROWS + PATCHES, ROWS - PATCHES), :] = table[PATCHES:]
     state = first[...]
@@ -163,7 +152,7 @@
 
     for g in range(group):
         rows = pl.ds(g * ROWS, ROWS)
-        key_bias = key_bias_all[step * group + g]
+        key_bias = key_bias_all[g]
         for pair in range(HEADS // 2):
             query = mix[rows, pl.ds(128 * pair, 128)] * jnp.asarray(SCALE, bf16)
             keys = mix[rows, pl.ds(D + 128 * pair, 128)]
@@ -184,26 +173,19 @@
     hat, _ = normalize(middle)
     normed = (hat * gains[1:2, :]).astype(bf16)
     result = middle
-    for j in range(FF // D):
-        cols = pl.ds(D * j, D)
-        a, slope = gelu_parts(dot(normed, w1[:, cols]), save)
-        a = a.astype(bf16)
-        if save:
-            act[:, cols] = a
-            dgelu[:, cols] = slope.astype(bf16)
-        result = result + dot(a, down[cols, :])
+    for j in range(FF // WIDE):
+        cols = pl.ds(WIDE * j, WIDE)
+        a, _ = gelu_parts(dot(normed, w1[:, cols]), False)
+        result = result + dot(a.astype(bf16), down[cols, :])
     out[...] = result
-
-    @pl.when(step == pl.num_programs(0) - 1)
-    def _():
-        win, wo, w1, w2 = layer_views(weights, packed, 1)
-        if packed:
-            natural_down(w2, down_one)
-            natural_protos(weights[0].at[:, pl.ds(PLACE["protos"], D)], weights[0].at[:, pl.ds(PLACE["rest"], 128)], protos)
-            late = (win, wo, w1, down_one, protos)
-        else:
-            late = (win, wo, w1, w2, weights[5])
-        class_forward(save, count, states, bias_all, late, gains_one, class_refs)
+    win, wo, w1, w2 = layer_views(weights, packed, 1)
+    if packed:
+        natural_down(w2, down_one)
+        natural_protos(weights[0].at[:, pl.ds(PLACE["protos"], D)], weights[0].at[:, pl.ds(PLACE["rest"], 128)], protos)
+        late = (win, wo, w1, down_one, protos)
+    else:
+        late = (win, wo, w1, w2, weights[5])
+    class_forward(save, count, out, bias_all, late, gains_one, class_refs)
 
 
 def class_forward(student, count, state, bias, weights, gains, refs):
@@ -274,7 +256,6 @@
     groups, group = patches.shape[:2]
     count = groups * group
     rows = count * ROWS
-    step = group * ROWS
     packed = net["packed"]
     if save:
         out_shape = [
@@ -284,8 +265,6 @@
             jax.ShapeDtypeStruct((count, HEADS, ROWS, ROWS), bf16),
             jax.ShapeDtypeStruct((rows, D), bf16),
             jax.ShapeDtypeStruct((rows, D), f32),
-            jax.ShapeDtypeStruct((rows, FF), bf16),
-            jax.ShapeDtypeStruct((rows, FF), bf16),
             jax.ShapeDtypeStruct((CR, PROTOS), f32),
             jax.ShapeDtypeStruct((n, 16, 128), bf16),
             jax.ShapeDtypeStruct((rows, 2 * D), bf16),
@@ -301,9 +280,9 @@
     else:
         out_shape = [jax.ShapeDtypeStruct((CR, PROTOS), f32)]
         scratch = [
-            pltpu.VMEM((step, D), f32),
-            pltpu.VMEM((step, 3 * D), bf16),
-            pltpu.VMEM((step, D), bf16),
+            pltpu.VMEM((rows, D), f32),
+            pltpu.VMEM((rows, 3 * D), bf16),
+            pltpu.VMEM((rows, D), bf16),
             pltpu.VMEM((rows, 2 * D), bf16),
             pltpu.VMEM((CR, D), f32),
             pltpu.VMEM((CR, D), f32),
@@ -315,18 +294,17 @@
     operands = (patches, table, bias, key_bias, gains, gains_one, *net["arrays"])
     return pl.pallas_call(
         lambda *refs: forward_kernel(save, packed, count, *refs),
-        grid=(groups,),
         in_specs=[whole()] * len(operands),
         out_specs=[whole()] * len(out_shape),
         out_shape=out_shape,
         scratch_shapes=scratch,
-        compiler_params=pltpu.CompilerParams(dimension_semantics=("arbitrary",), vmem_limit_bytes=megabytes(LIMITS[0 if save else 1])),
+        compiler_params=pltpu.CompilerParams(vmem_limit_bytes=megabytes(LIMITS[0 if save else 1])),
         cost_estimate=cost(30),
         name="student_forward" if save else "teacher_forward",
     )(*operands)
 
 
-LIMITS = [12, 18, 20, 14, 14, 10]
+LIMITS = [18, 18, 18, 18, 18, 10, 18]
 
 
 def megabytes(count):
@@ -501,43 +479,33 @@
     )(*args, *([me] if packed else []), gains, *weights)
 
 
-def mlp_back_kernel(packed, group, *refs):
-    (delta, act, dgelu, mid), (gains, ups, downs), refs = (step_rows(ref, group * ROWS) for ref in refs[:4]), refs[4:7], refs[7:]
+def mlp_back_kernel(packed, *refs):
+    delta, mid, gains, ups, downs = refs[:5]
     w1 = layer_views((ups,), True, 0)[2] if packed else ups.at[pl.ds(0, D)]
     w2 = downs.at[pl.ds(0, FF)]
-    first = pl.program_id(0) == 0
-    if packed:
-        me, d_mid, s_gain, keep, send, s_up, s_down = refs
+    if packed:
+        me, d_mid, s_gain, keep, send, s_up, s_down = refs[5:]
     else:
-        d_mid, s_gain, s_up, s_down = refs
-    d_mid = step_rows(d_mid, group * ROWS)
-
-    @pl.when(first)
-    def _():
-        s_up[...] = jnp.zeros(s_up.shape, f32)
-        s_down[...] = jnp.zeros(s_down.shape, f32)
-        s_gain[...] = jnp.zeros(s_gain.shape, f32)
-
+        d_mid, s_gain, s_up, s_down = refs[5:]
     d = delta[...]
     d_low = d.astype(bf16)
     hat, inv = normalize(mid[...])
     normed = (hat * gains[1:2, :]).astype(bf16)
     d_normed = None
-    for j in range(FF // D):
-        cols = pl.ds(D * j, D)
-        s_down[cols, :] += dot_at(act[:, cols], d_low)
-        d_exp = (dot_bt(d_low, w2[cols, :]) * dgelu[:, cols].astype(f32)).astype(bf16)
-        s_up[:, cols] += dot_at(normed, d_exp)
+    for j in range(FF // WIDE):
+        cols = pl.ds(WIDE * j, WIDE)
+        act, slope = gelu_parts(dot(normed, w1[:, cols]), True)
+        s_down[cols, :] = dot_at(act.astype(bf16), d_low)
+        d_exp = (dot_bt(d_low, w2[cols, :]) * slope).astype(bf16)
+        s_up[:, cols] = dot_at(normed, d_exp)
         part = dot_bt(d_exp, w1[:, cols])
         d_normed = part if d_normed is None else d_normed + part
     back, gain = norm_back(hat, inv, gains[1:2, :], d_normed)
-    s_gain[0:1, :] += gain
+    s_gain[...] = jnp.zeros((8, D), f32)
+    s_gain[0:1, :] = gain
     d_mid[...] = d + back
     if packed:
-
-        @pl.when(pl.program_id(0) == pl.num_programs(0) - 1)
-        def _():
-            pack_blocks(me[0], keep, send, [(s_up, 24), (s_down, 96)], [])
+        pack_blocks(me[0], keep, send, [(s_up, 24), (s_down, 96)], [])
 
 
 def backward_shapes(packed, slopes, chunk):
@@ -546,54 +514,29 @@
     return [jax.ShapeDtypeStruct(shape, f32) for shape in slopes], []
 
 
-def layer_zero_mlp_back(delta, act, dgelu, mid, net, gains, group, me):
+def layer_zero_mlp_back(delta, mid, net, gains, me):
     packed = net["fast"]
     weights = (net["arrays"][0], net["natural"][0]) if packed else net["arrays"][2:4]
     slopes, scratch = backward_shapes(packed, [(D, FF), (FF, D)], 1)
     scalar = [pl.BlockSpec(memory_space=pltpu.SMEM)] if packed else []
-    rows = delta.shape[0]
-    step = group * ROWS
     return pl.pallas_call(
-        lambda *refs: mlp_back_kernel(packed, group, *refs),
-        grid=(rows // step,),
-        in_specs=[whole()] * 7 + scalar,
+        lambda *refs: mlp_back_kernel(packed, *refs),
+        in_specs=[whole()] * 5 + scalar,
         out_specs=[whole()] * (2 + len(slopes)),
-        out_shape=[jax.ShapeDtypeStruct((rows, D), f32), jax.ShapeDtypeStruct((8, D), f32)] + slopes,
+        out_shape=[jax.ShapeDtypeStruct(delta.shape, f32), jax.ShapeDtypeStruct((8, D), f32)] + slopes,
         scratch_shapes=scratch,
-        compiler_params=pltpu.CompilerParams(dimension_semantics=("arbitrary",), vmem_limit_bytes=megabytes(LIMITS[3])),
-        cost_estimate=cost(17),
+        compiler_params=pltpu.CompilerParams(vmem_limit_bytes=megabytes(LIMITS[3])),
+        cost_estimate=cost(12),
         name="layer_zero_mlp_back",
-    )(delta, act, dgelu, mid, gains, *weights, *([me] if packed else []))
-
-
-def attention_back_kernel(packed, group, *refs):
-    (d_mid, state, mix, att) = (step_rows(ref, group * ROWS) for ref in refs[:4])
-    if packed:
-        (shares, pats, mixes, gains, gain_two, gain_one), refs = refs[4:10], refs[10:]
-    else:
-        (shares, pats, mixes, outs, gains, gain_two, gain_one), refs = refs[4:11], refs[11:]
-    base = pl.program_id(0) * group
-    share = shares.at[pl.ds(base, group)]
-    win, wo = layer_views((mixes,), True, 0)[:2] if packed else (mixes.at[pl.ds(0, D)], outs.at[pl.ds(0, D)])
-    if packed:
-        me, keep, send, s_in, s_out, s_patch, s_vector, d_att, dmix = refs
-    else:
-        s_in, s_out, s_patch, s_vector, d_att, dmix = refs
-
-    @pl.when(pl.program_id(0) == 0)
-    def _():
-        s_in[...] = jnp.zeros(s_in.shape, f32)
-        s_out[...] = jnp.zeros(s_out.shape, f32)
-        s_patch[...] = jnp.zeros(s_patch.shape, f32)
-        s_vector[...] = jnp.zeros(s_vector.shape, f32)
-        s_vector[ROWS + 1 : ROWS + 2, :] = gain_two[0:1, :]
-        s_vector[ROWS + 2 : ROWS + 5, :] = gain_one[0:3, :]
-
+    )(delta, mid, gains, *weights, *([me] if packed else []))
+
+
+def attention_back_kernel(count, d_mid, mix, share, att, wo, s_out, dmix, d_att):
     d_low = d_mid[...].astype(bf16)
-    s_out[...] += dot_at(att[...], d_low)
+    s_out[...] = dot_at(att[...], d_low)
     d_att[...] = dot_bt(d_low, wo[...]).astype(bf16)
     masks = half_masks()
-    for g in range(group):
+    for g in range(count):
         rows = pl.ds(g * ROWS, ROWS)
         for pair in range(HEADS // 2):
             lanes = [pl.ds(D * part + 128 * pair, 128) for part in range(3)]
@@ -618,45 +561,75 @@
             dmix[rows, lanes[0]] = dq.astype(bf16)
             dmix[rows, lanes[1]] = dk.astype(bf16)
             dmix[rows, lanes[2]] = dv.astype(bf16)
+
+
+def layer_zero_attention_back(d_mid, mix, share, att, net):
+    packed = net["packed"]
+    count, rows = share.shape[0], d_mid.shape[0]
+
+    def kernel(d_mid, mix, share, att, weight, *outs):
+        wo = layer_views((weight,), True, 0)[1] if packed else weight.at[pl.ds(0, D)]
+        attention_back_kernel(count, d_mid, mix, share, att, wo, *outs)
+
+    return pl.pallas_call(
+        kernel,
+        in_specs=[whole()] * 5,
+        out_specs=[whole()] * 2,
+        out_shape=[jax.ShapeDtypeStruct((D, D), f32), jax.ShapeDtypeStruct((rows, 3 * D), bf16)],
+        scratch_shapes=[pltpu.VMEM((rows, D), bf16)],
+        compiler_params=pltpu.CompilerParams(vmem_limit_bytes=megabytes(LIMITS[4])),
+        cost_estimate=cost(10),
+        name="layer_zero_attention_back",
+    )(d_mid, mix, share, att, net["arrays"][0 if packed else 1])
+
+
+def input_back_kernel(packed, *refs):
+    (d_mid, state, dmix, pats, s_out, mixes, gains, gain_two, gain_one) = refs[:9]
+    if packed:
+        me, keep, send, s_in, s_patch, s_vector = refs[9:]
+        win = layer_views((mixes,), True, 0)[0]
+    else:
+        s_in, s_patch, s_vector = refs[9:]
+        win = mixes.at[pl.ds(0, D)]
     hat, inv = normalize(state[...])
     normed = (hat * gains[0:1, :]).astype(bf16)
-    s_in[...] += dot_at(normed, dmix[...])
+    s_in[...] = dot_at(normed, dmix[...])
     back, gain = norm_back(hat, inv, gains[0:1, :], dot_bt(dmix[...], win[...]))
-    s_vector[ROWS : ROWS + 1, :] += gain
     d_state = d_mid[...] + back
-    for g in range(group):
+    table = patch = None
+    groups, per = pats.shape[:2]
+    for g in range(groups * per):
         one = d_state[g * ROWS : (g + 1) * ROWS]
-        s_vector[0:ROWS, :] += one
-        image = base + g
-        s_patch[...] += dot_at(pats[image // pats.shape[1], image % pats.shape[1]], one[:PATCHES].astype(bf16))
-    if packed:
-
-        @pl.when(pl.program_id(0) == pl.num_programs(0) - 1)
-        def _():
-            pack_blocks(me[0], keep, send, [(s_in, 24), (s_out, 24)], [(s_patch, 24), (s_vector, 8)])
-
-
-VECTORS = 256
-
-
-def layer_zero_attention_back(d_mid, state, mix, share, att, patches, net, gains, gain_two, gain_one, group, me):
+        part = dot_at(pats[g // per, g % per], one[:PATCHES].astype(bf16))
+        table = one if table is None else table + one
+        patch = part if patch is None else patch + part
+    s_patch[...] = patch
+    s_vector[0:ROWS, :] = table
+    s_vector[ROWS:, :] = jnp.zeros((VECTORS - ROWS, D), f32)
+    s_vector[ROWS : ROWS + 1, :] = gain
+    s_vector[ROWS + 1 : ROWS + 2, :] = gain_two[0:1, :]
+    s_vector[ROWS + 2 : ROWS + 5, :] = gain_one[0:3, :]
+    if packed:
+        pack_blocks(me[0], keep, send, [(s_in, 24), (s_out, 24)], [(s_patch, 24), (s_vector, 8)])
+
+
+def layer_zero_input_back(d_mid, state, dmix, patches, s_out, net, gains, gain_two, gain_one, me):
     packed = net["fast"]
-    weights = net["arrays"][:1] if packed else net["arrays"][:2]
-    slopes, scratch = backward_shapes(packed, [(D, 3 * D), (D, D), (PATCH_DIM, D), (VECTORS, D)], 2)
+    slopes, scratch = backward_shapes(packed, [(D, 3 * D), (PATCH_DIM, D), (VECTORS, D)], 2)
     scalar = [pl.BlockSpec(memory_space=pltpu.SMEM)] if packed else []
-    rows = d_mid.shape[0]
-    step = group * ROWS
     return pl.pallas_call(
-        lambda *refs: attention_back_kernel(packed, group, *refs),
-        grid=(rows // step,),
-        in_specs=[whole()] * (9 + len(weights)) + scalar,
+        lambda *refs: input_back_kernel(packed, *refs),
+        in_specs=[whole()] * 9 + scalar,
         out_specs=[whole()] * len(slopes),
         out_shape=slopes,
-        scratch_shapes=scratch + [pltpu.VMEM((step, D), bf16), pltpu.VMEM((step, 3 * D), bf16)],
-        compiler_params=pltpu.CompilerParams(dimension_semantics=("arbitrary",), vmem_limit_bytes=megabytes(LIMITS[4])),
-        cost_estimate=cost(21),
-        name="layer_zero_attention_back",
-    )(d_mid, state, mix, att, share, patches, *weights, gains, gain_two, gain_one, *([me] if packed else []))
+        scratch_shapes=scratch,
+        compiler_params=pltpu.CompilerParams(vmem_limit_bytes=megabytes(LIMITS[6])),
+        cost_estimate=cost(6),
+        name="layer_zero_input_back",
+    )(d_mid, state, dmix, patches, s_out, net["arrays"][0], gains, gain_two, gain_one, *([me] if packed else []))
+
+
+VECTORS = 256
 
 
 NAMES = ("mix", "out", "up", "down", "patch", "protos")
@@ -799,35 +772,41 @@
     return lax.ppermute(value, "dp", [(i, i ^ (1 << bit)) for i in range(size)])
 
 
-def core_stage(parts):
-    got = [swap(send, 0) for _, send in parts]
-    one, mlp, rest = [(keep.astype(f32) + g.astype(f32)).astype(bf16) for (keep, _), g in zip(parts, got)]
-
-    def join(path, places):
-        a, b, c = one[path, places], mlp[path, places], rest[path, places]
-        return jnp.concatenate([a[:, :288], c[:, :96], b, a[:, 288:320], c[:, 96:128], a[:, 320:], c[:, 128:]], 1)
-
-    return [(join(path, slice(0, 4)), join(path, slice(4, 8))) for path in range(3)]
-
-
-def axis_stage(stage, arrays):
+def after(value, other):
+    value, other = lax.optimization_barrier((value, other))
+    return value, other
+
+
+def core_stage(keep, send, other=None):
+    got = swap(send, 0)
+    if other is not None:
+        keep, other = after(keep, other)
+    total = (keep.astype(f32) + got.astype(f32)).astype(bf16)
+    return total if other is None else (total, other)
+
+
+def halves(total):
+    return [(total[path, :4], total[path, 4:]) for path in range(3)]
+
+
+def axis_stage(stage, arrays, other=None):
     got = [swap(arrays[path][1], BITS[PATHS[path][stage]]) for path in range(3)]
-    total = [arrays[path][0].astype(f32) + got[path].astype(f32) for path in range(3)]
+    kept = [keep for keep, _ in arrays]
+    if other is not None:
+        kept, other = after(kept, other)
+    total = [kept[path].astype(f32) + got[path].astype(f32) for path in range(3)]
     if stage == 3:
         return jnp.concatenate(total, 0)
     half = total[0].shape[0] // 2
     total = [t.astype(bf16) for t in total]
-    return [(t[:half], t[half:]) for t in total]
-
-
-def scatter_gradients(parts, me):
-    arrays = core_stage(parts)
-    for stage in (1, 2, 3):
-        arrays = axis_stage(stage, arrays)
+    arrays = [(t[:half], t[half:]) for t in total]
+    return arrays if other is None else (arrays, other)
+
+
+def last_stage(one, zero, me):
     upper = (me[0] >> 4) == 1
-    one, zero = arrays[:, :288], arrays[:, 288:576]
-    keep = jnp.concatenate([jnp.where(upper, one, zero), arrays[:, 576:640]], 1)
-    send = jnp.concatenate([jnp.where(upper, zero, one), arrays[:, 640:]], 1)
+    keep = jnp.concatenate([jnp.where(upper, one[:, :288], zero[:, :288]), one[:, 288:320], zero[:, 288:320]], 1)
+    send = jnp.concatenate([jnp.where(upper, zero[:, :288], one[:, :288]), one[:, 320:], zero[:, 320:]], 1)
     return keep, swap(send.astype(bf16), 4)
 
 
@@ -1022,26 +1001,36 @@
     (targets,) = forward(target_patches, table_of(teacher_rows), plain, teacher, teacher_gains0, teacher_gains1, False, n)
     if student["fast"]:
         targets, bias = lax.optimization_barrier((targets, bias))
-    state1, state0, mix, share, att, mid, act, dgelu, logs, sums, kv, queries, shares, att_c, mid_c, expanded, last, cls, *natural = forward(
+    state1, state0, mix, share, att, mid, logs, sums, kv, queries, shares, att_c, mid_c, expanded, last, cls, *natural = forward(
         anchor_patches, table_of(vector_rows), bias, student, gains0, gains1, True, n)
     student["natural"] = natural
     mean_sum = lax.all_to_all(sums, "dp", 0, 0, tiled=True)
     delta, gain_one, report, *one = layer_one_back(
         (logs, targets, mean_sum, state1, kv, queries, shares, att_c, mid_c, expanded, last, cls), student, gains1, inverse_count, me)
-    d_mid, gain_two, *mlp = layer_zero_mlp_back(delta, act, dgelu, mid, student, gains0, GROUP, me)
-    rest = layer_zero_attention_back(d_mid, state0, mix, share, att, anchor_patches, student, gains0, gain_two, gain_one, GROUP, me)
+    d_mid, gain_two, *mlp = layer_zero_mlp_back(delta, mid, student, gains0, me)
     if student["fast"]:
-        slopes, line = collect(*scatter_gradients([one, mlp, rest], me), report, n, attention_in.shape[0])
+        one, d_mid = core_stage(*one, d_mid)
+    out0, dmix = layer_zero_attention_back(d_mid, mix, share, att, student)
+    if student["fast"]:
+        one, dmix = axis_stage(1, halves(one), dmix)
+        mlp, dmix = core_stage(*mlp, dmix)
+    rest = layer_zero_input_back(d_mid, state0, dmix, anchor_patches, out0, student, gains0, gain_two, gain_one, me)
+    if student["fast"]:
+        one, rest = axis_stage(2, one, rest)
+        mlp, rest = axis_stage(1, halves(mlp), rest)
+        rest = axis_stage(1, halves(core_stage(*rest)))
+        zero = [tuple(jnp.concatenate([c[:, :96], b, c[:, 96:]], 1) for b, c in zip(bs, cs)) for bs, cs in zip(mlp, rest)]
+        zero, one = lax.optimization_barrier((zero, one))
+        keep, got = last_stage(axis_stage(3, one), axis_stage(3, axis_stage(2, zero)), me)
+        slopes, line = collect(keep, got, report, n, attention_in.shape[0])
         update = update_rows
     else:
-        slopes, line = collect_plain(one, mlp, rest, report, n)
+        mix0, patch0, vectors = rest
+        slopes, line = collect_plain(one, mlp, (mix0, out0, patch0, vectors), report, n)
         update = update_plain
     arrived = lax.all_to_all(line, "dp", 0, 0, tiled=True)
     *states, loss, norm = update(slopes, arrived, report, masters, firsts, seconds, fixes)
     return (loss[0, 0], norm[0, 0], *states)
-
-
-GROUP = 3
 
 
 def solution(mesh):

time: 274 us -> 258 us (0.942)
  waiting for transfers between devices: 89.4 us -> 74.3 us
  starting transfers between devices: 29.5 us -> 44 us
  Pallas kernels: 90.6 us -> 80.6 us
  other arithmetic: 7.46 us -> 3.3 us
    ppermute x26 -> x38, waiting for transfers between devices: 79.5 us -> 64.5 us  [swap(): return lax.ppermute(value, 'dp', [(i, i ^ 1 << bit) for i in range(size)])]
    ppermute x26 -> x38, starting transfers between devices: 26.2 us -> 40.7 us  [swap(): return lax.ppermute(value, 'dp', [(i, i ^ 1 << bit) for i in range(size)])]
    pallas_call x2, Pallas kernels: 41.8 us -> 34.2 us  [forward(): pl.pallas_call(lambda *refs: forward_kernel(save, packed, count, *refs),...]
    convert_element_type x3, other arithmetic: 5.55 us -> 1.21 us  [core_stage(): total = (keep.astype(f32) + got.astype(f32)).astype(bf16)]
    pallas_call x2 -> x3, Pallas kernels: 28.4 us -> 26.9 us  [the longest x1 13.2 us: layer_zero_mlp_back(): pl.pallas_call(lambda *refs: mlp_back_kernel(packed, *refs), in_specs=[wh...]
    unnamed x117 -> x81, local copies, waits for them, and re-layouts: 18.8 us -> 17.5 us
  transfers between devices with their start and end apart: 28 -> 40, of which waited for: 15 -> 22; matrix products, arithmetic and copies ran while one was open for 8% -> 7% of each run, Pallas kernels for 20% -> 19%
where the time goes in v1:
time: 258 us; the launch traced here: 254 us
  Pallas kernels  80.6 us (31%)
  waiting for transfers between devices  74.3 us (29%)
  starting transfers between devices  44 us (17%)
  local copies, waits for them, and re-layouts  24 us (9%)
  between operations  16.1 us (6%)
  blocking collectives  11.6 us (4%)
  other arithmetic  3.3 us (1%)
    ppermute x38, waiting for transfers between devices, swap(): return lax.ppermute(value, 'dp', [(i, i ^ 1 << bit) for i in range(size)])  64.5 us
    ppermute x38, starting transfers between devices, swap(): return lax.ppermute(value, 'dp', [(i, i ^ 1 << bit) for i in range(size)])  40.7 us
    pallas_call x2, Pallas kernels, forward(): pl.pallas_call(lambda *refs: forward_kernel(save, packed, count, *refs),...  34.2 us
    unnamed x81, local copies, waits for them, and re-layouts  17.5 us
    pallas_call x1, Pallas kernels, layer_zero_mlp_back(): pl.pallas_call(lambda *refs: mlp_back_kernel(packed, *refs), in_specs=[wh...  13.2 us
    all_to_all x1, blocking collectives, local(): mean_sum = lax.all_to_all(sums, 'dp', 0, 0, tiled=True)  11.6 us
    all_to_all x1, waiting for transfers between devices, local(): arrived = lax.all_to_all(line, 'dp', 0, 0, tiled=True)  9.79 us
    pallas_call x1, Pallas kernels, layer_one_back(): pl.pallas_call(lambda *refs: class_back_kernel(packed, count, inverse_cou...  8.67 us
  transfers between devices with their start and end apart: 40, of which 22 were waited for; matrix products, arithmetic and copies ran while one was open for 7% of the time, Pallas kernels for 19%

profile of v1, /device:TPU:0, one launch (start us, length us, event | category | flops | bytes accessed | tf_op | source)
XLA Modules:
  0.0 253.9 jit_solution(7567940709865529712)
XLA Ops:
  7.2 2.0 pack_weights.1
  9.3 4.1 %collective-permute-start = (bf16[24,5504]{1,0:T(8,128)(2,1)}, bf16[24,5504]{1,0:T(8,128)(2,1)S(1)}, u32[]{:S(2)}, u32[]{:S(2)}) collective-permute-start(bf16[24,5504]{1,0:T(8,128)(2,1)} %get-tuple-element.125), channel_id=1, source_target_pairs={{0,16},{1,17},{2,18},{3,19},{4,20},{5,21},{6,22},{7,23},{8,24},{9,... | collective-permute-start | bytes 792584 | tf_op jit(solution)/shard_map/ppermute | solution.py:772
  14.3 1.6 constant_dynamic-update-slice_fusion.9
  17.8 7.8 %collective-permute-done = bf16[24,5504]{1,0:T(8,128)(2,1)S(1)} collective-permute-done((bf16[24,5504]{1,0:T(8,128)(2,1)}, bf16[24,5504]{1,0:T(8,128)(2,1)S(1)}, u32[]{:S(2)}, u32[]{:S(2)}) %collective-permute-start) | collective-permute-done | bytes 264224 | tf_op jit(solution)/shard_map/ppermute | solution.py:772
  25.7 1.6 collective-permute-start.4
  28.9 2.8 %collective-permute-start.7 = (bf16[2,24,1920]{2,1,0:T(8,128)(2,1)S(1)}, bf16[2,24,1920]{2,1,0:T(8,128)(2,1)S(1)}, u32[]{:S(2)}, u32[]{:S(2)}) collective-permute-start(bf16[2,24,1920]{2,1,0:T(8,128)(2,1)S(1)} %pad_maximum_fusion.10), channel_id=1, source_target_pairs={{0,8},{1,9},{2,10},{3,11},{4,12},{5,13},{6,14},{7,15},{8,0},{9,1},... | collective-permute-start | bytes 552968 | tf_op jit(solution)/shard_map/ppermute | solution.py:772
  32.5 2.3 collective-permute-start.5
  39.9 9.9 %collective-permute-done.5 = bf16[4,24,1792]{2,1,0:T(8,128)(2,1)S(1)} collective-permute-done((bf16[4,24,1792]{2,1,0:T(8,128)(2,1)S(1)}, bf16[4,24,1792]{2,1,0:T(8,128)(2,1)S(1)}, u32[]{:S(2)}, u32[]{:S(2)}) %collective-permute-start.5) | collective-permute-done | bytes 344096 | tf_op jit(solution)/shard_map/ppermute | solution.py:772
  50.8 5.6 %collective-permute-done.8 = bf16[4,24,1920]{2,1,0:T(8,128)(2,1)S(1)} collective-permute-done((bf16[4,24,1920]{2,1,0:T(8,128)(2,1)S(1)}, bf16[4,24,1920]{2,1,0:T(8,128)(2,1)S(1)}, u32[]{:S(2)}, u32[]{:S(2)}) %collective-permute-start.8) | collective-permute-done | bytes 368672 | tf_op jit(solution)/shard_map/ppermute | solution.py:772
  58.7 12.0 %collective-permute-done.6 = bf16[8,24,1792]{2,1,0:T(8,128)(2,1)S(1)} collective-permute-done((bf16[8,24,1792]{2,1,0:T(8,128)(2,1)S(1)}, bf16[8,24,1792]{2,1,0:T(8,128)(2,1)S(1)}, u32[]{:S(2)}, u32[]{:S(2)}) %collective-permute-start.6) | collective-permute-done | bytes 688160 | tf_op jit(solution)/shard_map/ppermute | solution.py:772
  75.1 1.9 copy.60.refs_0_
  78.9 2.2 collective-permute-done.10.refs_3_.refs_9_.refs_15_.refs_21_
  81.2 5.3 %unpack_weights.1 = (bf16[768,1152]{1,0:T(8,128)(2,1)S(1)}, bf16[768,384]{1,0:T(8,128)(2,1)S(1)}, bf16[768,1536]{1,0:T(8,128)(2,1)S(1)}, bf16[3072,384]{1,0:T(8,...) custom-call(s32[1]{0:T(128)} %bitcast.3.me.refs_12_.refs_5_.refs_9_, ...), custom_call_target="tpu_custom_call" | custom-call | flops 8999999488 | bytes 27000000 | tf_op jit(solution)/shard_map/unpack_weights/pallas_call | solution.py:716
  86.7 16.8 %teacher_forward.1.refs_1_ = f32[16,1024]{1,0:T(8,128)S(1)} custom-call(bf16[2,3,196,768]{3,2,1,0:T(8,128)(2,1)S(1)} %copy.60.refs_0_, f32[208,384]{1,0:T(8,128)S(1)} %get-tuple-element.285.refs_1_, f32[6,1,208]{2,1,0:T(1,128)S(1)} %copy.61.refs_2_, bf16[6,208,128]{2,1,0:T(8,128)(2,1)S(1)} %broadcast_in_dim.45.refs_3_, f32[8,384]{1,0:T(8,128)S(1)} %concatenate.94.refs_4_, ...), custom_call_target="tpu_custom_call" | custom-call | flops 30000001024 | bytes 90000000 | tf_op jit(solution)/shard_map/teacher_forward/pallas_call | solution.py:295
  103.9 3.4 %copy-done.3 = bf16[768,5504]{1,0:T(8,128)(2,1)S(1)} copy-done((bf16[768,5504]{1,0:T(8,128)(2,1)S(1)}, bf16[768,5504]{1,0:T(8,128)(2,1)}, u32[]{:S(2)}) %copy-start.3) | copy-done | bytes 8454168
  107.3 17.3 %student_forward.1 = (f32[1248,384]{1,0:T(8,128)S(1)}, f32[1248,384]{1,0:T(8,128)S(1)}, bf16[1248,1152]{1,0:T(8,128)(2,1)S(1)}, bf16[6,6,208,208]{3,2,1,0:T(8,12...) custom-call(bf16[2,3,196,768]{3,2,1,0:T(8,128)(2,1)S(1)} %copy-done,, ...), custom_call_target="tpu_custom_call" | custom-call | flops 30000001024 | bytes 90000000 | tf_op jit(solution)/shard_map/student_forward/pallas_call | solution.py:295
  127.5 11.6 %all_to_all.10.refs_2_ = bf16[32,16,128]{2,1,0:T(8,128)(2,1)S(1)} all-to-all(bf16[32,16,128]{2,1,0:T(8,128)(2,1)S(1)} %get-tuple-element.136), channel_id=1, replica_groups=mesh['dp'=32] {'dp'}, dimensions={0} | all-to-all | bytes 262144 | tf_op jit(solution)/shard_map/all_to_all | solution.py:1007
  140.6 8.7 %layer_one_back.1 = (f32[1248,384]{1,0:T(8,128)S(1)}, f32[8,384]{1,0:T(8,128)S(1)}, f32[8,128]{1,0:T(8,128)S(1)}, bf16[3,8,352,128]{3,2,1,0:T(8,128)(2,1)S(1)}, bf16[3,8,352,128]{3,2,1,0:T(8,128)(2,1)S(1)}) custom-call(f32[16,1024]{1,0:T(8,128)S(1)} %get-tuple-element.134.refs_0_, f32[16,1024]{1,0:T(8,128)S(1)} %teacher_forward.1.refs_1_, ...), custom_call_target="tpu_custom_call" | custom-call | flops 12999999488 | bytes 39000000 | tf_op jit(solution)/shard_map/layer_one_back/pallas_call | solution.py:470
  149.6 13.2 %layer_zero_mlp_back.1 = (f32[1248,384]{1,0:T(8,128)S(1)}, f32[8,384]{1,0:T(8,128)S(1)}, bf16[3,8,192,128]{3,2,1,0:T(8,128)(2,1)S(1)}, bf16[3,8,192,128]{3,2,1,0:T(8,128)(2,1)S(1)}) custom-call(f32[1248,384]{1,0:T(8,128)S(1)} %get-tuple-element.149.refs_0_, f32[1248,384]{1,0:T(8,128)S(1)} %get-tuple-element.150.refs_1_, ...), custom_call_target="tpu_custom_call" | custom-call | flops 12000000000 | bytes 36000000 | tf_op jit(solution)/shard_map/layer_zero_mlp_back/pallas_call | solution.py:522
  163.1 8.2 %layer_zero_attention_back.1 = (f32[384,384]{1,0:T(8,128)S(1)}, bf16[1248,1152]{1,0:T(8,128)(2,1)S(1)}) custom-call(f32[1248,384]{1,0:T(8,128)S(1)} %get-tuple-element.157.d_mid.refs_0_, bf16[1248,1152]{1,0:T(8,128)(2,1)S(1)} %copy-done.26, bf16[6,6,208,208]{3,2,1,0:T(8,128)(2,1)S(1)} %get-tuple-element.159.share, ...), custom_call_target="tpu_custom_call" | custom-call | flops 10000000000 | bytes 30000000 | tf_op jit(solution)/shard_map/layer_zero_attention_back/pallas_call | solution.py:574
  177.2 5.5 %layer_zero_input_back.1 = (bf16[3,8,160,128]{3,2,1,0:T(8,128)(2,1)S(1)}, bf16[3,8,160,128]{3,2,1,0:T(8,128)(2,1)S(1)}) custom-call(f32[1248,384]{1,0:T(8,128)S(1)} %get-tuple-element.157.d_mid.refs_0_, f32[1248,384]{1,0:T(8,128)S(1)} %get-tuple-element.168.refs_1_, bf16[1248,1152]{1,0:T(8,128)(2,1)S(1)} %get-tuple-element.169.refs_2_, ...), custom_call_target="tpu_custom_call" | custom-call | flops 6000000000 | bytes 18000000 | tf_op jit(solution)/shard_map/layer_zero_input_back/pallas_call | solution.py:620
  187.6 2.1 collective-permute-start.25
  190.9 1.8 collective-permute-done.27
  196.4 2.6 %collective-permute-done.19 = bf16[4,160,128]{2,1,0:T(8,128)(2,1)S(1)} collective-permute-done((bf16[4,160,128]{2,1,0:T(8,128)(2,1)S(1)}, bf16[4,160,128]{2,1,0:T(8,128)(2,1)S(1)}, u32[]{:S(2)}, u32[]{:S(2)}) %collective-permute-start.19) | collective-permute-done | bytes 163872 | tf_op jit(solution)/shard_map/ppermute | solution.py:772
  202.6 2.3 collective-permute-start.29
  204.9 2.0 collective-permute-start.31
  209.5 2.8 %collective-permute-done.31 = bf16[2,352,128]{2,1,0:T(8,128)(2,1)S(1)} collective-permute-done((bf16[2,352,128]{2,1,0:T(8,128)(2,1)S(1)}, bf16[2,352,128]{2,1,0:T(8,128)(2,1)S(1)}, u32[]{:S(2)}, u32[]{:S(2)}) %collective-permute-start.31) | collective-permute-done | bytes 180256 | tf_op jit(solution)/shard_map/ppermute | solution.py:772
  215.0 2.9 %collective-permute-done.32 = bf16[1,352,128]{2,1,0:T(8,128)(2,1)S(1)} collective-permute-done((bf16[1,352,128]{2,1,0:T(8,128)(2,1)S(1)}, bf16[1,352,128]{2,1,0:T(8,128)(2,1)S(1)}, u32[]{:S(2)}, u32[]{:S(2)}) %collective-permute-start.32) | collective-permute-done | bytes 90144 | tf_op jit(solution)/shard_map/ppermute | solution.py:772
  219.8 9.4 %collective-permute-done.37.refs_1_ = bf16[3,352,128]{2,1,0:T(8,128)(2,1)S(1)} collective-permute-done((bf16[3,352,128]{2,1,0:T(8,128)(2,1)S(1)}, bf16[3,352,128]{2,1,0:T(8,128)(2,1)S(1)}, u32[]{:S(2)}, u32[]{:S(2)}) %collective-permute-start.37) | collective-permute-done | bytes 270368 | tf_op jit(solution)/shard_map/ppermute | solution.py:772
  230.3 3.2 %all-to-all-start.1 = ((bf16[32,8,512]{2,1,0:T(8,128)(2,1)}), bf16[32,8,512]{2,1,0:T(8,128)(2,1)S(1)}, u32[]{:S(2)}, u32[]{:S(2)}) async-start(bf16[32,8,512]{2,1,0:T(8,128)(2,1)} %get-tuple-element.197), calls=%async_computation.1 | async-start | bytes 524288 | tf_op jit(solution)/shard_map/all_to_all | solution.py:1031
  234.3 9.8 %all-to-all-done.1.refs_2_ = bf16[32,8,512]{2,1,0:T(8,128)(2,1)S(1)} async-done(((bf16[32,8,512]{2,1,0:T(8,128)(2,1)}), bf16[32,8,512]{2,1,0:T(8,128)(2,1)S(1)}, u32[]{:S(2)}, u32[]{:S(2)}) %all-to-all-start.1) | async-done | bytes 262176 | tf_op jit(solution)/shard_map/all_to_all | solution.py:1031
  244.3 2.6 %update_rows.1 = (f32[24,1152]{1,0:T(8,128)}, f32[24,384]{1,0:T(8,128)}, f32[24,1536]{1,0:T(8,128)}, f32[96,384]{1,0:T(8,128)}, f32[24,384]{1,0:T(8,128)}, /*ind...) custom-call(f32[2]{0:T(128)S(1)} %pad_maximum_fusion.20.refs_0_, ...), custom_call_target="tpu_custom_call" | custom-call | flops 4000000000 | bytes 12000000 | tf_op jit(solution)/shard_map/update_rows/pallas_call | solution.py:897
  (244 shorter events, 52.1 us)
Async XLA Ops:
  7.2 96.4 %all-gather.2.cloned.1.call-start = ((), (), s32[]{:S(2)}) async-start(), calls=%async_computation.2 | async-start | bytes 8718336 | tf_op jit(solution)/shard_map/all_gather | solution.py:749
  9.3 16.3 %collective-permute-start = (bf16[24,5504]{1,0:T(8,128)(2,1)}, bf16[24,5504]{1,0:T(8,128)(2,1)S(1)}, u32[]{:S(2)}, u32[]{:S(2)}) collective-permute-start(bf16[24,5504]{1,0:T(8,128)(2,1)} %get-tuple-element.125), channel_id=1, source_target_pairs={{0,16},{1,17},{2,18},{3,19},{4,20},{5,21},{6,22},{7,23},{8,24},{9,... | collective-permute-start | bytes 792584 | tf_op jit(solution)/shard_map/ppermute | solution.py:772
  25.7 6.8 %collective-permute-start.4 = (bf16[2,24,1792]{2,1,0:T(8,128)(2,1)S(1)}, bf16[2,24,1792]{2,1,0:T(8,128)(2,1)S(1)}, u32[]{:S(2)}, u32[]{:S(2)}) collective-permute-start(bf16[2,24,1792]{2,1,0:T(8,128)(2,1)S(1)} %pad_maximum_fusion.18), channel_id=1, source_target_pairs={{0,4},{1,5},{2,6},{3,7},{4,0},{5,1},{6,2},{7,3},{8,12},{9,13},{10,... | collective-permute-start | bytes 516104 | tf_op jit(solution)/shard_map/ppermute | solution.py:772
  27.3 7.5 %collective-permute-start.1 = (bf16[2,24,1792]{2,1,0:T(8,128)(2,1)S(1)}, bf16[2,24,1792]{2,1,0:T(8,128)(2,1)S(1)}, u32[]{:S(2)}, u32[]{:S(2)}) collective-permute-start(bf16[2,24,1792]{2,1,0:T(8,128)(2,1)S(1)} %pad_maximum_fusion.17), channel_id=1, source_target_pairs={{0,2},{1,3},{2,0},{3,1},{4,6},{5,7},{6,4},{7,5},{8,10},{9,11},{10,... | collective-permute-start | bytes 516104 | tf_op jit(solution)/shard_map/ppermute | solution.py:772
  28.9 9.8 %collective-permute-start.7 = (bf16[2,24,1920]{2,1,0:T(8,128)(2,1)S(1)}, bf16[2,24,1920]{2,1,0:T(8,128)(2,1)S(1)}, u32[]{:S(2)}, u32[]{:S(2)}) collective-permute-start(bf16[2,24,1920]{2,1,0:T(8,128)(2,1)S(1)} %pad_maximum_fusion.10), channel_id=1, source_target_pairs={{0,8},{1,9},{2,10},{3,11},{4,12},{5,13},{6,14},{7,15},{8,0},{9,1},... | collective-permute-start | bytes 552968 | tf_op jit(solution)/shard_map/ppermute | solution.py:772
  32.5 17.3 %collective-permute-start.5 = (bf16[4,24,1792]{2,1,0:T(8,128)(2,1)S(1)}, bf16[4,24,1792]{2,1,0:T(8,128)(2,1)S(1)}, u32[]{:S(2)}, u32[]{:S(2)}) collective-permute-start(bf16[4,24,1792]{2,1,0:T(8,128)(2,1)S(1)} %pad_maximum_fusion.8), channel_id=1, source_target_pairs={{0,8},{1,9},{2,10},{3,11},{4,12},{5,13},{6,14},{7,15},{8,0},{9,1},... | collective-permute-start | bytes 1032200 | tf_op jit(solution)/shard_map/ppermute | solution.py:772
  34.9 15.7 %collective-permute-start.2 = (bf16[4,24,1792]{2,1,0:T(8,128)(2,1)S(1)}, bf16[4,24,1792]{2,1,0:T(8,128)(2,1)S(1)}, u32[]{:S(2)}, u32[]{:S(2)}) collective-permute-start(bf16[4,24,1792]{2,1,0:T(8,128)(2,1)S(1)} %pad_maximum_fusion.7), channel_id=1, source_target_pairs={{0,4},{1,5},{2,6},{3,7},{4,0},{5,1},{6,2},{7,3},{8,12},{9,13},{10,... | collective-permute-start | bytes 1032200 | tf_op jit(solution)/shard_map/ppermute | solution.py:772
  38.8 17.6 %collective-permute-start.8 = (bf16[4,24,1920]{2,1,0:T(8,128)(2,1)S(1)}, bf16[4,24,1920]{2,1,0:T(8,128)(2,1)S(1)}, u32[]{:S(2)}, u32[]{:S(2)}) collective-permute-start(bf16[4,24,1920]{2,1,0:T(8,128)(2,1)S(1)} %pad_maximum_fusion.6), channel_id=1, source_target_pairs={{0,2},{1,3},{2,0},{3,1},{4,6},{5,7},{6,4},{7,5},{8,10},{9,11},{10,... | collective-permute-start | bytes 1105928 | tf_op jit(solution)/shard_map/ppermute | solution.py:772
  49.9 20.8 %collective-permute-start.6 = (bf16[8,24,1792]{2,1,0:T(8,128)(2,1)S(1)}, bf16[8,24,1792]{2,1,0:T(8,128)(2,1)S(1)}, u32[]{:S(2)}, u32[]{:S(2)}) collective-permute-start(bf16[8,24,1792]{2,1,0:T(8,128)(2,1)S(1)} %pad_maximum_fusion.2), channel_id=1, source_target_pairs={{0,2},{1,3},{2,0},{3,1},{4,6},{5,7},{6,4},{7,5},{8,10},{9,11},{10,... | collective-permute-start | bytes 2064392 | tf_op jit(solution)/shard_map/ppermute | solution.py:772
  50.7 21.8 %collective-permute-start.3 = (bf16[8,24,1792]{2,1,0:T(8,128)(2,1)S(1)}, bf16[8,24,1792]{2,1,0:T(8,128)(2,1)S(1)}, u32[]{:S(2)}, u32[]{:S(2)}) collective-permute-start(bf16[8,24,1792]{2,1,0:T(8,128)(2,1)S(1)} %pad_maximum_fusion.1), channel_id=1, source_target_pairs={{0,8},{1,9},{2,10},{3,11},{4,12},{5,13},{6,14},{7,15},{8,0},{9,1},... | collective-permute-start | bytes 2064392 | tf_op jit(solution)/shard_map/ppermute | solution.py:772
  56.5 15.2 %collective-permute-start.9 = (bf16[8,24,1920]{2,1,0:T(8,128)(2,1)S(1)}, bf16[8,24,1920]{2,1,0:T(8,128)(2,1)S(1)}, u32[]{:S(2)}, u32[]{:S(2)}) collective-permute-start(bf16[8,24,1920]{2,1,0:T(8,128)(2,1)S(1)} %pad_maximum_fusion), channel_id=1, source_target_pairs={{0,4},{1,5},{2,6},{3,7},{4,0},{5,1},{6,2},{7,3},{8,12},{9,13},{10,... | collective-permute-start | bytes 2211848 | tf_op jit(solution)/shard_map/ppermute | solution.py:772
  71.6 7.3 %collective-permute-start.11 = (bf16[16,24,1792]{2,1,0:T(8,128)(2,1)}, bf16[16,24,1792]{2,1,0:T(8,128)(2,1)}, u32[]{:S(2)}, u32[]{:S(2)}) collective-permute-start(bf16[16,24,1792]{2,1,0:T(8,128)(2,1)} %constant_dynamic-update-slice_fusion.5.refs_1_.refs_7_.refs_13_.refs_19_), channel_id=1, source_target_pairs={{0,1},{1,0},{2,3},{3,2},{4,5},{5,4},{6,7},{7,6},{8,9},{9,8},{10,11... | collective-permute-start | bytes 4128776 | tf_op jit(solution)/shard_map/ppermute | solution.py:772
  71.8 9.4 %collective-permute-start.12 = (bf16[16,24,1920]{2,1,0:T(8,128)(2,1)S(1)}, bf16[16,24,1920]{2,1,0:T(8,128)(2,1)S(1)}, u32[]{:S(2)}, u32[]{:S(2)}) collective-permute-start(bf16[16,24,1920]{2,1,0:T(8,128)(2,1)S(1)} %constant_dynamic-update-slice_fusion.10.refs_2_.refs_8_.refs_14_.refs_20_), channel_id=1, source_target_pairs={{0,1},{1,0},{2,3},{3,2},{4,5},{5,4},{6,7},{7,6},{8,9},{9,8},{10,11... | collective-permute-start | bytes 4423688 | tf_op jit(solution)/shard_map/ppermute | solution.py:772
  73.4 7.7 %collective-permute-start.10 = (bf16[16,24,1792]{2,1,0:T(8,128)(2,1)}, bf16[16,24,1792]{2,1,0:T(8,128)(2,1)}, u32[]{:S(2)}, u32[]{:S(2)}) collective-permute-start(bf16[16,24,1792]{2,1,0:T(8,128)(2,1)} %constant_dynamic-update-slice_fusion.refs_0_.refs_6_.refs_12_.refs_18_), channel_id=1, source_target_pairs={{0,1},{1,0},{2,3},{3,2},{4,5},{5,4},{6,7},{7,6},{8,9},{9,8},{10,11... | collective-permute-start | bytes 4128776 | tf_op jit(solution)/shard_map/ppermute | solution.py:772
  149.3 22.0 %collective-permute-start.13 = (bf16[3,8,352,128]{3,2,1,0:T(8,128)(2,1)S(1)}, bf16[3,8,352,128]{3,2,1,0:T(8,128)(2,1)S(1)}, u32[]{:S(2)}, u32[]{:S(2)}) collective-permute-start(bf16[3,8,352,128]{3,2,1,0:T(8,128)(2,1)S(1)} %get-tuple-element.156), channel_id=1, source_target_pairs={{0,1},{1,0},{2,3},{3,2},{4,5},{5,4},{6,7},{7,6},{8,9},{9,8},{10,11... | collective-permute-start | bytes 6488072 | tf_op jit(solution)/shard_map/ppermute | solution.py:772
  162.8 11.6 %collective-permute-start.14 = (bf16[3,8,192,128]{3,2,1,0:T(8,128)(2,1)S(1)}, bf16[3,8,192,128]{3,2,1,0:T(8,128)(2,1)S(1)}, u32[]{:S(2)}, u32[]{:S(2)}) collective-permute-start(bf16[3,8,192,128]{3,2,1,0:T(8,128)(2,1)S(1)} %get-tuple-element.164), channel_id=1, source_target_pairs={{0,1},{1,0},{2,3},{3,2},{4,5},{5,4},{6,7},{7,6},{8,9},{9,8},{10,11... | collective-permute-start | bytes 3538952 | tf_op jit(solution)/shard_map/ppermute | solution.py:772
  172.1 11.3 %collective-permute-start.16 = (bf16[4,352,128]{2,1,0:T(8,128)(2,1)S(1)}, bf16[4,352,128]{2,1,0:T(8,128)(2,1)S(1)}, u32[]{:S(2)}, u32[]{:S(2)}) collective-permute-start(bf16[4,352,128]{2,1,0:T(8,128)(2,1)S(1)} %get-tuple-element.228), channel_id=1, source_target_pairs={{0,4},{1,5},{2,6},{3,7},{4,0},{5,1},{6,2},{7,3},{8,12},{9,13},{10,... | collective-permute-start | bytes 1081352 | tf_op jit(solution)/shard_map/ppermute | solution.py:772
  172.9 11.6 %collective-permute-start.17 = (bf16[4,352,128]{2,1,0:T(8,128)(2,1)S(1)}, bf16[4,352,128]{2,1,0:T(8,128)(2,1)S(1)}, u32[]{:S(2)}, u32[]{:S(2)}) collective-permute-start(bf16[4,352,128]{2,1,0:T(8,128)(2,1)S(1)} %get-tuple-element.227), channel_id=1, source_target_pairs={{0,8},{1,9},{2,10},{3,11},{4,12},{5,13},{6,14},{7,15},{8,0},{9,1},... | collective-permute-start | bytes 1081352 | tf_op jit(solution)/shard_map/ppermute | solution.py:772
  173.5 11.2 %collective-permute-start.15 = (bf16[4,352,128]{2,1,0:T(8,128)(2,1)S(1)}, bf16[4,352,128]{2,1,0:T(8,128)(2,1)S(1)}, u32[]{:S(2)}, u32[]{:S(2)}) collective-permute-start(bf16[4,352,128]{2,1,0:T(8,128)(2,1)S(1)} %get-tuple-element.229), channel_id=1, source_target_pairs={{0,2},{1,3},{2,0},{3,1},{4,6},{5,7},{6,4},{7,5},{8,10},{9,11},{10,... | collective-permute-start | bytes 1081352 | tf_op jit(solution)/shard_map/ppermute | solution.py:772
  174.8 12.8 %collective-permute-start.24 = (bf16[4,192,128]{2,1,0:T(8,128)(2,1)S(1)}, bf16[4,192,128]{2,1,0:T(8,128)(2,1)S(1)}, u32[]{:S(2)}, u32[]{:S(2)}) collective-permute-start(bf16[4,192,128]{2,1,0:T(8,128)(2,1)S(1)} %get-tuple-element.233), channel_id=1, source_target_pairs={{0,8},{1,9},{2,10},{3,11},{4,12},{5,13},{6,14},{7,15},{8,0},{9,1},... | collective-permute-start | bytes 589832 | tf_op jit(solution)/shard_map/ppermute | solution.py:772
  176.2 13.6 %collective-permute-start.22 = (bf16[4,192,128]{2,1,0:T(8,128)(2,1)S(1)}, bf16[4,192,128]{2,1,0:T(8,128)(2,1)S(1)}, u32[]{:S(2)}, u32[]{:S(2)}) collective-permute-start(bf16[4,192,128]{2,1,0:T(8,128)(2,1)S(1)} %get-tuple-element.234), channel_id=1, source_target_pairs={{0,4},{1,5},{2,6},{3,7},{4,0},{5,1},{6,2},{7,3},{8,12},{9,13},{10,... | collective-permute-start | bytes 589832 | tf_op jit(solution)/shard_map/ppermute | solution.py:772
  183.4 7.4 %collective-permute-start.20 = (bf16[4,192,128]{2,1,0:T(8,128)(2,1)S(1)}, bf16[4,192,128]{2,1,0:T(8,128)(2,1)S(1)}, u32[]{:S(2)}, u32[]{:S(2)}) collective-permute-start(bf16[4,192,128]{2,1,0:T(8,128)(2,1)S(1)} %get-tuple-element.235), channel_id=1, source_target_pairs={{0,2},{1,3},{2,0},{3,1},{4,6},{5,7},{6,4},{7,5},{8,10},{9,11},{10,... | collective-permute-start | bytes 589832 | tf_op jit(solution)/shard_map/ppermute | solution.py:772
  184.9 7.9 %collective-permute-start.27 = (bf16[2,352,128]{2,1,0:T(8,128)(2,1)S(1)}, bf16[2,352,128]{2,1,0:T(8,128)(2,1)S(1)}, u32[]{:S(2)}, u32[]{:S(2)}) collective-permute-start(bf16[2,352,128]{2,1,0:T(8,128)(2,1)S(1)} %get-tuple-element.245), channel_id=1, source_target_pairs={{0,2},{1,3},{2,0},{3,1},{4,6},{5,7},{6,4},{7,5},{8,10},{9,11},{10,... | collective-permute-start | bytes 540680 | tf_op jit(solution)/shard_map/ppermute | solution.py:772
  185.9 6.9 %collective-permute-start.26 = (bf16[2,352,128]{2,1,0:T(8,128)(2,1)S(1)}, bf16[2,352,128]{2,1,0:T(8,128)(2,1)S(1)}, u32[]{:S(2)}, u32[]{:S(2)}) collective-permute-start(bf16[2,352,128]{2,1,0:T(8,128)(2,1)S(1)} %get-tuple-element.247), channel_id=1, source_target_pairs={{0,8},{1,9},{2,10},{3,11},{4,12},{5,13},{6,14},{7,15},{8,0},{9,1},... | collective-permute-start | bytes 540680 | tf_op jit(solution)/shard_map/ppermute | solution.py:772
  195.7 5.7 %collective-permute-start.23 = (bf16[4,160,128]{2,1,0:T(8,128)(2,1)S(1)}, bf16[4,160,128]{2,1,0:T(8,128)(2,1)S(1)}, u32[]{:S(2)}, u32[]{:S(2)}) collective-permute-start(bf16[4,160,128]{2,1,0:T(8,128)(2,1)S(1)} %get-tuple-element.242), channel_id=1, source_target_pairs={{0,8},{1,9},{2,10},{3,11},{4,12},{5,13},{6,14},{7,15},{8,0},{9,1},... | collective-permute-start | bytes 491528 | tf_op jit(solution)/shard_map/ppermute | solution.py:772
  201.8 6.5 %collective-permute-start.28 = (bf16[1,352,128]{2,1,0:T(8,128)(2,1)S(1)}, bf16[1,352,128]{2,1,0:T(8,128)(2,1)S(1)}, u32[]{:S(2)}, u32[]{:S(2)}) collective-permute-start(bf16[1,352,128]{2,1,0:T(8,128)(2,1)S(1)} %get-tuple-element.186), channel_id=1, source_target_pairs={{0,8},{1,9},{2,10},{3,11},{4,12},{5,13},{6,14},{7,15},{8,0},{9,1},... | collective-permute-start | bytes 270344 | tf_op jit(solution)/shard_map/ppermute | solution.py:772
  202.6 6.5 %collective-permute-start.29 = (bf16[1,352,128]{2,1,0:T(8,128)(2,1)S(1)}, bf16[1,352,128]{2,1,0:T(8,128)(2,1)S(1)}, u32[]{:S(2)}, u32[]{:S(2)}) collective-permute-start(bf16[1,352,128]{2,1,0:T(8,128)(2,1)S(1)} %get-tuple-element.188), channel_id=1, source_target_pairs={{0,2},{1,3},{2,0},{3,1},{4,6},{5,7},{6,4},{7,5},{8,10},{9,11},{10,... | collective-permute-start | bytes 270344 | tf_op jit(solution)/shard_map/ppermute | solution.py:772
  204.9 7.4 %collective-permute-start.31 = (bf16[2,352,128]{2,1,0:T(8,128)(2,1)S(1)}, bf16[2,352,128]{2,1,0:T(8,128)(2,1)S(1)}, u32[]{:S(2)}, u32[]{:S(2)}) collective-permute-start(bf16[2,352,128]{2,1,0:T(8,128)(2,1)S(1)} %pad_maximum_fusion.12), channel_id=1, source_target_pairs={{0,4},{1,5},{2,6},{3,7},{4,0},{5,1},{6,2},{7,3},{8,12},{9,13},{10,... | collective-permute-start | bytes 540680 | tf_op jit(solution)/shard_map/ppermute | solution.py:772
  206.9 6.9 %collective-permute-start.33 = (bf16[2,352,128]{2,1,0:T(8,128)(2,1)S(1)}, bf16[2,352,128]{2,1,0:T(8,128)(2,1)S(1)}, u32[]{:S(2)}, u32[]{:S(2)}) collective-permute-start(bf16[2,352,128]{2,1,0:T(8,128)(2,1)S(1)} %pad_maximum_fusion.14), channel_id=1, source_target_pairs={{0,8},{1,9},{2,10},{3,11},{4,12},{5,13},{6,14},{7,15},{8,0},{9,1},... | collective-permute-start | bytes 540680 | tf_op jit(solution)/shard_map/ppermute | solution.py:772
  208.3 5.7 %collective-permute-start.35 = (bf16[2,352,128]{2,1,0:T(8,128)(2,1)S(1)}, bf16[2,352,128]{2,1,0:T(8,128)(2,1)S(1)}, u32[]{:S(2)}, u32[]{:S(2)}) collective-permute-start(bf16[2,352,128]{2,1,0:T(8,128)(2,1)S(1)} %pad_maximum_fusion.16), channel_id=1, source_target_pairs={{0,2},{1,3},{2,0},{3,1},{4,6},{5,7},{6,4},{7,5},{8,10},{9,11},{10,... | collective-permute-start | bytes 540680 | tf_op jit(solution)/shard_map/ppermute | solution.py:772
  218.9 10.3 %collective-permute-start.37 = (bf16[3,352,128]{2,1,0:T(8,128)(2,1)S(1)}, bf16[3,352,128]{2,1,0:T(8,128)(2,1)S(1)}, u32[]{:S(2)}, u32[]{:S(2)}) collective-permute-start(bf16[3,352,128]{2,1,0:T(8,128)(2,1)S(1)} %pad_maximum_fusion.9), channel_id=1, source_target_pairs={{0,16},{1,17},{2,18},{3,19},{4,20},{5,21},{6,22},{7,23},{8,24},{9,... | collective-permute-start | bytes 811016 | tf_op jit(solution)/shard_map/ppermute | solution.py:772
  230.3 13.8 %all-to-all-start.1 = ((bf16[32,8,512]{2,1,0:T(8,128)(2,1)}), bf16[32,8,512]{2,1,0:T(8,128)(2,1)S(1)}, u32[]{:S(2)}, u32[]{:S(2)}) async-start(bf16[32,8,512]{2,1,0:T(8,128)(2,1)} %get-tuple-element.197), calls=%async_computation.1 | async-start | bytes 524288 | tf_op jit(solution)/shard_map/all_to_all | solution.py:1031
  (43 other events, 437.3 us)
Sparse Core Ops, SparseCore 0:
  11.5 92.0 all-gather.1

commit v2 on v1

--- a/solution.py
+++ b/solution.py
@@ -304,7 +304,7 @@
     )(*operands)
 
 
-LIMITS = [18, 18, 18, 18, 18, 10, 18]
+LIMITS = [14, 18, 18, 18, 18, 10, 18]
 
 
 def megabytes(count):

time: 258 us -> 255 us (0.988)
  local copies, waits for them, and re-layouts: 24 us -> 21.3 us
    unnamed x81 -> x77, local copies, waits for them, and re-layouts: 17.5 us -> 14.8 us
  transfers between devices with their start and end apart: 40 -> 40, of which waited for: 22 -> 22; matrix products, arithmetic and copies ran while one was open for 7% -> 7% of each run, Pallas kernels for 19% -> 20%
where the time goes in v2:
time: 255 us; the launch traced here: 251 us
  Pallas kernels  80.6 us (32%)
  waiting for transfers between devices  74.3 us (29%)
  starting transfers between devices  44 us (17%)
  local copies, waits for them, and re-layouts  21.3 us (8%)
  between operations  16.1 us (6%)
  blocking collectives  11.7 us (5%)
  other arithmetic  3.28 us (1%)
    ppermute x38, waiting for transfers between devices, swap(): return lax.ppermute(value, 'dp', [(i, i ^ 1 << bit) for i in range(size)])  64.4 us
    ppermute x38, starting transfers between devices, swap(): return lax.ppermute(value, 'dp', [(i, i ^ 1 << bit) for i in range(size)])  40.8 us
    pallas_call x2, Pallas kernels, forward(): pl.pallas_call(lambda *refs: forward_kernel(save, packed, count, *refs),...  34.2 us
    unnamed x77, local copies, waits for them, and re-layouts  14.8 us
    pallas_call x1, Pallas kernels, layer_zero_mlp_back(): pl.pallas_call(lambda *refs: mlp_back_kernel(packed, *refs), in_specs=[wh...  13.2 us
    all_to_all x1, blocking collectives, local(): mean_sum = lax.all_to_all(sums, 'dp', 0, 0, tiled=True)  11.7 us
    all_to_all x1, waiting for transfers between devices, local(): arrived = lax.all_to_all(line, 'dp', 0, 0, tiled=True)  9.79 us
    pallas_call x1, Pallas kernels, layer_one_back(): pl.pallas_call(lambda *refs: class_back_kernel(packed, count, inverse_cou...  8.7 us
  transfers between devices with their start and end apart: 40, of which 22 were waited for; matrix products, arithmetic and copies ran while one was open for 7% of the time, Pallas kernels for 20%

profile of v2, /device:TPU:0, one launch (start us, length us, event | category | flops | bytes accessed | tf_op | source)
XLA Modules:
  0.0 251.2 jit_solution(13386990343912373164)
XLA Ops:
  7.2 2.0 pack_weights.1
  9.3 4.1 %collective-permute-start = (bf16[24,5504]{1,0:T(8,128)(2,1)}, bf16[24,5504]{1,0:T(8,128)(2,1)S(1)}, u32[]{:S(2)}, u32[]{:S(2)}) collective-permute-start(bf16[24,5504]{1,0:T(8,128)(2,1)} %get-tuple-element.125), channel_id=1, source_target_pairs={{0,16},{1,17},{2,18},{3,19},{4,20},{5,21},{6,22},{7,23},{8,24},{9,... | collective-permute-start | bytes 792584 | tf_op jit(solution)/shard_map/ppermute | solution.py:772
  14.3 1.6 constant_dynamic-update-slice_fusion.9
  17.8 7.8 %collective-permute-done = bf16[24,5504]{1,0:T(8,128)(2,1)S(1)} collective-permute-done((bf16[24,5504]{1,0:T(8,128)(2,1)}, bf16[24,5504]{1,0:T(8,128)(2,1)S(1)}, u32[]{:S(2)}, u32[]{:S(2)}) %collective-permute-start) | collective-permute-done | bytes 264224 | tf_op jit(solution)/shard_map/ppermute | solution.py:772
  25.7 1.6 collective-permute-start.4
  28.9 2.8 %collective-permute-start.7 = (bf16[2,24,1920]{2,1,0:T(8,128)(2,1)S(1)}, bf16[2,24,1920]{2,1,0:T(8,128)(2,1)S(1)}, u32[]{:S(2)}, u32[]{:S(2)}) collective-permute-start(bf16[2,24,1920]{2,1,0:T(8,128)(2,1)S(1)} %pad_maximum_fusion.10), channel_id=1, source_target_pairs={{0,8},{1,9},{2,10},{3,11},{4,12},{5,13},{6,14},{7,15},{8,0},{9,1},... | collective-permute-start | bytes 552968 | tf_op jit(solution)/shard_map/ppermute | solution.py:772
  32.5 2.4 collective-permute-start.5
  39.9 9.9 %collective-permute-done.5 = bf16[4,24,1792]{2,1,0:T(8,128)(2,1)S(1)} collective-permute-done((bf16[4,24,1792]{2,1,0:T(8,128)(2,1)S(1)}, bf16[4,24,1792]{2,1,0:T(8,128)(2,1)S(1)}, u32[]{:S(2)}, u32[]{:S(2)}) %collective-permute-start.5) | collective-permute-done | bytes 344096 | tf_op jit(solution)/shard_map/ppermute | solution.py:772
  50.8 5.6 %collective-permute-done.8 = bf16[4,24,1920]{2,1,0:T(8,128)(2,1)S(1)} collective-permute-done((bf16[4,24,1920]{2,1,0:T(8,128)(2,1)S(1)}, bf16[4,24,1920]{2,1,0:T(8,128)(2,1)S(1)}, u32[]{:S(2)}, u32[]{:S(2)}) %collective-permute-start.8) | collective-permute-done | bytes 368672 | tf_op jit(solution)/shard_map/ppermute | solution.py:772
  58.7 12.0 %collective-permute-done.6 = bf16[8,24,1792]{2,1,0:T(8,128)(2,1)S(1)} collective-permute-done((bf16[8,24,1792]{2,1,0:T(8,128)(2,1)S(1)}, bf16[8,24,1792]{2,1,0:T(8,128)(2,1)S(1)}, u32[]{:S(2)}, u32[]{:S(2)}) %collective-permute-start.6) | collective-permute-done | bytes 688160 | tf_op jit(solution)/shard_map/ppermute | solution.py:772
  75.1 1.9 copy.60.refs_0_
  78.9 2.2 collective-permute-done.10.refs_3_.refs_9_.refs_15_.refs_21_
  81.2 5.3 %unpack_weights.1 = (bf16[768,1152]{1,0:T(8,128)(2,1)S(1)}, bf16[768,384]{1,0:T(8,128)(2,1)S(1)}, bf16[768,1536]{1,0:T(8,128)(2,1)S(1)}, bf16[3072,384]{1,0:T(8,...) custom-call(s32[1]{0:T(128)} %bitcast.3.me.refs_12_.refs_5_.refs_9_, ...), custom_call_target="tpu_custom_call" | custom-call | flops 8999999488 | bytes 27000000 | tf_op jit(solution)/shard_map/unpack_weights/pallas_call | solution.py:716
  86.7 16.8 %teacher_forward.1.refs_1_ = f32[16,1024]{1,0:T(8,128)S(1)} custom-call(bf16[2,3,196,768]{3,2,1,0:T(8,128)(2,1)S(1)} %copy.60.refs_0_, f32[208,384]{1,0:T(8,128)S(1)} %get-tuple-element.285.refs_1_, f32[6,1,208]{2,1,0:T(1,128)S(1)} %copy.61.refs_2_, bf16[6,208,128]{2,1,0:T(8,128)(2,1)S(1)} %broadcast_in_dim.45.refs_3_, f32[8,384]{1,0:T(8,128)S(1)} %concatenate.94.refs_4_, ...), custom_call_target="tpu_custom_call" | custom-call | flops 30000001024 | bytes 90000000 | tf_op jit(solution)/shard_map/teacher_forward/pallas_call | solution.py:295
  103.9 3.4 %copy-done.3 = bf16[768,5504]{1,0:T(8,128)(2,1)S(1)} copy-done((bf16[768,5504]{1,0:T(8,128)(2,1)S(1)}, bf16[768,5504]{1,0:T(8,128)(2,1)}, u32[]{:S(2)}) %copy-start.3) | copy-done | bytes 8454168
  107.3 17.4 %student_forward.1 = (f32[1248,384]{1,0:T(8,128)S(1)}, f32[1248,384]{1,0:T(8,128)S(1)}, bf16[1248,1152]{1,0:T(8,128)(2,1)S(1)}, bf16[6,6,208,208]{3,2,1,0:T(8,12...) custom-call(bf16[2,3,196,768]{3,2,1,0:T(8,128)(2,1)S(1)} %copy-done,, ...), custom_call_target="tpu_custom_call" | custom-call | flops 30000001024 | bytes 90000000 | tf_op jit(solution)/shard_map/student_forward/pallas_call | solution.py:295
  126.3 11.7 %all_to_all.10.refs_2_ = bf16[32,16,128]{2,1,0:T(8,128)(2,1)S(1)} all-to-all(bf16[32,16,128]{2,1,0:T(8,128)(2,1)S(1)} %get-tuple-element.136), channel_id=1, replica_groups=mesh['dp'=32] {'dp'}, dimensions={0} | all-to-all | bytes 262144 | tf_op jit(solution)/shard_map/all_to_all | solution.py:1007
  137.9 8.7 %layer_one_back.1 = (f32[1248,384]{1,0:T(8,128)S(1)}, f32[8,384]{1,0:T(8,128)S(1)}, f32[8,128]{1,0:T(8,128)S(1)}, bf16[3,8,352,128]{3,2,1,0:T(8,128)(2,1)S(1)}, bf16[3,8,352,128]{3,2,1,0:T(8,128)(2,1)S(1)}) custom-call(f32[16,1024]{1,0:T(8,128)S(1)} %get-tuple-element.134.refs_0_, f32[16,1024]{1,0:T(8,128)S(1)} %teacher_forward.1.refs_1_, ...), custom_call_target="tpu_custom_call" | custom-call | flops 12999999488 | bytes 39000000 | tf_op jit(solution)/shard_map/layer_one_back/pallas_call | solution.py:470
  146.9 13.2 %layer_zero_mlp_back.1 = (f32[1248,384]{1,0:T(8,128)S(1)}, f32[8,384]{1,0:T(8,128)S(1)}, bf16[3,8,192,128]{3,2,1,0:T(8,128)(2,1)S(1)}, bf16[3,8,192,128]{3,2,1,0:T(8,128)(2,1)S(1)}) custom-call(f32[1248,384]{1,0:T(8,128)S(1)} %get-tuple-element.149.refs_0_, f32[1248,384]{1,0:T(8,128)S(1)} %get-tuple-element.150.refs_1_, ...), custom_call_target="tpu_custom_call" | custom-call | flops 12000000000 | bytes 36000000 | tf_op jit(solution)/shard_map/layer_zero_mlp_back/pallas_call | solution.py:522
  160.5 8.2 %layer_zero_attention_back.1 = (f32[384,384]{1,0:T(8,128)S(1)}, bf16[1248,1152]{1,0:T(8,128)(2,1)S(1)}) custom-call(f32[1248,384]{1,0:T(8,128)S(1)} %get-tuple-element.157.d_mid.refs_0_, bf16[1248,1152]{1,0:T(8,128)(2,1)S(1)} %copy-done.26, bf16[6,6,208,208]{3,2,1,0:T(8,128)(2,1)S(1)} %get-tuple-element.159.share, ...), custom_call_target="tpu_custom_call" | custom-call | flops 10000000000 | bytes 30000000 | tf_op jit(solution)/shard_map/layer_zero_attention_back/pallas_call | solution.py:574
  174.5 5.5 %layer_zero_input_back.1 = (bf16[3,8,160,128]{3,2,1,0:T(8,128)(2,1)S(1)}, bf16[3,8,160,128]{3,2,1,0:T(8,128)(2,1)S(1)}) custom-call(f32[1248,384]{1,0:T(8,128)S(1)} %get-tuple-element.157.d_mid.refs_0_, f32[1248,384]{1,0:T(8,128)S(1)} %get-tuple-element.168.refs_1_, bf16[1248,1152]{1,0:T(8,128)(2,1)S(1)} %get-tuple-element.169.refs_2_, ...), custom_call_target="tpu_custom_call" | custom-call | flops 6000000000 | bytes 18000000 | tf_op jit(solution)/shard_map/layer_zero_input_back/pallas_call | solution.py:620
  184.9 2.2 collective-permute-start.25
  188.2 1.8 collective-permute-done.27
  193.7 2.6 %collective-permute-done.19 = bf16[4,160,128]{2,1,0:T(8,128)(2,1)S(1)} collective-permute-done((bf16[4,160,128]{2,1,0:T(8,128)(2,1)S(1)}, bf16[4,160,128]{2,1,0:T(8,128)(2,1)S(1)}, u32[]{:S(2)}, u32[]{:S(2)}) %collective-permute-start.19) | collective-permute-done | bytes 163872 | tf_op jit(solution)/shard_map/ppermute | solution.py:772
  199.9 2.3 collective-permute-start.29
  202.2 2.0 collective-permute-start.31
  206.9 2.8 %collective-permute-done.31 = bf16[2,352,128]{2,1,0:T(8,128)(2,1)S(1)} collective-permute-done((bf16[2,352,128]{2,1,0:T(8,128)(2,1)S(1)}, bf16[2,352,128]{2,1,0:T(8,128)(2,1)S(1)}, u32[]{:S(2)}, u32[]{:S(2)}) %collective-permute-start.31) | collective-permute-done | bytes 180256 | tf_op jit(solution)/shard_map/ppermute | solution.py:772
  212.3 2.9 %collective-permute-done.32 = bf16[1,352,128]{2,1,0:T(8,128)(2,1)S(1)} collective-permute-done((bf16[1,352,128]{2,1,0:T(8,128)(2,1)S(1)}, bf16[1,352,128]{2,1,0:T(8,128)(2,1)S(1)}, u32[]{:S(2)}, u32[]{:S(2)}) %collective-permute-start.32) | collective-permute-done | bytes 90144 | tf_op jit(solution)/shard_map/ppermute | solution.py:772
  217.1 9.3 %collective-permute-done.37.refs_1_ = bf16[3,352,128]{2,1,0:T(8,128)(2,1)S(1)} collective-permute-done((bf16[3,352,128]{2,1,0:T(8,128)(2,1)S(1)}, bf16[3,352,128]{2,1,0:T(8,128)(2,1)S(1)}, u32[]{:S(2)}, u32[]{:S(2)}) %collective-permute-start.37) | collective-permute-done | bytes 270368 | tf_op jit(solution)/shard_map/ppermute | solution.py:772
  227.6 3.1 %all-to-all-start.1 = ((bf16[32,8,512]{2,1,0:T(8,128)(2,1)}), bf16[32,8,512]{2,1,0:T(8,128)(2,1)S(1)}, u32[]{:S(2)}, u32[]{:S(2)}) async-start(bf16[32,8,512]{2,1,0:T(8,128)(2,1)} %get-tuple-element.197), calls=%async_computation.1 | async-start | bytes 524288 | tf_op jit(solution)/shard_map/all_to_all | solution.py:1031
  231.6 9.8 %all-to-all-done.1.refs_2_ = bf16[32,8,512]{2,1,0:T(8,128)(2,1)S(1)} async-done(((bf16[32,8,512]{2,1,0:T(8,128)(2,1)}), bf16[32,8,512]{2,1,0:T(8,128)(2,1)S(1)}, u32[]{:S(2)}, u32[]{:S(2)}) %all-to-all-start.1) | async-done | bytes 262176 | tf_op jit(solution)/shard_map/all_to_all | solution.py:1031
  241.5 2.6 %update_rows.1 = (f32[24,1152]{1,0:T(8,128)}, f32[24,384]{1,0:T(8,128)}, f32[24,1536]{1,0:T(8,128)}, f32[96,384]{1,0:T(8,128)}, f32[24,384]{1,0:T(8,128)}, /*ind...) custom-call(f32[2]{0:T(128)S(1)} %pad_maximum_fusion.20.refs_0_, ...), custom_call_target="tpu_custom_call" | custom-call | flops 4000000000 | bytes 12000000 | tf_op jit(solution)/shard_map/update_rows/pallas_call | solution.py:897
  (240 shorter events, 49.3 us)
Async XLA Ops:
  7.2 96.4 %all-gather.2.cloned.1.call-start = ((), (), s32[]{:S(2)}) async-start(), calls=%async_computation.2 | async-start | bytes 8718336 | tf_op jit(solution)/shard_map/all_gather | solution.py:749
  9.3 16.3 %collective-permute-start = (bf16[24,5504]{1,0:T(8,128)(2,1)}, bf16[24,5504]{1,0:T(8,128)(2,1)S(1)}, u32[]{:S(2)}, u32[]{:S(2)}) collective-permute-start(bf16[24,5504]{1,0:T(8,128)(2,1)} %get-tuple-element.125), channel_id=1, source_target_pairs={{0,16},{1,17},{2,18},{3,19},{4,20},{5,21},{6,22},{7,23},{8,24},{9,... | collective-permute-start | bytes 792584 | tf_op jit(solution)/shard_map/ppermute | solution.py:772
  25.7 6.8 %collective-permute-start.4 = (bf16[2,24,1792]{2,1,0:T(8,128)(2,1)S(1)}, bf16[2,24,1792]{2,1,0:T(8,128)(2,1)S(1)}, u32[]{:S(2)}, u32[]{:S(2)}) collective-permute-start(bf16[2,24,1792]{2,1,0:T(8,128)(2,1)S(1)} %pad_maximum_fusion.18), channel_id=1, source_target_pairs={{0,4},{1,5},{2,6},{3,7},{4,0},{5,1},{6,2},{7,3},{8,12},{9,13},{10,... | collective-permute-start | bytes 516104 | tf_op jit(solution)/shard_map/ppermute | solution.py:772
  27.3 7.5 %collective-permute-start.1 = (bf16[2,24,1792]{2,1,0:T(8,128)(2,1)S(1)}, bf16[2,24,1792]{2,1,0:T(8,128)(2,1)S(1)}, u32[]{:S(2)}, u32[]{:S(2)}) collective-permute-start(bf16[2,24,1792]{2,1,0:T(8,128)(2,1)S(1)} %pad_maximum_fusion.17), channel_id=1, source_target_pairs={{0,2},{1,3},{2,0},{3,1},{4,6},{5,7},{6,4},{7,5},{8,10},{9,11},{10,... | collective-permute-start | bytes 516104 | tf_op jit(solution)/shard_map/ppermute | solution.py:772
  28.9 9.8 %collective-permute-start.7 = (bf16[2,24,1920]{2,1,0:T(8,128)(2,1)S(1)}, bf16[2,24,1920]{2,1,0:T(8,128)(2,1)S(1)}, u32[]{:S(2)}, u32[]{:S(2)}) collective-permute-start(bf16[2,24,1920]{2,1,0:T(8,128)(2,1)S(1)} %pad_maximum_fusion.10), channel_id=1, source_target_pairs={{0,8},{1,9},{2,10},{3,11},{4,12},{5,13},{6,14},{7,15},{8,0},{9,1},... | collective-permute-start | bytes 552968 | tf_op jit(solution)/shard_map/ppermute | solution.py:772
  32.5 17.3 %collective-permute-start.5 = (bf16[4,24,1792]{2,1,0:T(8,128)(2,1)S(1)}, bf16[4,24,1792]{2,1,0:T(8,128)(2,1)S(1)}, u32[]{:S(2)}, u32[]{:S(2)}) collective-permute-start(bf16[4,24,1792]{2,1,0:T(8,128)(2,1)S(1)} %pad_maximum_fusion.8), channel_id=1, source_target_pairs={{0,8},{1,9},{2,10},{3,11},{4,12},{5,13},{6,14},{7,15},{8,0},{9,1},... | collective-permute-start | bytes 1032200 | tf_op jit(solution)/shard_map/ppermute | solution.py:772
  34.9 15.7 %collective-permute-start.2 = (bf16[4,24,1792]{2,1,0:T(8,128)(2,1)S(1)}, bf16[4,24,1792]{2,1,0:T(8,128)(2,1)S(1)}, u32[]{:S(2)}, u32[]{:S(2)}) collective-permute-start(bf16[4,24,1792]{2,1,0:T(8,128)(2,1)S(1)} %pad_maximum_fusion.7), channel_id=1, source_target_pairs={{0,4},{1,5},{2,6},{3,7},{4,0},{5,1},{6,2},{7,3},{8,12},{9,13},{10,... | collective-permute-start | bytes 1032200 | tf_op jit(solution)/shard_map/ppermute | solution.py:772
  38.8 17.6 %collective-permute-start.8 = (bf16[4,24,1920]{2,1,0:T(8,128)(2,1)S(1)}, bf16[4,24,1920]{2,1,0:T(8,128)(2,1)S(1)}, u32[]{:S(2)}, u32[]{:S(2)}) collective-permute-start(bf16[4,24,1920]{2,1,0:T(8,128)(2,1)S(1)} %pad_maximum_fusion.6), channel_id=1, source_target_pairs={{0,2},{1,3},{2,0},{3,1},{4,6},{5,7},{6,4},{7,5},{8,10},{9,11},{10,... | collective-permute-start | bytes 1105928 | tf_op jit(solution)/shard_map/ppermute | solution.py:772
  49.9 20.8 %collective-permute-start.6 = (bf16[8,24,1792]{2,1,0:T(8,128)(2,1)S(1)}, bf16[8,24,1792]{2,1,0:T(8,128)(2,1)S(1)}, u32[]{:S(2)}, u32[]{:S(2)}) collective-permute-start(bf16[8,24,1792]{2,1,0:T(8,128)(2,1)S(1)} %pad_maximum_fusion.2), channel_id=1, source_target_pairs={{0,2},{1,3},{2,0},{3,1},{4,6},{5,7},{6,4},{7,5},{8,10},{9,11},{10,... | collective-permute-start | bytes 2064392 | tf_op jit(solution)/shard_map/ppermute | solution.py:772
  50.7 21.8 %collective-permute-start.3 = (bf16[8,24,1792]{2,1,0:T(8,128)(2,1)S(1)}, bf16[8,24,1792]{2,1,0:T(8,128)(2,1)S(1)}, u32[]{:S(2)}, u32[]{:S(2)}) collective-permute-start(bf16[8,24,1792]{2,1,0:T(8,128)(2,1)S(1)} %pad_maximum_fusion.1), channel_id=1, source_target_pairs={{0,8},{1,9},{2,10},{3,11},{4,12},{5,13},{6,14},{7,15},{8,0},{9,1},... | collective-permute-start | bytes 2064392 | tf_op jit(solution)/shard_map/ppermute | solution.py:772
  56.5 15.2 %collective-permute-start.9 = (bf16[8,24,1920]{2,1,0:T(8,128)(2,1)S(1)}, bf16[8,24,1920]{2,1,0:T(8,128)(2,1)S(1)}, u32[]{:S(2)}, u32[]{:S(2)}) collective-permute-start(bf16[8,24,1920]{2,1,0:T(8,128)(2,1)S(1)} %pad_maximum_fusion), channel_id=1, source_target_pairs={{0,4},{1,5},{2,6},{3,7},{4,0},{5,1},{6,2},{7,3},{8,12},{9,13},{10,... | collective-permute-start | bytes 2211848 | tf_op jit(solution)/shard_map/ppermute | solution.py:772
  71.6 7.3 %collective-permute-start.11 = (bf16[16,24,1792]{2,1,0:T(8,128)(2,1)}, bf16[16,24,1792]{2,1,0:T(8,128)(2,1)}, u32[]{:S(2)}, u32[]{:S(2)}) collective-permute-start(bf16[16,24,1792]{2,1,0:T(8,128)(2,1)} %constant_dynamic-update-slice_fusion.5.refs_1_.refs_7_.refs_13_.refs_19_), channel_id=1, source_target_pairs={{0,1},{1,0},{2,3},{3,2},{4,5},{5,4},{6,7},{7,6},{8,9},{9,8},{10,11... | collective-permute-start | bytes 4128776 | tf_op jit(solution)/shard_map/ppermute | solution.py:772
  71.8 9.4 %collective-permute-start.12 = (bf16[16,24,1920]{2,1,0:T(8,128)(2,1)S(1)}, bf16[16,24,1920]{2,1,0:T(8,128)(2,1)S(1)}, u32[]{:S(2)}, u32[]{:S(2)}) collective-permute-start(bf16[16,24,1920]{2,1,0:T(8,128)(2,1)S(1)} %constant_dynamic-update-slice_fusion.10.refs_2_.refs_8_.refs_14_.refs_20_), channel_id=1, source_target_pairs={{0,1},{1,0},{2,3},{3,2},{4,5},{5,4},{6,7},{7,6},{8,9},{9,8},{10,11... | collective-permute-start | bytes 4423688 | tf_op jit(solution)/shard_map/ppermute | solution.py:772
  73.4 7.8 %collective-permute-start.10 = (bf16[16,24,1792]{2,1,0:T(8,128)(2,1)}, bf16[16,24,1792]{2,1,0:T(8,128)(2,1)}, u32[]{:S(2)}, u32[]{:S(2)}) collective-permute-start(bf16[16,24,1792]{2,1,0:T(8,128)(2,1)} %constant_dynamic-update-slice_fusion.refs_0_.refs_6_.refs_12_.refs_18_), channel_id=1, source_target_pairs={{0,1},{1,0},{2,3},{3,2},{4,5},{5,4},{6,7},{7,6},{8,9},{9,8},{10,11... | collective-permute-start | bytes 4128776 | tf_op jit(solution)/shard_map/ppermute | solution.py:772
  146.6 22.0 %collective-permute-start.13 = (bf16[3,8,352,128]{3,2,1,0:T(8,128)(2,1)S(1)}, bf16[3,8,352,128]{3,2,1,0:T(8,128)(2,1)S(1)}, u32[]{:S(2)}, u32[]{:S(2)}) collective-permute-start(bf16[3,8,352,128]{3,2,1,0:T(8,128)(2,1)S(1)} %get-tuple-element.156), channel_id=1, source_target_pairs={{0,1},{1,0},{2,3},{3,2},{4,5},{5,4},{6,7},{7,6},{8,9},{9,8},{10,11... | collective-permute-start | bytes 6488072 | tf_op jit(solution)/shard_map/ppermute | solution.py:772
  160.1 11.5 %collective-permute-start.14 = (bf16[3,8,192,128]{3,2,1,0:T(8,128)(2,1)S(1)}, bf16[3,8,192,128]{3,2,1,0:T(8,128)(2,1)S(1)}, u32[]{:S(2)}, u32[]{:S(2)}) collective-permute-start(bf16[3,8,192,128]{3,2,1,0:T(8,128)(2,1)S(1)} %get-tuple-element.164), channel_id=1, source_target_pairs={{0,1},{1,0},{2,3},{3,2},{4,5},{5,4},{6,7},{7,6},{8,9},{9,8},{10,11... | collective-permute-start | bytes 3538952 | tf_op jit(solution)/shard_map/ppermute | solution.py:772
  169.4 11.3 %collective-permute-start.16 = (bf16[4,352,128]{2,1,0:T(8,128)(2,1)S(1)}, bf16[4,352,128]{2,1,0:T(8,128)(2,1)S(1)}, u32[]{:S(2)}, u32[]{:S(2)}) collective-permute-start(bf16[4,352,128]{2,1,0:T(8,128)(2,1)S(1)} %get-tuple-element.228), channel_id=1, source_target_pairs={{0,4},{1,5},{2,6},{3,7},{4,0},{5,1},{6,2},{7,3},{8,12},{9,13},{10,... | collective-permute-start | bytes 1081352 | tf_op jit(solution)/shard_map/ppermute | solution.py:772
  170.1 11.6 %collective-permute-start.17 = (bf16[4,352,128]{2,1,0:T(8,128)(2,1)S(1)}, bf16[4,352,128]{2,1,0:T(8,128)(2,1)S(1)}, u32[]{:S(2)}, u32[]{:S(2)}) collective-permute-start(bf16[4,352,128]{2,1,0:T(8,128)(2,1)S(1)} %get-tuple-element.227), channel_id=1, source_target_pairs={{0,8},{1,9},{2,10},{3,11},{4,12},{5,13},{6,14},{7,15},{8,0},{9,1},... | collective-permute-start | bytes 1081352 | tf_op jit(solution)/shard_map/ppermute | solution.py:772
  170.8 11.2 %collective-permute-start.15 = (bf16[4,352,128]{2,1,0:T(8,128)(2,1)S(1)}, bf16[4,352,128]{2,1,0:T(8,128)(2,1)S(1)}, u32[]{:S(2)}, u32[]{:S(2)}) collective-permute-start(bf16[4,352,128]{2,1,0:T(8,128)(2,1)S(1)} %get-tuple-element.229), channel_id=1, source_target_pairs={{0,2},{1,3},{2,0},{3,1},{4,6},{5,7},{6,4},{7,5},{8,10},{9,11},{10,... | collective-permute-start | bytes 1081352 | tf_op jit(solution)/shard_map/ppermute | solution.py:772
  172.1 12.8 %collective-permute-start.24 = (bf16[4,192,128]{2,1,0:T(8,128)(2,1)S(1)}, bf16[4,192,128]{2,1,0:T(8,128)(2,1)S(1)}, u32[]{:S(2)}, u32[]{:S(2)}) collective-permute-start(bf16[4,192,128]{2,1,0:T(8,128)(2,1)S(1)} %get-tuple-element.233), channel_id=1, source_target_pairs={{0,8},{1,9},{2,10},{3,11},{4,12},{5,13},{6,14},{7,15},{8,0},{9,1},... | collective-permute-start | bytes 589832 | tf_op jit(solution)/shard_map/ppermute | solution.py:772
  173.5 13.6 %collective-permute-start.22 = (bf16[4,192,128]{2,1,0:T(8,128)(2,1)S(1)}, bf16[4,192,128]{2,1,0:T(8,128)(2,1)S(1)}, u32[]{:S(2)}, u32[]{:S(2)}) collective-permute-start(bf16[4,192,128]{2,1,0:T(8,128)(2,1)S(1)} %get-tuple-element.234), channel_id=1, source_target_pairs={{0,4},{1,5},{2,6},{3,7},{4,0},{5,1},{6,2},{7,3},{8,12},{9,13},{10,... | collective-permute-start | bytes 589832 | tf_op jit(solution)/shard_map/ppermute | solution.py:772
  180.7 7.4 %collective-permute-start.20 = (bf16[4,192,128]{2,1,0:T(8,128)(2,1)S(1)}, bf16[4,192,128]{2,1,0:T(8,128)(2,1)S(1)}, u32[]{:S(2)}, u32[]{:S(2)}) collective-permute-start(bf16[4,192,128]{2,1,0:T(8,128)(2,1)S(1)} %get-tuple-element.235), channel_id=1, source_target_pairs={{0,2},{1,3},{2,0},{3,1},{4,6},{5,7},{6,4},{7,5},{8,10},{9,11},{10,... | collective-permute-start | bytes 589832 | tf_op jit(solution)/shard_map/ppermute | solution.py:772
  182.1 7.9 %collective-permute-start.27 = (bf16[2,352,128]{2,1,0:T(8,128)(2,1)S(1)}, bf16[2,352,128]{2,1,0:T(8,128)(2,1)S(1)}, u32[]{:S(2)}, u32[]{:S(2)}) collective-permute-start(bf16[2,352,128]{2,1,0:T(8,128)(2,1)S(1)} %get-tuple-element.245), channel_id=1, source_target_pairs={{0,2},{1,3},{2,0},{3,1},{4,6},{5,7},{6,4},{7,5},{8,10},{9,11},{10,... | collective-permute-start | bytes 540680 | tf_op jit(solution)/shard_map/ppermute | solution.py:772
  183.3 6.9 %collective-permute-start.26 = (bf16[2,352,128]{2,1,0:T(8,128)(2,1)S(1)}, bf16[2,352,128]{2,1,0:T(8,128)(2,1)S(1)}, u32[]{:S(2)}, u32[]{:S(2)}) collective-permute-start(bf16[2,352,128]{2,1,0:T(8,128)(2,1)S(1)} %get-tuple-element.247), channel_id=1, source_target_pairs={{0,8},{1,9},{2,10},{3,11},{4,12},{5,13},{6,14},{7,15},{8,0},{9,1},... | collective-permute-start | bytes 540680 | tf_op jit(solution)/shard_map/ppermute | solution.py:772
  193.0 5.7 %collective-permute-start.23 = (bf16[4,160,128]{2,1,0:T(8,128)(2,1)S(1)}, bf16[4,160,128]{2,1,0:T(8,128)(2,1)S(1)}, u32[]{:S(2)}, u32[]{:S(2)}) collective-permute-start(bf16[4,160,128]{2,1,0:T(8,128)(2,1)S(1)} %get-tuple-element.242), channel_id=1, source_target_pairs={{0,8},{1,9},{2,10},{3,11},{4,12},{5,13},{6,14},{7,15},{8,0},{9,1},... | collective-permute-start | bytes 491528 | tf_op jit(solution)/shard_map/ppermute | solution.py:772
  199.1 6.5 %collective-permute-start.28 = (bf16[1,352,128]{2,1,0:T(8,128)(2,1)S(1)}, bf16[1,352,128]{2,1,0:T(8,128)(2,1)S(1)}, u32[]{:S(2)}, u32[]{:S(2)}) collective-permute-start(bf16[1,352,128]{2,1,0:T(8,128)(2,1)S(1)} %get-tuple-element.186), channel_id=1, source_target_pairs={{0,8},{1,9},{2,10},{3,11},{4,12},{5,13},{6,14},{7,15},{8,0},{9,1},... | collective-permute-start | bytes 270344 | tf_op jit(solution)/shard_map/ppermute | solution.py:772
  199.9 6.5 %collective-permute-start.29 = (bf16[1,352,128]{2,1,0:T(8,128)(2,1)S(1)}, bf16[1,352,128]{2,1,0:T(8,128)(2,1)S(1)}, u32[]{:S(2)}, u32[]{:S(2)}) collective-permute-start(bf16[1,352,128]{2,1,0:T(8,128)(2,1)S(1)} %get-tuple-element.188), channel_id=1, source_target_pairs={{0,2},{1,3},{2,0},{3,1},{4,6},{5,7},{6,4},{7,5},{8,10},{9,11},{10,... | collective-permute-start | bytes 270344 | tf_op jit(solution)/shard_map/ppermute | solution.py:772
  202.2 7.4 %collective-permute-start.31 = (bf16[2,352,128]{2,1,0:T(8,128)(2,1)S(1)}, bf16[2,352,128]{2,1,0:T(8,128)(2,1)S(1)}, u32[]{:S(2)}, u32[]{:S(2)}) collective-permute-start(bf16[2,352,128]{2,1,0:T(8,128)(2,1)S(1)} %pad_maximum_fusion.12), channel_id=1, source_target_pairs={{0,4},{1,5},{2,6},{3,7},{4,0},{5,1},{6,2},{7,3},{8,12},{9,13},{10,... | collective-permute-start | bytes 540680 | tf_op jit(solution)/shard_map/ppermute | solution.py:772
  204.3 6.9 %collective-permute-start.33 = (bf16[2,352,128]{2,1,0:T(8,128)(2,1)S(1)}, bf16[2,352,128]{2,1,0:T(8,128)(2,1)S(1)}, u32[]{:S(2)}, u32[]{:S(2)}) collective-permute-start(bf16[2,352,128]{2,1,0:T(8,128)(2,1)S(1)} %pad_maximum_fusion.14), channel_id=1, source_target_pairs={{0,8},{1,9},{2,10},{3,11},{4,12},{5,13},{6,14},{7,15},{8,0},{9,1},... | collective-permute-start | bytes 540680 | tf_op jit(solution)/shard_map/ppermute | solution.py:772
  205.6 5.7 %collective-permute-start.35 = (bf16[2,352,128]{2,1,0:T(8,128)(2,1)S(1)}, bf16[2,352,128]{2,1,0:T(8,128)(2,1)S(1)}, u32[]{:S(2)}, u32[]{:S(2)}) collective-permute-start(bf16[2,352,128]{2,1,0:T(8,128)(2,1)S(1)} %pad_maximum_fusion.16), channel_id=1, source_target_pairs={{0,2},{1,3},{2,0},{3,1},{4,6},{5,7},{6,4},{7,5},{8,10},{9,11},{10,... | collective-permute-start | bytes 540680 | tf_op jit(solution)/shard_map/ppermute | solution.py:772
  216.2 10.3 %collective-permute-start.37 = (bf16[3,352,128]{2,1,0:T(8,128)(2,1)S(1)}, bf16[3,352,128]{2,1,0:T(8,128)(2,1)S(1)}, u32[]{:S(2)}, u32[]{:S(2)}) collective-permute-start(bf16[3,352,128]{2,1,0:T(8,128)(2,1)S(1)} %pad_maximum_fusion.9), channel_id=1, source_target_pairs={{0,16},{1,17},{2,18},{3,19},{4,20},{5,21},{6,22},{7,23},{8,24},{9,... | collective-permute-start | bytes 811016 | tf_op jit(solution)/shard_map/ppermute | solution.py:772
  227.6 13.8 %all-to-all-start.1 = ((bf16[32,8,512]{2,1,0:T(8,128)(2,1)}), bf16[32,8,512]{2,1,0:T(8,128)(2,1)S(1)}, u32[]{:S(2)}, u32[]{:S(2)}) async-start(bf16[32,8,512]{2,1,0:T(8,128)(2,1)} %get-tuple-element.197), calls=%async_computation.1 | async-start | bytes 524288 | tf_op jit(solution)/shard_map/all_to_all | solution.py:1031
  (41 other events, 432.0 us)
Sparse Core Ops, SparseCore 0:
  11.5 92.0 all-gather.1

commit v3 on v2

--- a/solution.py
+++ b/solution.py
@@ -1016,10 +1016,10 @@
         mlp, dmix = core_stage(*mlp, dmix)
     rest = layer_zero_input_back(d_mid, state0, dmix, anchor_patches, out0, student, gains0, gain_two, gain_one, me)
     if student["fast"]:
-        one, rest = axis_stage(2, one, rest)
-        mlp, rest = axis_stage(1, halves(mlp), rest)
-        rest = axis_stage(1, halves(core_stage(*rest)))
-        zero = [tuple(jnp.concatenate([c[:, :96], b, c[:, 96:]], 1) for b, c in zip(bs, cs)) for bs, cs in zip(mlp, rest)]
+        rest = core_stage(*rest)
+        zero = halves(jnp.concatenate([rest[:, :, :96], mlp, rest[:, :, 96:]], 2))
+        zero, one = lax.optimization_barrier((zero, one))
+        zero, one = axis_stage(1, zero), axis_stage(2, one)
         zero, one = lax.optimization_barrier((zero, one))
         keep, got = last_stage(axis_stage(3, one), axis_stage(3, axis_stage(2, zero)), me)
         slopes, line = collect(keep, got, report, n, attention_in.shape[0])

time: 255 us -> 253 us (level)
  starting transfers between devices: 44 us -> 38.3 us
  waiting for transfers between devices: 74.3 us -> 77.5 us
    ppermute x38 -> x35, starting transfers between devices: 40.8 us -> 35.5 us  [swap(): return lax.ppermute(value, 'dp', [(i, i ^ 1 << bit) for i in range(size)])]
    ppermute x38 -> x35, waiting for transfers between devices: 64.4 us -> 67.6 us  [swap(): return lax.ppermute(value, 'dp', [(i, i ^ 1 << bit) for i in range(size)])]
    unnamed x77 -> x81, local copies, waits for them, and re-layouts: 14.8 us -> 15.1 us
  transfers between devices with their start and end apart: 40 -> 37, of which waited for: 22 -> 25; matrix products, arithmetic and copies ran while one was open for 7% -> 7% of each run, Pallas kernels for 20% -> 20%
where the time goes in v3:
time: 253 us; the launch traced here: 249 us
  Pallas kernels  80.6 us (32%)
  waiting for transfers between devices  77.5 us (31%)
  starting transfers between devices  38.3 us (15%)
  local copies, waits for them, and re-layouts  21.7 us (9%)
  between operations  16 us (6%)
  blocking collectives  11.6 us (5%)
  other arithmetic  3.35 us (1%)
    ppermute x35, waiting for transfers between devices, swap(): return lax.ppermute(value, 'dp', [(i, i ^ 1 << bit) for i in range(size)])  67.6 us
    ppermute x35, starting transfers between devices, swap(): return lax.ppermute(value, 'dp', [(i, i ^ 1 << bit) for i in range(size)])  35.5 us
    pallas_call x2, Pallas kernels, forward(): pl.pallas_call(lambda *refs: forward_kernel(save, packed, count, *refs),...  34.3 us
    unnamed x81, local copies, waits for them, and re-layouts  15.1 us
    pallas_call x1, Pallas kernels, layer_zero_mlp_back(): pl.pallas_call(lambda *refs: mlp_back_kernel(packed, *refs), in_specs=[wh...  13.1 us
    all_to_all x1, blocking collectives, local(): mean_sum = lax.all_to_all(sums, 'dp', 0, 0, tiled=True)  11.6 us
    all_to_all x1, waiting for transfers between devices, local(): arrived = lax.all_to_all(line, 'dp', 0, 0, tiled=True)  9.79 us
    pallas_call x1, Pallas kernels, layer_one_back(): pl.pallas_call(lambda *refs: class_back_kernel(packed, count, inverse_cou...  8.68 us
  transfers between devices with their start and end apart: 37, of which 25 were waited for; matrix products, arithmetic and copies ran while one was open for 7% of the time, Pallas kernels for 20%

profile of v3, /device:TPU:0, one launch (start us, length us, event | category | flops | bytes accessed | tf_op | source)
XLA Modules:
  0.0 249.0 jit_solution(10841185096932853867)
XLA Ops:
  7.2 2.0 pack_weights.1
  9.3 4.1 %collective-permute-start = (bf16[24,5504]{1,0:T(8,128)(2,1)}, bf16[24,5504]{1,0:T(8,128)(2,1)S(1)}, u32[]{:S(2)}, u32[]{:S(2)}) collective-permute-start(bf16[24,5504]{1,0:T(8,128)(2,1)} %get-tuple-element.127), channel_id=1, source_target_pairs={{0,16},{1,17},{2,18},{3,19},{4,20},{5,21},{6,22},{7,23},{8,24},{9,... | collective-permute-start | bytes 792584 | tf_op jit(solution)/shard_map/ppermute | solution.py:772
  14.3 1.6 constant_dynamic-update-slice_fusion.9
  17.8 7.8 %collective-permute-done = bf16[24,5504]{1,0:T(8,128)(2,1)S(1)} collective-permute-done((bf16[24,5504]{1,0:T(8,128)(2,1)}, bf16[24,5504]{1,0:T(8,128)(2,1)S(1)}, u32[]{:S(2)}, u32[]{:S(2)}) %collective-permute-start) | collective-permute-done | bytes 264224 | tf_op jit(solution)/shard_map/ppermute | solution.py:772
  25.7 1.6 collective-permute-start.4
  27.3 1.6 collective-permute-start.1
  28.9 2.8 %collective-permute-start.7 = (bf16[2,24,1920]{2,1,0:T(8,128)(2,1)S(1)}, bf16[2,24,1920]{2,1,0:T(8,128)(2,1)S(1)}, u32[]{:S(2)}, u32[]{:S(2)}) collective-permute-start(bf16[2,24,1920]{2,1,0:T(8,128)(2,1)S(1)} %pad_maximum_fusion.11), channel_id=1, source_target_pairs={{0,8},{1,9},{2,10},{3,11},{4,12},{5,13},{6,14},{7,15},{8,0},{9,1},... | collective-permute-start | bytes 552968 | tf_op jit(solution)/shard_map/ppermute | solution.py:772
  32.5 2.4 collective-permute-start.5
  39.9 9.9 %collective-permute-done.5 = bf16[4,24,1792]{2,1,0:T(8,128)(2,1)S(1)} collective-permute-done((bf16[4,24,1792]{2,1,0:T(8,128)(2,1)S(1)}, bf16[4,24,1792]{2,1,0:T(8,128)(2,1)S(1)}, u32[]{:S(2)}, u32[]{:S(2)}) %collective-permute-start.5) | collective-permute-done | bytes 344096 | tf_op jit(solution)/shard_map/ppermute | solution.py:772
  50.8 5.6 %collective-permute-done.8 = bf16[4,24,1920]{2,1,0:T(8,128)(2,1)S(1)} collective-permute-done((bf16[4,24,1920]{2,1,0:T(8,128)(2,1)S(1)}, bf16[4,24,1920]{2,1,0:T(8,128)(2,1)S(1)}, u32[]{:S(2)}, u32[]{:S(2)}) %collective-permute-start.8) | collective-permute-done | bytes 368672 | tf_op jit(solution)/shard_map/ppermute | solution.py:772
  58.7 12.0 %collective-permute-done.6 = bf16[8,24,1792]{2,1,0:T(8,128)(2,1)S(1)} collective-permute-done((bf16[8,24,1792]{2,1,0:T(8,128)(2,1)S(1)}, bf16[8,24,1792]{2,1,0:T(8,128)(2,1)S(1)}, u32[]{:S(2)}, u32[]{:S(2)}) %collective-permute-start.6) | collective-permute-done | bytes 688160 | tf_op jit(solution)/shard_map/ppermute | solution.py:772
  75.1 1.9 copy.60.refs_0_
  78.9 2.2 collective-permute-done.10.refs_3_.refs_9_.refs_15_.refs_21_
  81.2 5.3 %unpack_weights.1 = (bf16[768,1152]{1,0:T(8,128)(2,1)S(1)}, bf16[768,384]{1,0:T(8,128)(2,1)S(1)}, bf16[768,1536]{1,0:T(8,128)(2,1)S(1)}, bf16[3072,384]{1,0:T(8,...) custom-call(s32[1]{0:T(128)} %bitcast.3.me.refs_12_.refs_5_.refs_9_, ...), custom_call_target="tpu_custom_call" | custom-call | flops 8999999488 | bytes 27000000 | tf_op jit(solution)/shard_map/unpack_weights/pallas_call | solution.py:716
  86.7 16.8 %teacher_forward.1.refs_1_ = f32[16,1024]{1,0:T(8,128)S(1)} custom-call(bf16[2,3,196,768]{3,2,1,0:T(8,128)(2,1)S(1)} %copy.60.refs_0_, f32[208,384]{1,0:T(8,128)S(1)} %get-tuple-element.271.refs_1_, f32[6,1,208]{2,1,0:T(1,128)S(1)} %copy.61.refs_2_, bf16[6,208,128]{2,1,0:T(8,128)(2,1)S(1)} %broadcast_in_dim.45.refs_3_, f32[8,384]{1,0:T(8,128)S(1)} %concatenate.79.refs_4_, ...), custom_call_target="tpu_custom_call" | custom-call | flops 30000001024 | bytes 90000000 | tf_op jit(solution)/shard_map/teacher_forward/pallas_call | solution.py:295
  103.9 3.4 %copy-done.3 = bf16[768,5504]{1,0:T(8,128)(2,1)S(1)} copy-done((bf16[768,5504]{1,0:T(8,128)(2,1)S(1)}, bf16[768,5504]{1,0:T(8,128)(2,1)}, u32[]{:S(2)}) %copy-start.3) | copy-done | bytes 8454168
  107.3 17.4 %student_forward.1 = (f32[1248,384]{1,0:T(8,128)S(1)}, f32[1248,384]{1,0:T(8,128)S(1)}, bf16[1248,1152]{1,0:T(8,128)(2,1)S(1)}, bf16[6,6,208,208]{3,2,1,0:T(8,12...) custom-call(bf16[2,3,196,768]{3,2,1,0:T(8,128)(2,1)S(1)} %copy-done,, ...), custom_call_target="tpu_custom_call" | custom-call | flops 30000001024 | bytes 90000000 | tf_op jit(solution)/shard_map/student_forward/pallas_call | solution.py:295
  124.7 2.0 copy-done.25
  126.7 11.6 %all_to_all.10.refs_2_ = bf16[32,16,128]{2,1,0:T(8,128)(2,1)S(1)} all-to-all(bf16[32,16,128]{2,1,0:T(8,128)(2,1)S(1)} %get-tuple-element.138), channel_id=1, replica_groups=mesh['dp'=32] {'dp'}, dimensions={0} | all-to-all | bytes 262144 | tf_op jit(solution)/shard_map/all_to_all | solution.py:1007
  138.3 8.7 %layer_one_back.1 = (f32[1248,384]{1,0:T(8,128)S(1)}, f32[8,384]{1,0:T(8,128)S(1)}, f32[8,128]{1,0:T(8,128)S(1)}, bf16[3,8,352,128]{3,2,1,0:T(8,128)(2,1)S(1)}, bf16[3,8,352,128]{3,2,1,0:T(8,128)(2,1)S(1)}) custom-call(f32[16,1024]{1,0:T(8,128)S(1)} %get-tuple-element.136.refs_0_, f32[16,1024]{1,0:T(8,128)S(1)} %teacher_forward.1.refs_1_, ...), custom_call_target="tpu_custom_call" | custom-call | flops 12999999488 | bytes 39000000 | tf_op jit(solution)/shard_map/layer_one_back/pallas_call | solution.py:470
  147.3 13.1 %layer_zero_mlp_back.1 = (f32[1248,384]{1,0:T(8,128)S(1)}, f32[8,384]{1,0:T(8,128)S(1)}, bf16[3,8,192,128]{3,2,1,0:T(8,128)(2,1)S(1)}, bf16[3,8,192,128]{3,2,1,0:T(8,128)(2,1)S(1)}) custom-call(f32[1248,384]{1,0:T(8,128)S(1)} %get-tuple-element.152.refs_0_, f32[1248,384]{1,0:T(8,128)S(1)} %get-tuple-element.153.refs_1_, ...), custom_call_target="tpu_custom_call" | custom-call | flops 12000000000 | bytes 36000000 | tf_op jit(solution)/shard_map/layer_zero_mlp_back/pallas_call | solution.py:522
  160.8 8.2 %layer_zero_attention_back.1 = (f32[384,384]{1,0:T(8,128)S(1)}, bf16[1248,1152]{1,0:T(8,128)(2,1)S(1)}) custom-call(f32[1248,384]{1,0:T(8,128)S(1)} %get-tuple-element.156.d_mid.refs_0_, bf16[1248,1152]{1,0:T(8,128)(2,1)S(1)} %get-tuple-element.161.mix, bf16[6,6,208,208]{3,2,1,0:T(8,128)(2,1)S(1)} %copy-done.26, bf16[1248,384]{1,0:T(8,128)(2,1)S(1)} %copy-done.28, ...), custom_call_target="tpu_custom_call" | custom-call | flops 10000000000 | bytes 30000000 | tf_op jit(solution)/shard_map/layer_zero_attention_back/pallas_call | solution.py:574
  171.9 5.6 %layer_zero_input_back.1 = (bf16[3,8,160,128]{3,2,1,0:T(8,128)(2,1)S(1)}, bf16[3,8,160,128]{3,2,1,0:T(8,128)(2,1)S(1)}) custom-call(f32[1248,384]{1,0:T(8,128)S(1)} %get-tuple-element.156.d_mid.refs_0_, f32[1248,384]{1,0:T(8,128)S(1)} %get-tuple-element.157.refs_1_, bf16[1248,1152]{1,0:T(8,128)(2,1)S(1)} %get-tuple-element.166.refs_2_, ...), custom_call_target="tpu_custom_call" | custom-call | flops 6000000000 | bytes 18000000 | tf_op jit(solution)/shard_map/layer_zero_input_back/pallas_call | solution.py:620
  178.0 2.3 collective-permute-done.17
  191.5 4.6 %collective-permute-done.21 = bf16[4,352,128]{2,1,0:T(8,128)(2,1)S(1)} collective-permute-done((bf16[4,352,128]{2,1,0:T(8,128)(2,1)S(1)}, bf16[4,352,128]{2,1,0:T(8,128)(2,1)S(1)}, u32[]{:S(2)}, u32[]{:S(2)}) %collective-permute-start.21) | collective-permute-done | bytes 360480 | tf_op jit(solution)/shard_map/ppermute | solution.py:772
  199.4 1.7 collective-permute-start.27
  204.0 2.6 %collective-permute-done.28 = bf16[2,352,128]{2,1,0:T(8,128)(2,1)S(1)} collective-permute-done((bf16[2,352,128]{2,1,0:T(8,128)(2,1)S(1)}, bf16[2,352,128]{2,1,0:T(8,128)(2,1)S(1)}, u32[]{:S(2)}, u32[]{:S(2)}) %collective-permute-start.28) | collective-permute-done | bytes 180256 | tf_op jit(solution)/shard_map/ppermute | solution.py:772
  212.6 1.7 collective-permute-done.33
  215.3 9.4 %collective-permute-done.34.refs_1_ = bf16[3,352,128]{2,1,0:T(8,128)(2,1)S(1)} collective-permute-done((bf16[3,352,128]{2,1,0:T(8,128)(2,1)S(1)}, bf16[3,352,128]{2,1,0:T(8,128)(2,1)S(1)}, u32[]{:S(2)}, u32[]{:S(2)}) %collective-permute-start.34) | collective-permute-done | bytes 270368 | tf_op jit(solution)/shard_map/ppermute | solution.py:772
  225.9 2.8 %all-to-all-start.1 = ((bf16[32,8,512]{2,1,0:T(8,128)(2,1)}), bf16[32,8,512]{2,1,0:T(8,128)(2,1)S(1)}, u32[]{:S(2)}, u32[]{:S(2)}) async-start(bf16[32,8,512]{2,1,0:T(8,128)(2,1)} %get-tuple-element.201), calls=%async_computation.1 | async-start | bytes 524288 | tf_op jit(solution)/shard_map/all_to_all | solution.py:1031
  229.4 9.8 %all-to-all-done.1.refs_2_ = bf16[32,8,512]{2,1,0:T(8,128)(2,1)S(1)} async-done(((bf16[32,8,512]{2,1,0:T(8,128)(2,1)}), bf16[32,8,512]{2,1,0:T(8,128)(2,1)S(1)}, u32[]{:S(2)}, u32[]{:S(2)}) %all-to-all-start.1) | async-done | bytes 262176 | tf_op jit(solution)/shard_map/all_to_all | solution.py:1031
  239.4 2.6 %update_rows.1 = (f32[24,1152]{1,0:T(8,128)}, f32[24,384]{1,0:T(8,128)}, f32[24,1536]{1,0:T(8,128)}, f32[96,384]{1,0:T(8,128)}, f32[24,384]{1,0:T(8,128)}, /*ind...) custom-call(f32[2]{0:T(128)S(1)} %pad_maximum_fusion.15.refs_0_, ...), custom_call_target="tpu_custom_call" | custom-call | flops 4000000000 | bytes 12000000 | tf_op jit(solution)/shard_map/update_rows/pallas_call | solution.py:897
  (227 shorter events, 47.9 us)
Async XLA Ops:
  7.2 96.4 %all-gather.2.cloned.1.call-start = ((), (), s32[]{:S(2)}) async-start(), calls=%async_computation.2 | async-start | bytes 8718336 | tf_op jit(solution)/shard_map/all_gather | solution.py:749
  9.3 16.3 %collective-permute-start = (bf16[24,5504]{1,0:T(8,128)(2,1)}, bf16[24,5504]{1,0:T(8,128)(2,1)S(1)}, u32[]{:S(2)}, u32[]{:S(2)}) collective-permute-start(bf16[24,5504]{1,0:T(8,128)(2,1)} %get-tuple-element.127), channel_id=1, source_target_pairs={{0,16},{1,17},{2,18},{3,19},{4,20},{5,21},{6,22},{7,23},{8,24},{9,... | collective-permute-start | bytes 792584 | tf_op jit(solution)/shard_map/ppermute | solution.py:772
  25.7 6.8 %collective-permute-start.4 = (bf16[2,24,1792]{2,1,0:T(8,128)(2,1)S(1)}, bf16[2,24,1792]{2,1,0:T(8,128)(2,1)S(1)}, u32[]{:S(2)}, u32[]{:S(2)}) collective-permute-start(bf16[2,24,1792]{2,1,0:T(8,128)(2,1)S(1)} %pad_maximum_fusion.13), channel_id=1, source_target_pairs={{0,4},{1,5},{2,6},{3,7},{4,0},{5,1},{6,2},{7,3},{8,12},{9,13},{10,... | collective-permute-start | bytes 516104 | tf_op jit(solution)/shard_map/ppermute | solution.py:772
  27.3 7.5 %collective-permute-start.1 = (bf16[2,24,1792]{2,1,0:T(8,128)(2,1)S(1)}, bf16[2,24,1792]{2,1,0:T(8,128)(2,1)S(1)}, u32[]{:S(2)}, u32[]{:S(2)}) collective-permute-start(bf16[2,24,1792]{2,1,0:T(8,128)(2,1)S(1)} %pad_maximum_fusion.12), channel_id=1, source_target_pairs={{0,2},{1,3},{2,0},{3,1},{4,6},{5,7},{6,4},{7,5},{8,10},{9,11},{10,... | collective-permute-start | bytes 516104 | tf_op jit(solution)/shard_map/ppermute | solution.py:772
  28.9 9.8 %collective-permute-start.7 = (bf16[2,24,1920]{2,1,0:T(8,128)(2,1)S(1)}, bf16[2,24,1920]{2,1,0:T(8,128)(2,1)S(1)}, u32[]{:S(2)}, u32[]{:S(2)}) collective-permute-start(bf16[2,24,1920]{2,1,0:T(8,128)(2,1)S(1)} %pad_maximum_fusion.11), channel_id=1, source_target_pairs={{0,8},{1,9},{2,10},{3,11},{4,12},{5,13},{6,14},{7,15},{8,0},{9,1},... | collective-permute-start | bytes 552968 | tf_op jit(solution)/shard_map/ppermute | solution.py:772
  32.5 17.4 %collective-permute-start.5 = (bf16[4,24,1792]{2,1,0:T(8,128)(2,1)S(1)}, bf16[4,24,1792]{2,1,0:T(8,128)(2,1)S(1)}, u32[]{:S(2)}, u32[]{:S(2)}) collective-permute-start(bf16[4,24,1792]{2,1,0:T(8,128)(2,1)S(1)} %pad_maximum_fusion.9), channel_id=1, source_target_pairs={{0,8},{1,9},{2,10},{3,11},{4,12},{5,13},{6,14},{7,15},{8,0},{9,1},... | collective-permute-start | bytes 1032200 | tf_op jit(solution)/shard_map/ppermute | solution.py:772
  34.9 15.7 %collective-permute-start.2 = (bf16[4,24,1792]{2,1,0:T(8,128)(2,1)S(1)}, bf16[4,24,1792]{2,1,0:T(8,128)(2,1)S(1)}, u32[]{:S(2)}, u32[]{:S(2)}) collective-permute-start(bf16[4,24,1792]{2,1,0:T(8,128)(2,1)S(1)} %pad_maximum_fusion.8), channel_id=1, source_target_pairs={{0,4},{1,5},{2,6},{3,7},{4,0},{5,1},{6,2},{7,3},{8,12},{9,13},{10,... | collective-permute-start | bytes 1032200 | tf_op jit(solution)/shard_map/ppermute | solution.py:772
  38.8 17.6 %collective-permute-start.8 = (bf16[4,24,1920]{2,1,0:T(8,128)(2,1)S(1)}, bf16[4,24,1920]{2,1,0:T(8,128)(2,1)S(1)}, u32[]{:S(2)}, u32[]{:S(2)}) collective-permute-start(bf16[4,24,1920]{2,1,0:T(8,128)(2,1)S(1)} %pad_maximum_fusion.7), channel_id=1, source_target_pairs={{0,2},{1,3},{2,0},{3,1},{4,6},{5,7},{6,4},{7,5},{8,10},{9,11},{10,... | collective-permute-start | bytes 1105928 | tf_op jit(solution)/shard_map/ppermute | solution.py:772
  49.9 20.8 %collective-permute-start.6 = (bf16[8,24,1792]{2,1,0:T(8,128)(2,1)S(1)}, bf16[8,24,1792]{2,1,0:T(8,128)(2,1)S(1)}, u32[]{:S(2)}, u32[]{:S(2)}) collective-permute-start(bf16[8,24,1792]{2,1,0:T(8,128)(2,1)S(1)} %pad_maximum_fusion.3), channel_id=1, source_target_pairs={{0,2},{1,3},{2,0},{3,1},{4,6},{5,7},{6,4},{7,5},{8,10},{9,11},{10,... | collective-permute-start | bytes 2064392 | tf_op jit(solution)/shard_map/ppermute | solution.py:772
  50.7 21.8 %collective-permute-start.3 = (bf16[8,24,1792]{2,1,0:T(8,128)(2,1)S(1)}, bf16[8,24,1792]{2,1,0:T(8,128)(2,1)S(1)}, u32[]{:S(2)}, u32[]{:S(2)}) collective-permute-start(bf16[8,24,1792]{2,1,0:T(8,128)(2,1)S(1)} %pad_maximum_fusion.2), channel_id=1, source_target_pairs={{0,8},{1,9},{2,10},{3,11},{4,12},{5,13},{6,14},{7,15},{8,0},{9,1},... | collective-permute-start | bytes 2064392 | tf_op jit(solution)/shard_map/ppermute | solution.py:772
  56.5 15.2 %collective-permute-start.9 = (bf16[8,24,1920]{2,1,0:T(8,128)(2,1)S(1)}, bf16[8,24,1920]{2,1,0:T(8,128)(2,1)S(1)}, u32[]{:S(2)}, u32[]{:S(2)}) collective-permute-start(bf16[8,24,1920]{2,1,0:T(8,128)(2,1)S(1)} %pad_maximum_fusion.1), channel_id=1, source_target_pairs={{0,4},{1,5},{2,6},{3,7},{4,0},{5,1},{6,2},{7,3},{8,12},{9,13},{10,... | collective-permute-start | bytes 2211848 | tf_op jit(solution)/shard_map/ppermute | solution.py:772
  71.7 7.3 %collective-permute-start.11 = (bf16[16,24,1792]{2,1,0:T(8,128)(2,1)}, bf16[16,24,1792]{2,1,0:T(8,128)(2,1)}, u32[]{:S(2)}, u32[]{:S(2)}) collective-permute-start(bf16[16,24,1792]{2,1,0:T(8,128)(2,1)} %constant_dynamic-update-slice_fusion.5.refs_1_.refs_7_.refs_13_.refs_19_), channel_id=1, source_target_pairs={{0,1},{1,0},{2,3},{3,2},{4,5},{5,4},{6,7},{7,6},{8,9},{9,8},{10,11... | collective-permute-start | bytes 4128776 | tf_op jit(solution)/shard_map/ppermute | solution.py:772
  71.8 9.4 %collective-permute-start.12 = (bf16[16,24,1920]{2,1,0:T(8,128)(2,1)S(1)}, bf16[16,24,1920]{2,1,0:T(8,128)(2,1)S(1)}, u32[]{:S(2)}, u32[]{:S(2)}) collective-permute-start(bf16[16,24,1920]{2,1,0:T(8,128)(2,1)S(1)} %constant_dynamic-update-slice_fusion.10.refs_2_.refs_8_.refs_14_.refs_20_), channel_id=1, source_target_pairs={{0,1},{1,0},{2,3},{3,2},{4,5},{5,4},{6,7},{7,6},{8,9},{9,8},{10,11... | collective-permute-start | bytes 4423688 | tf_op jit(solution)/shard_map/ppermute | solution.py:772
  73.4 7.8 %collective-permute-start.10 = (bf16[16,24,1792]{2,1,0:T(8,128)(2,1)}, bf16[16,24,1792]{2,1,0:T(8,128)(2,1)}, u32[]{:S(2)}, u32[]{:S(2)}) collective-permute-start(bf16[16,24,1792]{2,1,0:T(8,128)(2,1)} %constant_dynamic-update-slice_fusion.refs_0_.refs_6_.refs_12_.refs_18_), channel_id=1, source_target_pairs={{0,1},{1,0},{2,3},{3,2},{4,5},{5,4},{6,7},{7,6},{8,9},{9,8},{10,11... | collective-permute-start | bytes 4128776 | tf_op jit(solution)/shard_map/ppermute | solution.py:772
  147.0 22.0 %collective-permute-start.13 = (bf16[3,8,352,128]{3,2,1,0:T(8,128)(2,1)S(1)}, bf16[3,8,352,128]{3,2,1,0:T(8,128)(2,1)S(1)}, u32[]{:S(2)}, u32[]{:S(2)}) collective-permute-start(bf16[3,8,352,128]{3,2,1,0:T(8,128)(2,1)S(1)} %get-tuple-element.160), channel_id=1, source_target_pairs={{0,1},{1,0},{2,3},{3,2},{4,5},{5,4},{6,7},{7,6},{8,9},{9,8},{10,11... | collective-permute-start | bytes 6488072 | tf_op jit(solution)/shard_map/ppermute | solution.py:772
  160.4 17.2 %collective-permute-start.15 = (bf16[3,8,192,128]{3,2,1,0:T(8,128)(2,1)S(1)}, bf16[3,8,192,128]{3,2,1,0:T(8,128)(2,1)S(1)}, u32[]{:S(2)}, u32[]{:S(2)}) collective-permute-start(bf16[3,8,192,128]{3,2,1,0:T(8,128)(2,1)S(1)} %get-tuple-element.173), channel_id=1, source_target_pairs={{0,1},{1,0},{2,3},{3,2},{4,5},{5,4},{6,7},{7,6},{8,9},{9,8},{10,11... | collective-permute-start | bytes 3538952 | tf_op jit(solution)/shard_map/ppermute | solution.py:772
  169.7 10.6 %collective-permute-start.17 = (bf16[4,352,128]{2,1,0:T(8,128)(2,1)S(1)}, bf16[4,352,128]{2,1,0:T(8,128)(2,1)S(1)}, u32[]{:S(2)}, u32[]{:S(2)}) collective-permute-start(bf16[4,352,128]{2,1,0:T(8,128)(2,1)S(1)} %get-tuple-element.232), channel_id=1, source_target_pairs={{0,4},{1,5},{2,6},{3,7},{4,0},{5,1},{6,2},{7,3},{8,12},{9,13},{10,... | collective-permute-start | bytes 1081352 | tf_op jit(solution)/shard_map/ppermute | solution.py:772
  170.5 10.1 %collective-permute-start.18 = (bf16[4,352,128]{2,1,0:T(8,128)(2,1)S(1)}, bf16[4,352,128]{2,1,0:T(8,128)(2,1)S(1)}, u32[]{:S(2)}, u32[]{:S(2)}) collective-permute-start(bf16[4,352,128]{2,1,0:T(8,128)(2,1)S(1)} %get-tuple-element.231), channel_id=1, source_target_pairs={{0,8},{1,9},{2,10},{3,11},{4,12},{5,13},{6,14},{7,15},{8,0},{9,1},... | collective-permute-start | bytes 1081352 | tf_op jit(solution)/shard_map/ppermute | solution.py:772
  171.1 9.8 %collective-permute-start.16 = (bf16[4,352,128]{2,1,0:T(8,128)(2,1)S(1)}, bf16[4,352,128]{2,1,0:T(8,128)(2,1)S(1)}, u32[]{:S(2)}, u32[]{:S(2)}) collective-permute-start(bf16[4,352,128]{2,1,0:T(8,128)(2,1)S(1)} %get-tuple-element.233), channel_id=1, source_target_pairs={{0,2},{1,3},{2,0},{3,1},{4,6},{5,7},{6,4},{7,5},{8,10},{9,11},{10,... | collective-permute-start | bytes 1081352 | tf_op jit(solution)/shard_map/ppermute | solution.py:772
  181.7 5.8 %collective-permute-start.24 = (bf16[2,352,128]{2,1,0:T(8,128)(2,1)S(1)}, bf16[2,352,128]{2,1,0:T(8,128)(2,1)S(1)}, u32[]{:S(2)}, u32[]{:S(2)}) collective-permute-start(bf16[2,352,128]{2,1,0:T(8,128)(2,1)S(1)} %get-tuple-element.188), channel_id=1, source_target_pairs={{0,2},{1,3},{2,0},{3,1},{4,6},{5,7},{6,4},{7,5},{8,10},{9,11},{10,... | collective-permute-start | bytes 540680 | tf_op jit(solution)/shard_map/ppermute | solution.py:772
  182.6 7.5 %collective-permute-start.23 = (bf16[2,352,128]{2,1,0:T(8,128)(2,1)S(1)}, bf16[2,352,128]{2,1,0:T(8,128)(2,1)S(1)}, u32[]{:S(2)}, u32[]{:S(2)}) collective-permute-start(bf16[2,352,128]{2,1,0:T(8,128)(2,1)S(1)} %get-tuple-element.186), channel_id=1, source_target_pairs={{0,8},{1,9},{2,10},{3,11},{4,12},{5,13},{6,14},{7,15},{8,0},{9,1},... | collective-permute-start | bytes 540680 | tf_op jit(solution)/shard_map/ppermute | solution.py:772
  183.9 7.5 %collective-permute-start.22 = (bf16[2,352,128]{2,1,0:T(8,128)(2,1)S(1)}, bf16[2,352,128]{2,1,0:T(8,128)(2,1)S(1)}, u32[]{:S(2)}, u32[]{:S(2)}) collective-permute-start(bf16[2,352,128]{2,1,0:T(8,128)(2,1)S(1)} %get-tuple-element.184), channel_id=1, source_target_pairs={{0,4},{1,5},{2,6},{3,7},{4,0},{5,1},{6,2},{7,3},{8,12},{9,13},{10,... | collective-permute-start | bytes 540680 | tf_op jit(solution)/shard_map/ppermute | solution.py:772
  185.0 11.1 %collective-permute-start.21 = (bf16[4,352,128]{2,1,0:T(8,128)(2,1)S(1)}, bf16[4,352,128]{2,1,0:T(8,128)(2,1)S(1)}, u32[]{:S(2)}, u32[]{:S(2)}) collective-permute-start(bf16[4,352,128]{2,1,0:T(8,128)(2,1)S(1)} %get-tuple-element.182), channel_id=1, source_target_pairs={{0,8},{1,9},{2,10},{3,11},{4,12},{5,13},{6,14},{7,15},{8,0},{9,1},... | collective-permute-start | bytes 1081352 | tf_op jit(solution)/shard_map/ppermute | solution.py:772
  185.7 11.5 %collective-permute-start.20 = (bf16[4,352,128]{2,1,0:T(8,128)(2,1)S(1)}, bf16[4,352,128]{2,1,0:T(8,128)(2,1)S(1)}, u32[]{:S(2)}, u32[]{:S(2)}) collective-permute-start(bf16[4,352,128]{2,1,0:T(8,128)(2,1)S(1)} %get-tuple-element.180), channel_id=1, source_target_pairs={{0,4},{1,5},{2,6},{3,7},{4,0},{5,1},{6,2},{7,3},{8,12},{9,13},{10,... | collective-permute-start | bytes 1081352 | tf_op jit(solution)/shard_map/ppermute | solution.py:772
  187.5 9.9 %collective-permute-start.19 = (bf16[4,352,128]{2,1,0:T(8,128)(2,1)S(1)}, bf16[4,352,128]{2,1,0:T(8,128)(2,1)S(1)}, u32[]{:S(2)}, u32[]{:S(2)}) collective-permute-start(bf16[4,352,128]{2,1,0:T(8,128)(2,1)S(1)} %get-tuple-element.178), channel_id=1, source_target_pairs={{0,2},{1,3},{2,0},{3,1},{4,6},{5,7},{6,4},{7,5},{8,10},{9,11},{10,... | collective-permute-start | bytes 1081352 | tf_op jit(solution)/shard_map/ppermute | solution.py:772
  197.6 5.6 %collective-permute-start.25 = (bf16[1,352,128]{2,1,0:T(8,128)(2,1)S(1)}, bf16[1,352,128]{2,1,0:T(8,128)(2,1)S(1)}, u32[]{:S(2)}, u32[]{:S(2)}) collective-permute-start(bf16[1,352,128]{2,1,0:T(8,128)(2,1)S(1)} %get-tuple-element.190), channel_id=1, source_target_pairs={{0,8},{1,9},{2,10},{3,11},{4,12},{5,13},{6,14},{7,15},{8,0},{9,1},... | collective-permute-start | bytes 270344 | tf_op jit(solution)/shard_map/ppermute | solution.py:772
  198.3 5.5 %collective-permute-start.26 = (bf16[1,352,128]{2,1,0:T(8,128)(2,1)S(1)}, bf16[1,352,128]{2,1,0:T(8,128)(2,1)S(1)}, u32[]{:S(2)}, u32[]{:S(2)}) collective-permute-start(bf16[1,352,128]{2,1,0:T(8,128)(2,1)S(1)} %get-tuple-element.192), channel_id=1, source_target_pairs={{0,2},{1,3},{2,0},{3,1},{4,6},{5,7},{6,4},{7,5},{8,10},{9,11},{10,... | collective-permute-start | bytes 270344 | tf_op jit(solution)/shard_map/ppermute | solution.py:772
  201.1 5.5 %collective-permute-start.28 = (bf16[2,352,128]{2,1,0:T(8,128)(2,1)S(1)}, bf16[2,352,128]{2,1,0:T(8,128)(2,1)S(1)}, u32[]{:S(2)}, u32[]{:S(2)}) collective-permute-start(bf16[2,352,128]{2,1,0:T(8,128)(2,1)S(1)} %get-tuple-element.196), channel_id=1, source_target_pairs={{0,4},{1,5},{2,6},{3,7},{4,0},{5,1},{6,2},{7,3},{8,12},{9,13},{10,... | collective-permute-start | bytes 540680 | tf_op jit(solution)/shard_map/ppermute | solution.py:772
  201.4 6.5 %collective-permute-start.30 = (bf16[2,352,128]{2,1,0:T(8,128)(2,1)S(1)}, bf16[2,352,128]{2,1,0:T(8,128)(2,1)S(1)}, u32[]{:S(2)}, u32[]{:S(2)}) collective-permute-start(bf16[2,352,128]{2,1,0:T(8,128)(2,1)S(1)} %get-tuple-element.198), channel_id=1, source_target_pairs={{0,8},{1,9},{2,10},{3,11},{4,12},{5,13},{6,14},{7,15},{8,0},{9,1},... | collective-permute-start | bytes 540680 | tf_op jit(solution)/shard_map/ppermute | solution.py:772
  203.1 6.5 %collective-permute-start.32 = (bf16[2,352,128]{2,1,0:T(8,128)(2,1)S(1)}, bf16[2,352,128]{2,1,0:T(8,128)(2,1)S(1)}, u32[]{:S(2)}, u32[]{:S(2)}) collective-permute-start(bf16[2,352,128]{2,1,0:T(8,128)(2,1)S(1)} %get-tuple-element.200), channel_id=1, source_target_pairs={{0,2},{1,3},{2,0},{3,1},{4,6},{5,7},{6,4},{7,5},{8,10},{9,11},{10,... | collective-permute-start | bytes 540680 | tf_op jit(solution)/shard_map/ppermute | solution.py:772
  214.4 10.3 %collective-permute-start.34 = (bf16[3,352,128]{2,1,0:T(8,128)(2,1)S(1)}, bf16[3,352,128]{2,1,0:T(8,128)(2,1)S(1)}, u32[]{:S(2)}, u32[]{:S(2)}) collective-permute-start(bf16[3,352,128]{2,1,0:T(8,128)(2,1)S(1)} %pad_maximum_fusion.10), channel_id=1, source_target_pairs={{0,16},{1,17},{2,18},{3,19},{4,20},{5,21},{6,22},{7,23},{8,24},{9,... | collective-permute-start | bytes 811016 | tf_op jit(solution)/shard_map/ppermute | solution.py:772
  225.9 13.4 %all-to-all-start.1 = ((bf16[32,8,512]{2,1,0:T(8,128)(2,1)}), bf16[32,8,512]{2,1,0:T(8,128)(2,1)S(1)}, u32[]{:S(2)}, u32[]{:S(2)}) async-start(bf16[32,8,512]{2,1,0:T(8,128)(2,1)} %get-tuple-element.201), calls=%async_computation.1 | async-start | bytes 524288 | tf_op jit(solution)/shard_map/all_to_all | solution.py:1031
  (40 other events, 441.0 us)
Sparse Core Ops, SparseCore 0:
  11.5 92.0 all-gather.1
